TPU v7x, 512 devices: a whole 4x8x8 slice. The times are simulated.
512 devices in a mesh: len: 16 (over z, core), wid: 8 (over y), hgt: 4 (over x).
Axes of the slice: x: 4, y: 8, z: 8, core: 2. Of those that a mesh axis runs over, the one named last changes fastest.
Arguments:
- pressure_now: float32 [64, 512, 2048], P('hgt', 'wid', 'len')
- pressure_old: float32 [64, 512, 2048], P('hgt', 'wid', 'len')
- classes: int32 [64, 512, 2048], P('hgt', 'wid', 'len'), may hold values from 0 to 8, as said below
- admittance: float32 [8], replicated, may hold values from 0.05 to 1.5
- source_cells: int32 [4, 3], replicated, may hold values from 0 to 2047, as said below
- source_signal: float32 [16, 4], replicated, may hold values from -6 to 6
- receiver_cells: int32 [128, 3], replicated, may hold values from 0 to 2047, as said below
Outputs:
- pressure: float32 [64, 512, 2048], P('hgt', 'wid', 'len')
- traces: float32 [16, 128], replicated
Inputs may be any that keep to these rules, and one draw needn't show every extreme that they name: 0 is air; 1 to 8 are wall classes; every cell on the grid's outer faces is a wall. `source_cells`: each row holds a cell's height, width and length coordinates, inside the grid. `receiver_cells`: each row holds a cell's height, width and length coordinates, inside the grid.
All inputs are finite; a program needn't handle non-finite values.
Results may differ from a plain program's by a relative error of at most 0.000022.
Values sent between devices are 32-bit elements; how exact they have to be, the bound alone decides.
No kernel may reach another device: no remote copies, remote signals or barrier semaphores. Data moves between devices by JAX's collectives and lax.ppermute only.
A program may use at most 64 MiB of HBM per device.

v0:
```python
import jax
import jax.numpy as jnp
from jax import lax
from jax.sharding import PartitionSpec as P

courant_sq = 1.0 / 3.0


def with_halo(cells, sides, width):
    for axis, dim in sides:
        count = lax.axis_size(axis)
        ends = count - 1
        head = lax.slice_in_dim(cells, 0, width, axis=dim)
        tail = lax.slice_in_dim(cells, cells.shape[dim] - width, cells.shape[dim], axis=dim)
        cells = jnp.concatenate(
            [
                lax.ppermute(tail, axis, [(i, (i + 1) % count) for i in range(ends)]),
                cells,
                lax.ppermute(head, axis, [((i + 1) % count, i) for i in range(ends)]),
            ],
            axis=dim,
        )
    return cells


def lookup(classes, admittance):
    loss = jnp.zeros(classes.shape, jnp.float32)
    for index in range(admittance.shape[0]):
        loss = loss + jnp.where(classes == index + 1, admittance[index], jnp.float32(0.0))
    return loss


def update(now, old, padded, loss):
    beside = padded[2:, 1:-1, 1:-1] + padded[:-2, 1:-1, 1:-1]
    beside = beside + padded[1:-1, 2:, 1:-1] + padded[1:-1, :-2, 1:-1]
    beside = beside + padded[1:-1, 1:-1, 2:] + padded[1:-1, 1:-1, :-2]
    return (2.0 * now - (1.0 - loss) * old + courant_sq * (beside - 6.0 * now)) / (1.0 + loss)


def locate(field, cells, anchor):
    local = cells - anchor[None, :]
    limits = jnp.array(field.shape, jnp.int32)
    valid = jnp.all((local >= 0) & (local < limits[None, :]), axis=1)
    local = jnp.clip(local, 0, limits[None, :] - 1)
    return (local, valid)


def inject(field, cells, values, anchor):
    local, valid = locate(field, cells, anchor)
    return field.at[local[:, 0], local[:, 1], local[:, 2]].add(
        jnp.where(valid, values, jnp.float32(0.0))
    )


def sample(field, cells, anchor):
    local, valid = locate(field, cells, anchor)
    return jnp.where(valid, field[local[:, 0], local[:, 1], local[:, 2]], jnp.float32(0.0))


def report(values):
    return lax.psum(values, ("len", "wid", "hgt"))


def per_device(
    pressure_now, pressure_old, classes, admittance, source_cells, source_signal, receiver_cells
):
    high, wide, deep = pressure_now.shape
    anchor = jnp.stack(
        [lax.axis_index("hgt") * high, lax.axis_index("wid") * wide, lax.axis_index("len") * deep]
    )
    loss = lookup(classes, admittance)

    def advance(carry, signal_row):
        now, old = carry
        padded = with_halo(now, (("hgt", 0), ("wid", 1), ("len", 2)), 1)
        fresh = inject(update(now, old, padded, loss), source_cells, signal_row, anchor)
        return ((fresh, now), report(sample(fresh, receiver_cells, anchor)))

    (now, old), recorded = lax.scan(advance, (pressure_now, pressure_old), source_signal)
    return (now, recorded)


def solution(mesh):
    placed = (
        P("hgt", "wid", "len"),
        P("hgt", "wid", "len"),
        P("hgt", "wid", "len"),
        P(),
        P(),
        P(),
        P(),
    )
    return jax.shard_map(
        per_device,
        mesh=mesh,
        in_specs=placed,
        out_specs=(P("hgt", "wid", "len"), P()),
        check_vma=False,
    )
```

profile of v0, /device:TPU:1, one launch (start us, length us, event | category | flops | bytes accessed | tf_op | source)
XLA Modules:
  0.0 2149.7 jit_solution(6690696709907322391)
XLA Ops:
  3.2 5.4 select_add_fusion
  12.0 2136.9 %while.20 = (s32[]{:T(128)}, f32[16,64,128]{2,1,0:T(8,128)S(1)}, f32[16,64,128]{2,1,0:T(8,128)}, f32[16,128]{1,0:T(8,128)}, f32[16,64,128]{2,1,0:T(8,128)S(1)}, ...) while((s32[]{:T(128)}, f32[16,64,128]{2,1,0:T(8,128)S(1)}, ...), condition=%wide.region_5.6_spmd.clone.clone, body=%wide.region_2.5_spmd.sunk.clone.clone.sunk | while | flops 3584650 | bytes 8024557 | solution.py:79
  28.0 7.1 collective-permute-start.4
  45.6 103.4 %psum.16 = f32[1,128]{1,0:T(1,128)S(1)} all-reduce(f32[1,128]{1,0:T(1,128)S(1)} %select_bitcast_fusion.2), channel_id=1, replica_groups=mesh['len'=16,'wid'=8,'hgt'=4] {'len','wid','hgt'}, use_global_device_ids=true, to_apply=%region_4.4 | all-reduce | flops 128 | bytes 1024 | tf_op jit(solution)/shard_map/while/body/eval_jaxpr/psum | solution.py:61
  166.4 5.6 collective-permute-start.4
  182.6 98.2 %psum.16 = f32[1,128]{1,0:T(1,128)S(1)} all-reduce(f32[1,128]{1,0:T(1,128)S(1)} %select_bitcast_fusion.2), channel_id=1, replica_groups=mesh['len'=16,'wid'=8,'hgt'=4] {'len','wid','hgt'}, use_global_device_ids=true, to_apply=%region_4.4 | all-reduce | flops 128 | bytes 1024 | tf_op jit(solution)/shard_map/while/body/eval_jaxpr/psum | solution.py:61
  293.1 4.4 collective-permute-start.3
  298.8 6.6 collective-permute-start.4
  315.9 98.0 %psum.16 = f32[1,128]{1,0:T(1,128)S(1)} all-reduce(f32[1,128]{1,0:T(1,128)S(1)} %select_bitcast_fusion.2), channel_id=1, replica_groups=mesh['len'=16,'wid'=8,'hgt'=4] {'len','wid','hgt'}, use_global_device_ids=true, to_apply=%region_4.4 | all-reduce | flops 128 | bytes 1024 | tf_op jit(solution)/shard_map/while/body/eval_jaxpr/psum | solution.py:61
  426.2 4.6 collective-permute-start.3
  432.2 6.6 collective-permute-start.4
  449.2 98.0 %psum.16 = f32[1,128]{1,0:T(1,128)S(1)} all-reduce(f32[1,128]{1,0:T(1,128)S(1)} %select_bitcast_fusion.2), channel_id=1, replica_groups=mesh['len'=16,'wid'=8,'hgt'=4] {'len','wid','hgt'}, use_global_device_ids=true, to_apply=%region_4.4 | all-reduce | flops 128 | bytes 1024 | tf_op jit(solution)/shard_map/while/body/eval_jaxpr/psum | solution.py:61
  559.5 4.6 collective-permute-start.3
  565.5 6.6 collective-permute-start.4
  582.5 98.0 %psum.16 = f32[1,128]{1,0:T(1,128)S(1)} all-reduce(f32[1,128]{1,0:T(1,128)S(1)} %select_bitcast_fusion.2), channel_id=1, replica_groups=mesh['len'=16,'wid'=8,'hgt'=4] {'len','wid','hgt'}, use_global_device_ids=true, to_apply=%region_4.4 | all-reduce | flops 128 | bytes 1024 | tf_op jit(solution)/shard_map/while/body/eval_jaxpr/psum | solution.py:61
  692.8 4.6 collective-permute-start.3
  698.8 6.6 collective-permute-start.4
  715.8 98.0 %psum.16 = f32[1,128]{1,0:T(1,128)S(1)} all-reduce(f32[1,128]{1,0:T(1,128)S(1)} %select_bitcast_fusion.2), channel_id=1, replica_groups=mesh['len'=16,'wid'=8,'hgt'=4] {'len','wid','hgt'}, use_global_device_ids=true, to_apply=%region_4.4 | all-reduce | flops 128 | bytes 1024 | tf_op jit(solution)/shard_map/while/body/eval_jaxpr/psum | solution.py:61
  826.1 4.6 collective-permute-start.3
  832.1 6.6 collective-permute-start.4
  849.2 98.0 %psum.16 = f32[1,128]{1,0:T(1,128)S(1)} all-reduce(f32[1,128]{1,0:T(1,128)S(1)} %select_bitcast_fusion.2), channel_id=1, replica_groups=mesh['len'=16,'wid'=8,'hgt'=4] {'len','wid','hgt'}, use_global_device_ids=true, to_apply=%region_4.4 | all-reduce | flops 128 | bytes 1024 | tf_op jit(solution)/shard_map/while/body/eval_jaxpr/psum | solution.py:61
  959.4 4.6 collective-permute-start.3
  965.4 6.6 collective-permute-start.4
  982.5 98.0 %psum.16 = f32[1,128]{1,0:T(1,128)S(1)} all-reduce(f32[1,128]{1,0:T(1,128)S(1)} %select_bitcast_fusion.2), channel_id=1, replica_groups=mesh['len'=16,'wid'=8,'hgt'=4] {'len','wid','hgt'}, use_global_device_ids=true, to_apply=%region_4.4 | all-reduce | flops 128 | bytes 1024 | tf_op jit(solution)/shard_map/while/body/eval_jaxpr/psum | solution.py:61
  1092.7 4.6 collective-permute-start.3
  1098.7 6.6 collective-permute-start.4
  1115.8 98.0 %psum.16 = f32[1,128]{1,0:T(1,128)S(1)} all-reduce(f32[1,128]{1,0:T(1,128)S(1)} %select_bitcast_fusion.2), channel_id=1, replica_groups=mesh['len'=16,'wid'=8,'hgt'=4] {'len','wid','hgt'}, use_global_device_ids=true, to_apply=%region_4.4 | all-reduce | flops 128 | bytes 1024 | tf_op jit(solution)/shard_map/while/body/eval_jaxpr/psum | solution.py:61
  1226.0 4.6 collective-permute-start.3
  1232.0 6.6 collective-permute-start.4
  1249.1 98.0 %psum.16 = f32[1,128]{1,0:T(1,128)S(1)} all-reduce(f32[1,128]{1,0:T(1,128)S(1)} %select_bitcast_fusion.2), channel_id=1, replica_groups=mesh['len'=16,'wid'=8,'hgt'=4] {'len','wid','hgt'}, use_global_device_ids=true, to_apply=%region_4.4 | all-reduce | flops 128 | bytes 1024 | tf_op jit(solution)/shard_map/while/body/eval_jaxpr/psum | solution.py:61
  1359.4 4.6 collective-permute-start.3
  1365.3 6.6 collective-permute-start.4
  1382.4 98.0 %psum.16 = f32[1,128]{1,0:T(1,128)S(1)} all-reduce(f32[1,128]{1,0:T(1,128)S(1)} %select_bitcast_fusion.2), channel_id=1, replica_groups=mesh['len'=16,'wid'=8,'hgt'=4] {'len','wid','hgt'}, use_global_device_ids=true, to_apply=%region_4.4 | all-reduce | flops 128 | bytes 1024 | tf_op jit(solution)/shard_map/while/body/eval_jaxpr/psum | solution.py:61
  1492.7 4.6 collective-permute-start.3
  1498.6 6.6 collective-permute-start.4
  1515.7 98.0 %psum.16 = f32[1,128]{1,0:T(1,128)S(1)} all-reduce(f32[1,128]{1,0:T(1,128)S(1)} %select_bitcast_fusion.2), channel_id=1, replica_groups=mesh['len'=16,'wid'=8,'hgt'=4] {'len','wid','hgt'}, use_global_device_ids=true, to_apply=%region_4.4 | all-reduce | flops 128 | bytes 1024 | tf_op jit(solution)/shard_map/while/body/eval_jaxpr/psum | solution.py:61
  1626.0 4.6 collective-permute-start.3
  1632.0 6.6 collective-permute-start.4
  1649.0 98.0 %psum.16 = f32[1,128]{1,0:T(1,128)S(1)} all-reduce(f32[1,128]{1,0:T(1,128)S(1)} %select_bitcast_fusion.2), channel_id=1, replica_groups=mesh['len'=16,'wid'=8,'hgt'=4] {'len','wid','hgt'}, use_global_device_ids=true, to_apply=%region_4.4 | all-reduce | flops 128 | bytes 1024 | tf_op jit(solution)/shard_map/while/body/eval_jaxpr/psum | solution.py:61
  1759.3 4.6 collective-permute-start.3
  1765.3 6.6 collective-permute-start.4
  1782.3 98.0 %psum.16 = f32[1,128]{1,0:T(1,128)S(1)} all-reduce(f32[1,128]{1,0:T(1,128)S(1)} %select_bitcast_fusion.2), channel_id=1, replica_groups=mesh['len'=16,'wid'=8,'hgt'=4] {'len','wid','hgt'}, use_global_device_ids=true, to_apply=%region_4.4 | all-reduce | flops 128 | bytes 1024 | tf_op jit(solution)/shard_map/while/body/eval_jaxpr/psum | solution.py:61
  1892.6 4.6 collective-permute-start.3
  1898.6 6.6 collective-permute-start.4
  1915.7 98.0 %psum.16 = f32[1,128]{1,0:T(1,128)S(1)} all-reduce(f32[1,128]{1,0:T(1,128)S(1)} %select_bitcast_fusion.2), channel_id=1, replica_groups=mesh['len'=16,'wid'=8,'hgt'=4] {'len','wid','hgt'}, use_global_device_ids=true, to_apply=%region_4.4 | all-reduce | flops 128 | bytes 1024 | tf_op jit(solution)/shard_map/while/body/eval_jaxpr/psum | solution.py:61
  2025.9 4.6 collective-permute-start.3
  2031.9 6.6 collective-permute-start.4
  2049.0 98.0 %psum.16 = f32[1,128]{1,0:T(1,128)S(1)} all-reduce(f32[1,128]{1,0:T(1,128)S(1)} %select_bitcast_fusion.2), channel_id=1, replica_groups=mesh['len'=16,'wid'=8,'hgt'=4] {'len','wid','hgt'}, use_global_device_ids=true, to_apply=%region_4.4 | all-reduce | flops 128 | bytes 1024 | tf_op jit(solution)/shard_map/while/body/eval_jaxpr/psum | solution.py:61
  (910 shorter events, 398.3 us)
Async XLA Ops:
  12.1 6.1 collective-permute-start
  28.0 10.6 collective-permute-start.4
  151.1 5.6 collective-permute-start
  166.4 8.5 collective-permute-start.4
  282.8 5.8 collective-permute-start
  291.8 5.7 collective-permute-start.2
  298.8 9.4 collective-permute-start.4
  415.9 5.8 collective-permute-start
  424.9 5.9 collective-permute-start.2
  432.2 9.4 collective-permute-start.4
  549.2 5.8 collective-permute-start
  558.2 5.9 collective-permute-start.2
  565.5 9.4 collective-permute-start.4
  682.5 5.8 collective-permute-start
  691.5 5.9 collective-permute-start.2
  698.8 9.4 collective-permute-start.4
  815.8 5.8 collective-permute-start
  824.8 5.9 collective-permute-start.2
  832.1 9.4 collective-permute-start.4
  949.1 5.8 collective-permute-start
  958.1 5.9 collective-permute-start.2
  965.4 9.4 collective-permute-start.4
  1082.5 5.8 collective-permute-start
  1091.4 5.9 collective-permute-start.2
  1098.7 9.4 collective-permute-start.4
  1215.8 5.8 collective-permute-start
  1224.7 5.9 collective-permute-start.2
  1226.0 5.4 collective-permute-start.3
  1232.0 9.4 collective-permute-start.4
  1349.1 5.8 collective-permute-start
  1358.1 5.9 collective-permute-start.2
  1359.4 5.4 collective-permute-start.3
  1365.3 9.4 collective-permute-start.4
  1482.4 5.8 collective-permute-start
  1491.4 5.9 collective-permute-start.2
  1498.6 9.4 collective-permute-start.4
  1615.7 5.8 collective-permute-start
  1624.7 5.9 collective-permute-start.2
  1632.0 9.4 collective-permute-start.4
  1749.0 5.8 collective-permute-start
  1758.0 5.9 collective-permute-start.2
  1765.3 9.4 collective-permute-start.4
  1882.3 5.8 collective-permute-start
  1891.3 5.9 collective-permute-start.2
  1898.6 9.4 collective-permute-start.4
  2015.6 5.8 collective-permute-start
  2024.6 5.9 collective-permute-start.2
  2031.9 9.4 collective-permute-start.4
  (234 other events, 2832.1 us)
where the time goes:
time: 2160 us; the launch traced here: 2150 us
  blocking collectives  1570 us (73%)
  starting transfers between devices  308 us (14%)
  local copies, waits for them, and re-layouts  109 us (5%)
  waiting for transfers between devices  84.5 us (4%)
  other arithmetic  70.1 us (3%)
    psum x16, blocking collectives, report(): return lax.psum(values, ('len', 'wid', 'hgt'))  1570 us
    ppermute x48, starting transfers between devices, with_halo(): lax.ppermute(tail, axis, [(i, (i + 1) % count) for i in range(ends)])  236 us
    ppermute x48, starting transfers between devices, with_halo(): lax.ppermute(head, axis, [((i + 1) % count, i) for i in range(ends)])  72.8 us
    ppermute x48, waiting for transfers between devices, with_halo(): lax.ppermute(head, axis, [((i + 1) % count, i) for i in range(ends)])  72.4 us
  transfers between devices with their start and end apart: 96, of which 48 were waited for; matrix products, arithmetic and copies ran while one was open for 2% of the time, Pallas kernels for 0%

commit v1 on v0

v1 whole, which is shorter than its diff:
```python
import functools

import jax
import jax.numpy as jnp
from jax import lax
from jax.experimental import pallas as pl
from jax.experimental.pallas import tpu as pltpu
from jax.sharding import PartitionSpec as P

STEPS = 16
HALO = 16
LANES = 128
HIGH, WIDE, DEEP = 16, 64, 128
TALL = HIGH + 2 * HALO
BROAD = WIDE + 2 * HALO
COLS = BROAD // 8
CHUNK = 4
VMEM = pl.BlockSpec(memory_space=pltpu.VMEM)
SMEM = pl.BlockSpec(memory_space=pltpu.SMEM)


def lane_ids():
    return lax.broadcasted_iota(jnp.int32, (8, LANES), 1)


def regroup(rows, order):
    return jnp.take_along_axis(rows, order, axis=1, mode="promise_in_bounds")


def even_odd():
    lane = lane_ids()
    return jnp.where(lane < 64, 2 * lane, 2 * lane - 127)


def in_order():
    lane = lane_ids()
    return (lane // 2) + 64 * (lane % 2)


def pack_kernel(adm_ref, now_ref, old_ref, cls_ref, s_ref, left_ref, right_ref):
    lane = lane_ids()
    order = even_odd()

    def layer(h, carry):
        heads, tails = [], []
        for j in range(WIDE // 8):
            rows = pl.ds(8 * j, 8)
            kinds = cls_ref[h, rows, :]
            loss = jnp.zeros((8, LANES), jnp.float32)
            for index in range(adm_ref.shape[0]):
                loss = loss + jnp.where(kinds == index + 1, adm_ref[index], jnp.float32(0.0))
            gain = jnp.float32(1.0 / 3.0) / (1.0 + loss)
            head = jnp.zeros((8, LANES), jnp.float32)
            tail = jnp.zeros((8, LANES), jnp.float32)
            for a, field in enumerate((now_ref[h, rows, :], old_ref[h, rows, :], gain)):
                split = regroup(field, order)
                s_ref[a, h, rows, :] = split
                for parity in range(2):
                    at = 8 * (2 * a + parity)
                    inside = (lane >= at) & (lane < at + 8)
                    head = jnp.where(inside, pltpu.roll(split, (at - 64 * parity) % LANES, 1), head)
                    tail = jnp.where(
                        inside, pltpu.roll(split, (at - 56 - 64 * parity) % LANES, 1), tail
                    )
            heads.append(head)
            tails.append(tail)
        half = WIDE // 16
        for j in range(half):
            rows = pl.ds(8 * j, 8)
            left_ref[h, rows, :] = heads[j] + pltpu.roll(heads[j + half], 64, 1)
            right_ref[h, rows, :] = tails[j] + pltpu.roll(tails[j + half], 64, 1)
        return carry

    lax.fori_loop(0, HIGH, layer, 0)


def edge_kernel(from_right_ref, from_left_ref, e_ref):
    lane = lane_ids()

    def layer(h, carry):
        half = WIDE // 16
        for j in range(half):
            rows = pl.ds(8 * j, 8)
            a, b = from_right_ref[h, rows, :], from_left_ref[h, rows, :]
            first = jnp.where(lane < 48, a, jnp.float32(0.0))
            first = jnp.where((lane >= 56) & (lane < 104), pltpu.roll(b, 56, 1), first)
            second = jnp.where(lane < 48, pltpu.roll(a, 64, 1), jnp.float32(0.0))
            second = jnp.where((lane >= 56) & (lane < 104), pltpu.roll(b, 120, 1), second)
            e_ref[h, rows, :] = first
            e_ref[h, pl.ds(8 * (j + half), 8), :] = second
        return carry

    lax.fori_loop(0, HIGH, layer, 0)


def march_kernel(
    src_ref, sig_ref, rec_ref, *refs
):
    pieces = refs[:18]
    out_ref, trace_ref = refs[18:20]
    a_ref, b_ref, p_ref, temp, plain, hist, todo = refs[20:]
    lane = lane_ids()
    row = lax.broadcasted_iota(jnp.int32, (8, LANES), 0)
    zero = jnp.float32(0.0)
    fringe = ((lane >= 64) & (lane < 72)) | (lane >= 120)
    corner = (
        lax.axis_index("hgt") * HIGH - HALO,
        lax.axis_index("wid") * WIDE - HALO,
        lax.axis_index("len") * DEEP,
    )

    for part in range(3):
        cells = pieces[6 * part : 6 * part + 3]
        edges = pieces[6 * part + 3 : 6 * part + 6]

        def layer(h, carry):
            at = part * HIGH + h
            for k, (lo, n) in enumerate(((0, 16), (16, 64), (80, 16))):
                for a in range(3):
                    temp[a, pl.ds(lo, n), :] = cells[k][a, h]
                temp[3, pl.ds(lo, n), :] = edges[k][h]
            for j in range(COLS):
                edge = temp[3, pl.ds(j, 8, stride=COLS), :]
                for a, ref in enumerate((a_ref, b_ref, p_ref)):
                    main = temp[a, pl.ds(j, 8, stride=COLS), :]
                    for parity in range(2):
                        near = pltpu.roll(edge, 64 - 8 * (2 * a + parity), 1)
                        near = jnp.where(fringe, near, zero)
                        mid = pltpu.roll(main, 64, 1) if parity else main
                        ref[parity, at, j] = jnp.where(lane < 64, mid, near)
            return carry

        lax.fori_loop(0, HIGH, layer, 0)

    def note(r, count):
        h = rec_ref[0, r] - corner[0]
        w = rec_ref[1, r] - corner[1]
        d = rec_ref[2, r] - corner[2]
        mine = (h >= HALO) & (h < HALO + HIGH) & (w >= HALO) & (w < HALO + WIDE)
        mine = mine & (d >= 0) & (d < DEEP)

        @pl.when(mine)
        def _():
            todo[0, count] = r
            todo[1, count] = h
            todo[2, count] = w % COLS
            todo[3, count] = w // COLS
            todo[4, count] = d % 2
            todo[5, count] = d // 2

        return count + mine.astype(jnp.int32)

    count = lax.fori_loop(0, rec_ref.shape[1], note, jnp.int32(0))

    points = []
    for s in range(src_ref.shape[0]):
        h = src_ref[s, 0] - corner[0]
        w = src_ref[s, 1] - corner[1]
        d = src_ref[s, 2] - corner[2] + HALO
        near = (h >= 0) & (h < TALL) & (w >= 0) & (w < BROAD) & (d >= 0) & (d < DEEP + 2 * HALO)
        h = jnp.clip(h, 0, TALL - 1)
        w = jnp.clip(w, 0, BROAD - 1)
        d = jnp.clip(d, 0, DEEP + 2 * HALO - 1)
        place = (d // 2 + LANES - HALO // 2) % LANES
        points.append((near, d % 2, h, w % COLS, (row == w // COLS) & (lane == place)))

    def step(now, old, t):
        def chunk(i, carry):
            for u in range(CHUNK):
                h = t + 1 + CHUNK * i + u
                for parity in range(2):
                    other = [now[1 - parity, h, j] for j in range(COLS)]
                    mine = [now[parity, h, j] for j in range(COLS)]
                    for j in range(COLS):
                        before = mine[j - 1] if j > 0 else pltpu.roll(mine[COLS - 1], 1, 0)
                        after = mine[j + 1] if j < COLS - 1 else pltpu.roll(mine[0], 7, 0)
                        beside = other[j] + pltpu.roll(other[j], 127 if parity else 1, 1)
                        total = (now[parity, h - 1, j] + now[parity, h + 1, j]) + (before + after)
                        total = total + beside
                        past = old[parity, h, j]
                        old[parity, h, j] = past + p_ref[parity, h, j] * (total - 6.0 * past)
            return carry

        trips = (TALL - 2 * (t + 1) + CHUNK - 1) // CHUNK
        lax.fori_loop(0, trips, chunk, 0)
        for s, (near, parity, h, j, spot) in enumerate(points):

            @pl.when(near)
            def _():
                old[parity, h, j] = old[parity, h, j] + jnp.where(spot, sig_ref[t, s], zero)

        def keep(i, carry):
            value = old[todo[4, i], todo[1, i], todo[2, i], pl.ds(todo[3, i], 1), :]
            hist[i, pl.ds(t, 1), :] = value
            return carry

        lax.fori_loop(0, count, keep, 0)

    def pair(i, carry):
        step(a_ref, b_ref, 2 * i)
        step(b_ref, a_ref, 2 * i + 1)
        return carry

    lax.fori_loop(0, STEPS // 2, pair, 0)

    trace_ref[...] = jnp.zeros((STEPS, LANES), jnp.float32)
    wide_lane = lax.broadcasted_iota(jnp.int32, (STEPS, LANES), 1)

    def gather(i, carry):
        number = todo[0, i]
        moved = pltpu.roll(hist[i], (number - todo[5, i] + LANES) % LANES, 1)
        trace_ref[...] = jnp.where(wide_lane == number, moved, trace_ref[...])
        return carry

    lax.fori_loop(0, count, gather, 0)

    order = in_order()

    def finish(h, carry):
        for j in range(COLS):
            even, odd = a_ref[0, HALO + h, j], a_ref[1, HALO + h, j]
            joined = jnp.where(lane < 64, even, pltpu.roll(odd, 64, 1))
            plain[pl.ds(j, 8, stride=COLS), :] = regroup(joined, order)
        out_ref[h] = plain[pl.ds(HALO, WIDE), :]
        return carry

    lax.fori_loop(0, HIGH, finish, 0)


def field(*shape):
    return jax.ShapeDtypeStruct(shape, jnp.float32)


def pack(admittance, now, old, classes):
    return pl.pallas_call(
        pack_kernel,
        out_shape=(
            field(3, HIGH, WIDE, LANES),
            field(HIGH, WIDE // 2, LANES),
            field(HIGH, WIDE // 2, LANES),
        ),
        in_specs=[SMEM, VMEM, VMEM, VMEM],
        out_specs=(VMEM, VMEM, VMEM),
        name="pack",
        compiler_params=pltpu.CompilerParams(vmem_limit_bytes=12 << 20),
    )(admittance, now, old, classes)


def edge(from_right, from_left):
    return pl.pallas_call(
        edge_kernel,
        out_shape=field(HIGH, WIDE, LANES),
        in_specs=[VMEM, VMEM],
        out_specs=VMEM,
        name="edge",
        compiler_params=pltpu.CompilerParams(vmem_limit_bytes=12 << 20),
    )(from_right, from_left)


def march(sources, signal, receivers, pieces):
    return pl.pallas_call(
        march_kernel,
        out_shape=(field(HIGH, WIDE, DEEP), field(STEPS, LANES)),
        in_specs=[SMEM] * 3 + [VMEM] * 18,
        out_specs=(VMEM, VMEM),
        scratch_shapes=[
            pltpu.VMEM((2, TALL + 4, COLS, 8, LANES), jnp.float32),
            pltpu.VMEM((2, TALL + 4, COLS, 8, LANES), jnp.float32),
            pltpu.VMEM((2, TALL + 4, COLS, 8, LANES), jnp.float32),
            pltpu.VMEM((4, BROAD, LANES), jnp.float32),
            pltpu.VMEM((BROAD, LANES), jnp.float32),
            pltpu.VMEM((LANES, STEPS, LANES), jnp.float32),
            pltpu.SMEM((8, LANES), jnp.int32),
        ],
        name="march",
        compiler_params=pltpu.CompilerParams(vmem_limit_bytes=52 << 20),
    )(sources, signal, receivers, *pieces)


def shift(x, axes, moves):
    sizes = [lax.axis_size(a) for a in axes]
    pairs = []
    for start in range(functools.reduce(lambda a, b: a * b, sizes)):
        place, rest = [], start
        for size in reversed(sizes):
            place.insert(0, rest % size)
            rest //= size
        goal = [a + b for a, b in zip(place, moves)]
        if all(0 <= g < size for g, size in zip(goal, sizes)):
            end = 0
            for g, size in zip(goal, sizes):
                end = end * size + g
            pairs.append((start, end))
    return lax.ppermute(x, axes if len(axes) > 1 else axes[0], pairs)


def spread(x):
    rows = x.ndim - 2
    head = lax.slice_in_dim(x, 0, HALO, axis=rows)
    tail = lax.slice_in_dim(x, WIDE - HALO, WIDE, axis=rows)
    both = ("wid", "hgt")
    return [
        [shift(tail, both, (1, 1)), shift(x, ("hgt",), (1,)), shift(head, both, (-1, 1))],
        [shift(tail, ("wid",), (1,)), x, shift(head, ("wid",), (-1,))],
        [shift(tail, both, (1, -1)), shift(x, ("hgt",), (-1,)), shift(head, both, (-1, -1))],
    ]


def report(values):
    count = lax.axis_size("len")
    pairs = [[2 * i, 2 * i + 1] for i in range(count // 2)]
    column = [list(range(core, count, 2)) for core in range(2)]
    values = lax.psum(values, "len", axis_index_groups=pairs)

    def total(values, axes, size, groups=None):
        copies = jnp.broadcast_to(values[None], (size,) + values.shape)
        got = lax.all_to_all(copies, axes, 0, 0, axis_index_groups=groups, tiled=True)
        return jnp.sum(got, axis=0)

    values = total(values, "len", count // 2, column)
    sides = lax.axis_size("wid") * lax.axis_size("hgt")
    return total(values, ("wid", "hgt"), sides)


def per_device(
    pressure_now, pressure_old, classes, admittance, source_cells, source_signal, receiver_cells
):
    s, to_left, to_right = pack(admittance, pressure_now, pressure_old, classes)
    from_right = shift(to_left, ("len",), (-1,))
    from_left = shift(to_right, ("len",), (1,))
    cells = spread(s)
    edges = spread(edge(from_right, from_left))
    pieces = []
    for part in range(3):
        pieces += cells[part] + edges[part]
    now, traces = march(source_cells, source_signal, receiver_cells.T, pieces)
    return now, report(traces)


def solution(mesh):
    block = P("hgt", "wid", "len")
    return jax.shard_map(
        per_device,
        mesh=mesh,
        in_specs=(block, block, block, P(), P(), P(), P()),
        out_specs=(block, P()),
        check_vma=False,
    )
```

time: 2160 us -> 189 us (0.09)
  blocking collectives: 1570 us -> 50.9 us
  starting transfers between devices: 308 us -> 60.7 us
  local copies, waits for them, and re-layouts: 109 us -> 11.7 us
  waiting for transfers between devices: 84.5 us -> 8.92 us
  other arithmetic: 70.1 us -> 0.64 us
  Pallas kernels: 0 us -> 52.3 us
    psum x16 -> x1, blocking collectives: 1570 us -> 7.36 us  [report(): values = lax.psum(values, 'len', axis_index_groups=pairs)]
    ppermute x96 -> x18, starting transfers between devices: 308 us -> 60.7 us  [shift(): return lax.ppermute(x, axes if len(axes) > 1 else axes[0], pairs)]
    ppermute x96 -> x18, waiting for transfers between devices: 84.5 us -> 8.92 us  [shift(): return lax.ppermute(x, axes if len(axes) > 1 else axes[0], pairs)]
    pallas_call x0 -> x3, Pallas kernels: none -> 52.3 us  [the longest x1 46.4 us: march(): pl.pallas_call(march_kernel, out_shape=(field(HIGH, WIDE, DEEP), field(ST...]
    all_to_all x0 -> x2, blocking collectives: none -> 43.6 us  [total(): lax.all_to_all(copies, axes, 0, 0, axis_index_groups=groups, tiled=True)]
    while x416 -> x0, local copies, waits for them, and re-layouts: 35.1 us -> none
    div x16 -> x0, other arithmetic: 28.7 us -> none  [update(): (2.0 * now - (1.0 - loss) * old + courant_sq * (beside - 6.0 * now)) / (1...]
    gather x16 -> x0, local copies, waits for them, and re-layouts: 23.7 us -> none  [sample(): field[local[:, 0], local[:, 1], local[:, 2]]]
  transfers between devices with their start and end apart: 96 -> 18, of which waited for: 48 -> 3; matrix products, arithmetic and copies ran while one was open for 2% -> 1% of each run, Pallas kernels for 0% -> 1%
where the time goes in v1:
time: 189 us; the launch traced here: 186 us
  starting transfers between devices  60.7 us (32%)
  Pallas kernels  52.3 us (28%)
  blocking collectives  50.9 us (27%)
  local copies, waits for them, and re-layouts  11.7 us (6%)
  waiting for transfers between devices  8.92 us (5%)
    ppermute x18, starting transfers between devices, shift(): return lax.ppermute(x, axes if len(axes) > 1 else axes[0], pairs)  60.7 us
    pallas_call x1, Pallas kernels, march(): pl.pallas_call(march_kernel, out_shape=(field(HIGH, WIDE, DEEP), field(ST...  46.4 us
    all_to_all x2, blocking collectives, total(): lax.all_to_all(copies, axes, 0, 0, axis_index_groups=groups, tiled=True)  43.6 us
    unnamed x39, local copies, waits for them, and re-layouts  10.9 us
    ppermute x18, waiting for transfers between devices, shift(): return lax.ppermute(x, axes if len(axes) > 1 else axes[0], pairs)  8.92 us
    psum x1, blocking collectives, report(): values = lax.psum(values, 'len', axis_index_groups=pairs)  7.36 us
    pallas_call x1, Pallas kernels, pack(): pl.pallas_call(pack_kernel, out_shape=(field(3, HIGH, WIDE, LANES), field...  4.67 us
  transfers between devices with their start and end apart: 18, of which 3 were waited for; matrix products, arithmetic and copies ran while one was open for 1% of the time, Pallas kernels for 1%

profile of v1, /device:TPU:1, one launch (start us, length us, event | category | flops | bytes accessed | tf_op | source)
XLA Modules:
  0.0 186.2 jit_solution(16657719830658620135)
XLA Ops:
  0.6 1.0 copy-done.2
  1.7 1.0 copy-done.3
  2.7 1.0 copy-done.4
  3.8 0.7 copy-done.15
  4.4 4.7 %pack.1 = (f32[3,16,64,128]{3,2,1,0:T(8,128)S(1)}, f32[16,32,128]{2,1,0:T(8,128)S(1)}, f32[16,32,128]{2,1,0:T(8,128)S(1)}) custom-call(f32[8]{0:T(128)S(1)} %copy-done.15, f32[16,64,128]{2,1,0:T(8,128)S(1)} %copy-done.2, f32[16,64,128]{2,1,0:T(8,128)S(1)} %copy-done.3, s32[16,64,128]{2,1,0:T(8,128)S(1)} %copy-done.4), custom_call_target="tpu_custom_call" | custom-call | tf_op jit(solution)/shard_map/pack/pallas_call | solution.py:235
  9.1 8.8 %collective-permute-start.3 = (f32[16,32,128]{2,1,0:T(8,128)S(1)}, f32[16,32,128]{2,1,0:T(8,128)S(1)}, u32[]{:S(2)}, u32[]{:S(2)}) collective-permute-start(f32[16,32,128]{2,1,0:T(8,128)S(1)} %get-tuple-element.8), channel_id=1, source_target_pairs={{32,0},{64,32},{96,64},{128,96},{160,128},{192,160},{224,192},{256... | collective-permute-start | bytes 786440 | tf_op jit(solution)/shard_map/ppermute | solution.py:294
  17.9 1.9 %collective-permute-start.4 = (f32[16,32,128]{2,1,0:T(8,128)S(1)}, f32[16,32,128]{2,1,0:T(8,128)S(1)}, u32[]{:S(2)}, u32[]{:S(2)}) collective-permute-start(f32[16,32,128]{2,1,0:T(8,128)S(1)} %get-tuple-element.9), channel_id=1, source_target_pairs={{0,32},{32,64},{64,96},{96,128},{128,160},{160,192},{192,224},{224... | collective-permute-start | bytes 786440 | tf_op jit(solution)/shard_map/ppermute | solution.py:294
  19.8 0.0 copy-start.13
  19.8 0.0 copy-start.14
  19.9 1.3 collective-permute-start.13
  21.2 5.2 %collective-permute-start.1 = (f32[3,16,64,128]{3,2,1,0:T(8,128)S(1)}, f32[3,16,64,128]{3,2,1,0:T(8,128)}, u32[]{:S(2)}, u32[]{:S(2)}) collective-permute-start(f32[3,16,64,128]{3,2,1,0:T(8,128)S(1)} %get-tuple-element.7.refs_7_), channel_id=1, source_target_pairs={{0,1},{1,2},{2,3},{4,5},{5,6},{6,7},{8,9},{9,10},{10,11},{12,13},{... | collective-permute-start | bytes 4718600 | tf_op jit(solution)/shard_map/ppermute | solution.py:294
  26.3 1.3 edge.1.refs_10_
  27.6 0.0 copy-start.1
  27.7 1.3 collective-permute-start.17
  29.0 1.3 collective-permute-start.11
  30.3 0.8 fusion
  31.1 0.7 collective-permute-start.7
  31.7 2.6 %collective-permute-done.17.refs_17_ = f32[16,16,128]{2,1,0:T(8,128)S(1)} collective-permute-done((f32[16,16,128]{2,1,0:T(8,128)S(1)}, f32[16,16,128]{2,1,0:T(8,128)S(1)}, u32[]{:S(2)}, u32[]{:S(2)}) %collective-permute-start.17) | collective-permute-done | bytes 131104 | tf_op jit(solution)/shard_map/ppermute | solution.py:294
  34.4 0.7 collective-permute-start.15
  35.0 0.0 collective-permute-done.11.refs_11_
  35.1 1.3 collective-permute-start.14
  36.4 0.6 copy-done.5
  37.0 3.2 %collective-permute-start.10 = (f32[16,16,128]{2,1,0:T(8,128)S(1)}, f32[16,16,128]{2,1,0:T(8,128)S(1)}, u32[]{:S(2)}, u32[]{:S(2)}) collective-permute-start(f32[16,16,128]{2,1,0:T(8,128)S(1)} %get-tuple-element.15), channel_id=1, source_target_pairs={{0,4},{4,8},{8,12},{12,16},{16,20},{20,24},{24,28},{1,5},{5,9},{9,... | collective-permute-start | bytes 393224 | tf_op jit(solution)/shard_map/ppermute | solution.py:294
  40.2 0.0 collective-permute-done.15.refs_15_
  40.2 0.7 copy-done.7
  40.9 1.3 collective-permute-start.9
  42.2 0.7 copy-done.9
  42.9 9.3 %collective-permute-start.5 = (f32[16,16,128]{2,1,0:T(8,128)S(1)}, f32[16,16,128]{2,1,0:T(8,128)S(1)}, u32[]{:S(2)}, u32[]{:S(2)}) collective-permute-start(f32[16,16,128]{2,1,0:T(8,128)S(1)} %get-tuple-element.15), channel_id=1, source_target_pairs={{0,5},{1,6},{2,7},{4,9},{5,10},{6,11},{8,13},{9,14},{10,15},{12,17... | collective-permute-start | bytes 393224 | tf_op jit(solution)/shard_map/ppermute | solution.py:294
  52.2 1.9 %collective-permute-done.5.refs_3_ = f32[16,16,128]{2,1,0:T(8,128)S(1)} collective-permute-done((f32[16,16,128]{2,1,0:T(8,128)S(1)}, f32[16,16,128]{2,1,0:T(8,128)S(1)}, u32[]{:S(2)}, u32[]{:S(2)}) %collective-permute-start.5) | collective-permute-done | bytes 131104 | tf_op jit(solution)/shard_map/ppermute | solution.py:294
  54.1 0.7 copy-done.11
  54.8 0.7 collective-permute-start.2
  55.5 0.7 collective-permute-start.12
  56.2 0.0 copy-done.16
  56.2 6.0 %collective-permute-start.8 = (f32[3,16,16,128]{3,2,1,0:T(8,128)}, f32[3,16,16,128]{3,2,1,0:T(8,128)S(1)}, u32[]{:S(2)}, u32[]{:S(2)}) collective-permute-start(f32[3,16,16,128]{3,2,1,0:T(8,128)} %get-tuple-element.13), channel_id=1, source_target_pairs={{0,4},{4,8},{8,12},{12,16},{16,20},{20,24},{24,28},{1,5},{5,9},{9,... | collective-permute-start | bytes 1179656 | tf_op jit(solution)/shard_map/ppermute | solution.py:294
  62.2 1.3 collective-permute-start.16
  63.5 7.2 %collective-permute-start.6 = (f32[16,64,128]{2,1,0:T(8,128)S(1)}, f32[16,64,128]{2,1,0:T(8,128)}, u32[]{:S(2)}, u32[]{:S(2)}) collective-permute-start(f32[16,64,128]{2,1,0:T(8,128)S(1)} %edge.1.refs_10_), channel_id=1, source_target_pairs={{0,1},{1,2},{2,3},{4,5},{5,6},{6,7},{8,9},{9,10},{10,11},{12,13},{... | collective-permute-start | bytes 1572872 | tf_op jit(solution)/shard_map/ppermute | solution.py:294
  70.8 8.7 %collective-permute-start = (f32[3,16,16,128]{3,2,1,0:T(8,128)}, f32[3,16,16,128]{3,2,1,0:T(8,128)S(1)}, u32[]{:S(2)}, u32[]{:S(2)}) collective-permute-start(f32[3,16,16,128]{3,2,1,0:T(8,128)} %get-tuple-element.13), channel_id=1, source_target_pairs={{0,5},{1,6},{2,7},{4,9},{5,10},{6,11},{8,13},{9,14},{10,15},{12,17... | collective-permute-start | bytes 1179656 | tf_op jit(solution)/shard_map/ppermute | solution.py:294
  79.5 0.8 copy.10.sig_ref
  80.3 4.3 %collective-permute-done.refs_0_ = f32[3,16,16,128]{3,2,1,0:T(8,128)S(1)} collective-permute-done((f32[3,16,16,128]{3,2,1,0:T(8,128)}, f32[3,16,16,128]{3,2,1,0:T(8,128)S(1)}, u32[]{:S(2)}, u32[]{:S(2)}) %collective-permute-start) | collective-permute-done | bytes 393248 | tf_op jit(solution)/shard_map/ppermute | solution.py:294
  84.6 0.9 copy-done.6
  85.5 0.9 copy-done.8
  86.4 0.9 copy-done.10
  87.3 0.9 copy-done.12
  88.2 46.4 %march.1 = (f32[16,64,128]{2,1,0:T(8,128)}, f32[16,128]{1,0:T(8,128)S(1)}) custom-call(s32[4,3]{1,0:T(4,128)S(1)} %copy-done.13, f32[16,4]{1,0:T(8,128)S(1)} %copy.10.sig_ref, s32[3,128]{1,0:T(4,128)S(1)} %bitcast.1, f32[3,16,16,128]{3,2,1,0:T(8,128)S(1)} %collective-permute-done.refs_0_, f32[3,16,64,128]{3,2,1,0:T(8,128)} %collective-permute-done.1.refs_1_, ...), custom_call_target="tpu_custom_call" | custom-call | tf_op jit(solution)/shard_map/march/pallas_call | solution.py:261
  134.6 7.4 %psum.7 = f32[16,128]{1,0:T(8,128)S(1)} all-reduce(f32[16,128]{1,0:T(8,128)S(1)} %get-tuple-element.11), channel_id=1, replica_groups={{0,32},{64,96},{128,160},{192,224},{256,288},{320,352},{384,416},{448,4..., use_global_device_ids=true, to_apply=%region_0.0 | all-reduce | flops 2048 | bytes 16384 | tf_op jit(solution)/shard_map/psum | solution.py:313
  142.0 16.5 %all_to_all.10 = f32[8,16,128]{2,1,0:T(8,128)S(1)} all-to-all(f32[8,16,128]{2,1,0:T(8,128)S(1)} %broadcast_in_dim.4), channel_id=1, replica_groups={{0,64,128,192,256,320,384,448},{32,96,160,224,288,352,416,480},{1,65,12..., dimensions={0} | all-to-all | bytes 131072 | tf_op jit(solution)/shard_map/all_to_all | solution.py:317
  158.5 27.0 %all_to_all.11 = f32[32,16,128]{2,1,0:T(8,128)S(1)} all-to-all(f32[32,16,128]{2,1,0:T(8,128)S(1)} %broadcast_in_dim.5), channel_id=1, replica_groups=mesh['len'=16,'wid'=8,'hgt'=4] {'wid','hgt'}, dimensions={0} | all-to-all | bytes 524288 | tf_op jit(solution)/shard_map/all_to_all | solution.py:317
  185.6 0.6 reduce_sum.19
  (39 shorter events, 0.1 us)
Async XLA Ops:
  0.6 1.0 copy-start.2
  1.7 1.0 copy-start.3
  2.7 1.0 copy-start.4
  3.8 0.7 copy-start.15
  9.1 22.0 %copy-start = (f32[3,16,64,128]{3,2,1,0:T(8,128)}, f32[3,16,64,128]{3,2,1,0:T(8,128)S(1)}, u32[]{:S(2)}) copy-start(f32[3,16,64,128]{3,2,1,0:T(8,128)S(1)} %get-tuple-element.7.refs_7_) | copy-start | bytes 4718596
  9.1 17.2 %collective-permute-start.3 = (f32[16,32,128]{2,1,0:T(8,128)S(1)}, f32[16,32,128]{2,1,0:T(8,128)S(1)}, u32[]{:S(2)}, u32[]{:S(2)}) collective-permute-start(f32[16,32,128]{2,1,0:T(8,128)S(1)} %get-tuple-element.8), channel_id=1, source_target_pairs={{32,0},{64,32},{96,64},{128,96},{160,128},{192,160},{224,192},{256... | collective-permute-start | bytes 786440 | tf_op jit(solution)/shard_map/ppermute | solution.py:294
  17.9 8.4 %collective-permute-start.4 = (f32[16,32,128]{2,1,0:T(8,128)S(1)}, f32[16,32,128]{2,1,0:T(8,128)S(1)}, u32[]{:S(2)}, u32[]{:S(2)}) collective-permute-start(f32[16,32,128]{2,1,0:T(8,128)S(1)} %get-tuple-element.9), channel_id=1, source_target_pairs={{0,32},{32,64},{64,96},{96,128},{128,160},{160,192},{192,224},{224... | collective-permute-start | bytes 786440 | tf_op jit(solution)/shard_map/ppermute | solution.py:294
  19.8 64.7 %copy-start.13 = (s32[4,3]{1,0:T(4,128)S(1)}, s32[4,3]{1,0:T(4,128)}, u32[]{:S(2)}) copy-start(s32[4,3]{1,0:T(4,128)} %src_ref.1) | copy-start | bytes 148
  19.8 64.7 %copy-start.14 = (s32[128,3]{0,1:T(4,128)S(1)}, s32[128,3]{0,1:T(4,128)}, u32[]{:S(2)}) copy-start(s32[128,3]{0,1:T(4,128)} %param.13) | copy-start | bytes 4612
  19.9 64.7 %collective-permute-start.13 = (f32[3,16,64,128]{3,2,1,0:T(8,128)S(1)}, f32[3,16,64,128]{3,2,1,0:T(8,128)}, u32[]{:S(2)}, u32[]{:S(2)}) collective-permute-start(f32[3,16,64,128]{3,2,1,0:T(8,128)S(1)} %get-tuple-element.7.refs_7_), channel_id=1, source_target_pairs={{1,0},{2,1},{3,2},{5,4},{6,5},{7,6},{9,8},{10,9},{11,10},{13,12},{... | collective-permute-start | bytes 4718600 | tf_op jit(solution)/shard_map/ppermute | solution.py:294
  21.2 63.4 %collective-permute-start.1 = (f32[3,16,64,128]{3,2,1,0:T(8,128)S(1)}, f32[3,16,64,128]{3,2,1,0:T(8,128)}, u32[]{:S(2)}, u32[]{:S(2)}) collective-permute-start(f32[3,16,64,128]{3,2,1,0:T(8,128)S(1)} %get-tuple-element.7.refs_7_), channel_id=1, source_target_pairs={{0,1},{1,2},{2,3},{4,5},{5,6},{6,7},{8,9},{9,10},{10,11},{12,13},{... | collective-permute-start | bytes 4718600 | tf_op jit(solution)/shard_map/ppermute | solution.py:294
  27.6 56.9 %copy-start.1 = (f32[16,64,128]{2,1,0:T(8,128)}, f32[16,64,128]{2,1,0:T(8,128)S(1)}, u32[]{:S(2)}) copy-start(f32[16,64,128]{2,1,0:T(8,128)S(1)} %edge.1.refs_10_) | copy-start | bytes 1572868
  27.7 6.7 %collective-permute-start.17 = (f32[16,16,128]{2,1,0:T(8,128)S(1)}, f32[16,16,128]{2,1,0:T(8,128)S(1)}, u32[]{:S(2)}, u32[]{:S(2)}) collective-permute-start(f32[16,16,128]{2,1,0:T(8,128)S(1)} %get-tuple-element.14), channel_id=1, source_target_pairs={{5,0},{6,1},{7,2},{9,4},{10,5},{11,6},{13,8},{14,9},{15,10},{17,12... | collective-permute-start | bytes 393224 | tf_op jit(solution)/shard_map/ppermute | solution.py:294
  29.0 6.1 %collective-permute-start.11 = (f32[16,16,128]{2,1,0:T(8,128)S(1)}, f32[16,16,128]{2,1,0:T(8,128)S(1)}, u32[]{:S(2)}, u32[]{:S(2)}) collective-permute-start(f32[16,16,128]{2,1,0:T(8,128)S(1)} %get-tuple-element.14), channel_id=1, source_target_pairs={{4,0},{8,4},{12,8},{16,12},{20,16},{24,20},{28,24},{5,1},{9,5},{13... | collective-permute-start | bytes 393224 | tf_op jit(solution)/shard_map/ppermute | solution.py:294
  31.1 5.3 %collective-permute-start.7 = (f32[16,16,128]{2,1,0:T(8,128)S(1)}, f32[16,16,128]{2,1,0:T(8,128)S(1)}, u32[]{:S(2)}, u32[]{:S(2)}) collective-permute-start(f32[16,16,128]{2,1,0:T(8,128)S(1)} %get-tuple-element.14), channel_id=1, source_target_pairs={{4,1},{5,2},{6,3},{8,5},{9,6},{10,7},{12,9},{13,10},{14,11},{16,13... | collective-permute-start | bytes 393224 | tf_op jit(solution)/shard_map/ppermute | solution.py:294
  34.4 5.9 %collective-permute-start.15 = (f32[16,16,128]{2,1,0:T(8,128)S(1)}, f32[16,16,128]{2,1,0:T(8,128)S(1)}, u32[]{:S(2)}, u32[]{:S(2)}) collective-permute-start(f32[16,16,128]{2,1,0:T(8,128)S(1)} %get-tuple-element.15), channel_id=1, source_target_pairs={{1,4},{2,5},{3,6},{5,8},{6,9},{7,10},{9,12},{10,13},{11,14},{13,16... | collective-permute-start | bytes 393224 | tf_op jit(solution)/shard_map/ppermute | solution.py:294
  35.1 20.4 %collective-permute-start.14 = (f32[3,16,16,128]{3,2,1,0:T(8,128)S(1)}, f32[3,16,16,128]{3,2,1,0:T(8,128)S(1)}, u32[]{:S(2)}, u32[]{:S(2)}) collective-permute-start(f32[3,16,16,128]{3,2,1,0:T(8,128)S(1)} %get-tuple-element.12), channel_id=1, source_target_pairs={{5,0},{6,1},{7,2},{9,4},{10,5},{11,6},{13,8},{14,9},{15,10},{17,12... | collective-permute-start | bytes 1179656 | tf_op jit(solution)/shard_map/ppermute | solution.py:294
  36.4 0.7 copy-start.5
  37.0 5.2 %collective-permute-start.10 = (f32[16,16,128]{2,1,0:T(8,128)S(1)}, f32[16,16,128]{2,1,0:T(8,128)S(1)}, u32[]{:S(2)}, u32[]{:S(2)}) collective-permute-start(f32[16,16,128]{2,1,0:T(8,128)S(1)} %get-tuple-element.15), channel_id=1, source_target_pairs={{0,4},{4,8},{8,12},{12,16},{16,20},{20,24},{24,28},{1,5},{5,9},{9,... | collective-permute-start | bytes 393224 | tf_op jit(solution)/shard_map/ppermute | solution.py:294
  40.2 0.7 copy-start.7
  40.9 15.3 %collective-permute-start.9 = (f32[3,16,16,128]{3,2,1,0:T(8,128)S(1)}, f32[3,16,16,128]{3,2,1,0:T(8,128)S(1)}, u32[]{:S(2)}, u32[]{:S(2)}) collective-permute-start(f32[3,16,16,128]{3,2,1,0:T(8,128)S(1)} %get-tuple-element.12), channel_id=1, source_target_pairs={{4,0},{8,4},{12,8},{16,12},{20,16},{24,20},{28,24},{5,1},{9,5},{13... | collective-permute-start | bytes 1179656 | tf_op jit(solution)/shard_map/ppermute | solution.py:294
  42.2 0.7 copy-start.9
  42.9 11.2 %collective-permute-start.5 = (f32[16,16,128]{2,1,0:T(8,128)S(1)}, f32[16,16,128]{2,1,0:T(8,128)S(1)}, u32[]{:S(2)}, u32[]{:S(2)}) collective-permute-start(f32[16,16,128]{2,1,0:T(8,128)S(1)} %get-tuple-element.15), channel_id=1, source_target_pairs={{0,5},{1,6},{2,7},{4,9},{5,10},{6,11},{8,13},{9,14},{10,15},{12,17... | collective-permute-start | bytes 393224 | tf_op jit(solution)/shard_map/ppermute | solution.py:294
  54.1 0.7 copy-start.11
  54.8 7.4 %collective-permute-start.2 = (f32[3,16,16,128]{3,2,1,0:T(8,128)S(1)}, f32[3,16,16,128]{3,2,1,0:T(8,128)S(1)}, u32[]{:S(2)}, u32[]{:S(2)}) collective-permute-start(f32[3,16,16,128]{3,2,1,0:T(8,128)S(1)} %get-tuple-element.12), channel_id=1, source_target_pairs={{4,1},{5,2},{6,3},{8,5},{9,6},{10,7},{12,9},{13,10},{14,11},{16,13... | collective-permute-start | bytes 1179656 | tf_op jit(solution)/shard_map/ppermute | solution.py:294
  55.5 0.8 copy-start.16
  55.5 8.1 %collective-permute-start.12 = (f32[3,16,16,128]{3,2,1,0:T(8,128)}, f32[3,16,16,128]{3,2,1,0:T(8,128)S(1)}, u32[]{:S(2)}, u32[]{:S(2)}) collective-permute-start(f32[3,16,16,128]{3,2,1,0:T(8,128)} %get-tuple-element.13), channel_id=1, source_target_pairs={{1,4},{2,5},{3,6},{5,8},{6,9},{7,10},{9,12},{10,13},{11,14},{13,16... | collective-permute-start | bytes 1179656 | tf_op jit(solution)/shard_map/ppermute | solution.py:294
  56.2 14.6 %copy-start.17 = (f32[3,16,16,128]{3,2,1,0:T(8,128)}, f32[3,16,16,128]{3,2,1,0:T(8,128)S(1)}, u32[]{:S(2)}) copy-start(f32[3,16,16,128]{3,2,1,0:T(8,128)S(1)} %collective-permute-done.9.refs_8_) | copy-start | bytes 1179652
  56.2 14.6 %collective-permute-start.8 = (f32[3,16,16,128]{3,2,1,0:T(8,128)}, f32[3,16,16,128]{3,2,1,0:T(8,128)S(1)}, u32[]{:S(2)}, u32[]{:S(2)}) collective-permute-start(f32[3,16,16,128]{3,2,1,0:T(8,128)} %get-tuple-element.13), channel_id=1, source_target_pairs={{0,4},{4,8},{8,12},{12,16},{16,20},{20,24},{24,28},{1,5},{5,9},{9,... | collective-permute-start | bytes 1179656 | tf_op jit(solution)/shard_map/ppermute | solution.py:294
  62.2 22.3 %collective-permute-start.16 = (f32[16,64,128]{2,1,0:T(8,128)S(1)}, f32[16,64,128]{2,1,0:T(8,128)}, u32[]{:S(2)}, u32[]{:S(2)}) collective-permute-start(f32[16,64,128]{2,1,0:T(8,128)S(1)} %edge.1.refs_10_), channel_id=1, source_target_pairs={{1,0},{2,1},{3,2},{5,4},{6,5},{7,6},{9,8},{10,9},{11,10},{13,12},{... | collective-permute-start | bytes 1572872 | tf_op jit(solution)/shard_map/ppermute | solution.py:294
  63.5 7.3 %copy-start.18 = (f32[3,16,16,128]{3,2,1,0:T(8,128)}, f32[3,16,16,128]{3,2,1,0:T(8,128)S(1)}, u32[]{:S(2)}) copy-start(f32[3,16,16,128]{3,2,1,0:T(8,128)S(1)} %collective-permute-done.12.refs_12_) | copy-start | bytes 1179652
  63.5 21.0 %collective-permute-start.6 = (f32[16,64,128]{2,1,0:T(8,128)S(1)}, f32[16,64,128]{2,1,0:T(8,128)}, u32[]{:S(2)}, u32[]{:S(2)}) collective-permute-start(f32[16,64,128]{2,1,0:T(8,128)S(1)} %edge.1.refs_10_), channel_id=1, source_target_pairs={{0,1},{1,2},{2,3},{4,5},{5,6},{6,7},{8,9},{9,10},{10,11},{12,13},{... | collective-permute-start | bytes 1572872 | tf_op jit(solution)/shard_map/ppermute | solution.py:294
  70.8 13.7 %collective-permute-start = (f32[3,16,16,128]{3,2,1,0:T(8,128)}, f32[3,16,16,128]{3,2,1,0:T(8,128)S(1)}, u32[]{:S(2)}, u32[]{:S(2)}) collective-permute-start(f32[3,16,16,128]{3,2,1,0:T(8,128)} %get-tuple-element.13), channel_id=1, source_target_pairs={{0,5},{1,6},{2,7},{4,9},{5,10},{6,11},{8,13},{9,14},{10,15},{12,17... | collective-permute-start | bytes 1179656 | tf_op jit(solution)/shard_map/ppermute | solution.py:294
  84.6 0.9 copy-start.6
  85.5 0.9 copy-start.8
  86.4 0.9 copy-start.10
  87.3 0.9 copy-start.12

commit v2 on v0

v2 whole, which is shorter than its diff:
```python
import functools

import jax
import jax.numpy as jnp
from jax import lax
from jax.experimental import pallas as pl
from jax.experimental.pallas import tpu as pltpu
from jax.sharding import PartitionSpec as P

STEPS = 16
HALO = 16
LANES = 128
HIGH, WIDE, DEEP = 16, 64, 128
HALF = HIGH // 2
TALL = HIGH + 2 * HALO
BROAD = WIDE + 2 * HALO
COLS = BROAD // 8
RIM = 3 * 2 * HALO + BROAD
VMEM = pl.BlockSpec(memory_space=pltpu.VMEM)
SMEM = pl.BlockSpec(memory_space=pltpu.SMEM)


def lane_ids():
    return lax.broadcasted_iota(jnp.int32, (8, LANES), 1)


def regroup(rows, order):
    return jnp.take_along_axis(rows, order, axis=1, mode="promise_in_bounds")


def even_odd():
    lane = lane_ids()
    return jnp.where(lane < 64, 2 * lane, 2 * lane - 127)


def in_order():
    lane = lane_ids()
    return (lane // 2) + 64 * (lane % 2)


def pack_kernel(adm_ref, now_ref, old_ref, cls_ref, s_ref, left_ref, right_ref):
    lane = lane_ids()
    order = even_odd()

    def layer(h, carry):
        rims = []
        for j in range(WIDE // 8):
            rows = pl.ds(8 * j, 8)
            kinds = cls_ref[h, rows, :]
            loss = jnp.zeros((8, LANES), jnp.float32)
            for index in range(adm_ref.shape[0]):
                loss = jnp.where(kinds == index + 1, adm_ref[index], loss)
            gain = jnp.float32(1.0 / 3.0) / (1.0 + loss)
            rim = None
            for a, field in enumerate((now_ref[h, rows, :], old_ref[h, rows, :], gain)):
                split = regroup(field, order)
                s_ref[h, a, rows, :] = split
                moved = pltpu.roll(split, 72, 1)
                both = jnp.where((lane < 8) | ((lane >= 56) & (lane < 64)), split, moved)
                if a == 0:
                    rim = both
                else:
                    both = pltpu.roll(both, 16 * a, 1)
                    here = (lane >= 16 * a) & (lane < 16 * a + 16)
                    here = here | ((lane >= 56 + 16 * a) & (lane < 72 + 16 * a))
                    rim = jnp.where(here, both, rim)
            rims.append(rim)
        half = WIDE // 16
        for j in range(half):
            rows = pl.ds(8 * j, 8)
            other = pltpu.roll(rims[j + half], 64, 1)
            left_ref[h, rows, :] = jnp.where(lane < 56, rims[j], other)
            right_ref[h, rows, :] = jnp.where((lane >= 56) & (lane < 104), rims[j], other)
        return carry

    lax.fori_loop(0, now_ref.shape[0], layer, 0)


def edge_kernel(from_right_ref, from_left_ref, s_ref, e_ref, head_ref, tail_ref):
    lane = lane_ids()
    zero = jnp.float32(0.0)
    used = (lane < 48) | ((lane >= 56) & (lane < 104))

    def layer(h, carry):
        half = WIDE // 16
        for j in range(half):
            rows = pl.ds(8 * j, 8)
            a, b = from_right_ref[h, rows, :], from_left_ref[h, rows, :]
            first = jnp.where(lane < 48, a, b)
            second = pltpu.roll(jnp.where((lane >= 64) & (lane < 112), a, b), 64, 1)
            e_ref[h, rows, :] = jnp.where(used, first, zero)
            e_ref[h, pl.ds(8 * (j + half), 8), :] = jnp.where(used, second, zero)
        for a in range(3):
            head_ref[h, a] = s_ref[h, a, pl.ds(0, HALO), :]
            tail_ref[h, a] = s_ref[h, a, pl.ds(WIDE - HALO, HALO), :]
        head_ref[h, 3] = e_ref[h, pl.ds(0, HALO), :]
        tail_ref[h, 3] = e_ref[h, pl.ds(WIDE - HALO, HALO), :]
        return carry

    lax.fori_loop(0, HIGH, layer, 0)


def beside_lanes(i):
    lane = lane_ids()
    k = lane % 8
    n = (HALO - i) // 2
    right = lane < 48
    return right, n, (right & (k < n)) | (~right & (k >= 8 - n))


def rim_kernel(e_ref, before_ref, after_ref, low_ref, top_ref):
    row = lax.broadcasted_iota(jnp.int32, (HALO, LANES), 0)

    def pair(out_ref, i, near, far):
        for a in range(3):
            at = 2 * HALO * a
            kept = jnp.where(row > i, before_ref[near, a], pltpu.roll(before_ref[far, a], i, 0))
            out_ref[i, pl.ds(at, HALO), :] = kept
            moved = pltpu.roll(after_ref[far, a], (HALO - i) % HALO, 0)
            out_ref[i, pl.ds(at + HALO, HALO), :] = jnp.where(row < HALO - i - 1, after_ref[near, a], moved)
        right, n, mask = beside_lanes(i)
        for j in range(COLS):
            if j < HALO // 8:
                a, b = before_ref[near, 3, pl.ds(8 * j, 8), :], before_ref[far, 3, pl.ds(8 * j, 8), :]
            elif j < COLS - HALO // 8:
                at = 8 * j - HALO
                a, b = e_ref[near, pl.ds(at, 8), :], e_ref[far, pl.ds(at, 8), :]
            else:
                at = 8 * j - HALO - WIDE
                a, b = after_ref[near, 3, pl.ds(at, 8), :], after_ref[far, 3, pl.ds(at, 8), :]
            moved = jnp.where(right, pltpu.roll(b, n, 1), pltpu.roll(b, LANES - n, 1))
            out_ref[i, pl.ds(6 * HALO + 8 * j, 8), :] = jnp.where(mask, a, moved)

    def both(i, carry):
        pair(low_ref, i, i, HIGH - 1 - i)
        pair(top_ref, i, HIGH - 1 - i, i)
        return carry

    lax.fori_loop(0, HALF, both, 0)


def fill(refs, temp, at):
    lane = lane_ids()
    zero = jnp.float32(0.0)
    fringe = ((lane >= 64) & (lane < 72)) | (lane >= 120)
    for j in range(COLS):
        edge = temp[3, pl.ds(j, 8, stride=COLS), :]
        for a, ref in enumerate(refs):
            main = temp[a, pl.ds(j, 8, stride=COLS), :]
            for parity in range(2):
                near = pltpu.roll(edge, 64 - 8 * (2 * a + parity), 1)
                near = jnp.where(fringe, near, zero)
                mid = pltpu.roll(main, 64, 1) if parity else main
                ref[parity, at, j] = jnp.where(lane < 64, mid, near)


def fill_own(refs, temp, s_ref, e_ref, before_ref, after_ref):
    def layer(h, carry):
        for a in range(3):
            temp[a, pl.ds(HALO, WIDE), :] = s_ref[h, a]
        temp[3, pl.ds(HALO, WIDE), :] = e_ref[h]
        for a in range(4):
            temp[a, pl.ds(0, HALO), :] = before_ref[h, a]
            temp[a, pl.ds(HALO + WIDE, HALO), :] = after_ref[h, a]
        fill(refs, temp, HALO + h)
        return carry

    lax.fori_loop(0, HIGH, layer, 0)


def fill_beside(refs, temp, s_ref, rim_ref, layers):
    def pair(i, carry):
        near, far = layers(i)
        for a in range(3):
            temp[a, pl.ds(0, HALO), :] = rim_ref[i, pl.ds(2 * HALO * a, HALO), :]
            temp[a, pl.ds(HALO, WIDE), :] = s_ref[near % HIGH, a]
            temp[a, pl.ds(HALO + WIDE, HALO), :] = rim_ref[i, pl.ds(2 * HALO * a + HALO, HALO), :]
        temp[3] = rim_ref[i, pl.ds(6 * HALO, BROAD), :]
        fill(refs, temp, near)
        for a in range(3):
            before = rim_ref[i, pl.ds(2 * HALO * a, HALO), :]
            temp[a, pl.ds(0, HALO), :] = pltpu.roll(before, (HALO - i) % HALO, 0)
            temp[a, pl.ds(HALO, WIDE), :] = s_ref[far % HIGH, a]
            after = rim_ref[i, pl.ds(2 * HALO * a + HALO, HALO), :]
            temp[a, pl.ds(HALO + WIDE, HALO), :] = pltpu.roll(after, i, 0)
        right, n, _ = beside_lanes(i)
        k = lane_ids() % 8
        mask = (right & (k < 8 - n)) | (~right & (k >= n))
        for j in range(COLS):
            both = rim_ref[i, pl.ds(6 * HALO + 8 * j, 8), :]
            moved = jnp.where(right, pltpu.roll(both, LANES - n, 1), pltpu.roll(both, n, 1))
            temp[3, pl.ds(8 * j, 8), :] = jnp.where(mask, moved, jnp.float32(0.0))
        fill(refs, temp, far)
        return carry

    lax.fori_loop(0, HALF, pair, 0)


def corner():
    return (
        lax.axis_index("hgt") * HIGH - HALO,
        lax.axis_index("wid") * WIDE - HALO,
        lax.axis_index("len") * DEEP,
    )


def list_receivers(rec_ref, todo):
    start = corner()

    def note(r, count):
        h = rec_ref[0, r] - start[0]
        w = rec_ref[1, r] - start[1]
        d = rec_ref[2, r] - start[2]
        mine = (h >= HALO) & (h < HALO + HIGH) & (w >= HALO) & (w < HALO + WIDE)
        mine = mine & (d >= 0) & (d < DEEP)

        @pl.when(mine)
        def _():
            todo[0, count] = r
            todo[1, count] = h
            todo[2, count] = w % COLS
            todo[3, count] = w // COLS
            todo[4, count] = d % 2
            todo[5, count] = d // 2

        return count + mine.astype(jnp.int32)

    return lax.fori_loop(0, rec_ref.shape[1], note, jnp.int32(0))


def list_sources(src_ref):
    lane = lane_ids()
    row = lax.broadcasted_iota(jnp.int32, (8, LANES), 0)
    start = corner()
    points = []
    for s in range(src_ref.shape[0]):
        h = src_ref[s, 0] - start[0]
        w = src_ref[s, 1] - start[1]
        d = src_ref[s, 2] - start[2] + HALO
        near = (h >= 0) & (h < TALL) & (w >= 0) & (w < BROAD) & (d >= 0) & (d < DEEP + 2 * HALO)
        h = jnp.clip(h, 0, TALL - 1)
        w = jnp.clip(w, 0, BROAD - 1)
        d = jnp.clip(d, 0, DEEP + 2 * HALO - 1)
        place = (d // 2 + LANES - HALO // 2) % LANES
        points.append((near, d % 2, h, w % COLS, (row == w // COLS) & (lane == place)))
    return points


def sweep(now, old, p_ref, low, high):
    def chunk(first, layers):
        for u in range(layers):
            h = first + u
            for parity in range(2):
                other = [now[1 - parity, h, j] for j in range(COLS)]
                mine = [now[parity, h, j] for j in range(COLS)]
                for j in range(COLS):
                    before = mine[j - 1] if j > 0 else pltpu.roll(mine[COLS - 1], 1, 0)
                    after = mine[j + 1] if j < COLS - 1 else pltpu.roll(mine[0], 7, 0)
                    beside = other[j] + pltpu.roll(other[j], 127 if parity else 1, 1)
                    total = (now[parity, h - 1, j] + now[parity, h + 1, j]) + (before + after)
                    total = total + beside
                    past = old[parity, h, j]
                    old[parity, h, j] = past + p_ref[parity, h, j] * (total - 6.0 * past)

    fours = (high - low) // 4

    def four(i, carry):
        chunk(low + 4 * i, 4)
        return carry

    def two(i, carry):
        chunk(low + 4 * fours + 2 * i, 2)
        return carry

    lax.fori_loop(0, fours, four, 0)
    lax.fori_loop(0, (high - low - 4 * fours) // 2, two, 0)


def march_kernel(src_ref, sig_ref, rec_ref, *refs):
    s_ref, e_ref, before_ref, after_ref = refs[:4]
    under, under_rim, over, over_rim = refs[4:8]
    out_ref, trace_ref = refs[8:10]
    a_ref, b_ref, p_ref, temp, hist, todo = refs[10:]
    zero = jnp.float32(0.0)
    fields = (a_ref, b_ref, p_ref)

    fill_own(fields, temp, s_ref, e_ref, before_ref, after_ref)
    fill_beside(fields, temp, under, under_rim, lambda i: (HALO - 1 - i, i))
    fill_beside(fields, temp, over, over_rim, lambda i: (HALO + HIGH + i, TALL - 1 - i))

    count = list_receivers(rec_ref, todo)
    points = list_sources(src_ref)

    def step(now, old, t):
        sweep(now, old, p_ref, t + 1, TALL - t - 1)
        for s, (near, parity, h, j, spot) in enumerate(points):

            @pl.when(near)
            def _():
                old[parity, h, j] = old[parity, h, j] + jnp.where(spot, sig_ref[t, s], zero)

        def keep(i, carry):
            value = old[todo[4, i], todo[1, i], todo[2, i], pl.ds(todo[3, i], 1), :]
            hist[i, pl.ds(t, 1), :] = value
            return carry

        lax.fori_loop(0, count, keep, 0)

    def pair(i, carry):
        step(a_ref, b_ref, 2 * i)
        step(b_ref, a_ref, 2 * i + 1)
        return carry

    lax.fori_loop(0, STEPS // 2, pair, 0)

    trace_ref[0] = jnp.zeros((STEPS, LANES), jnp.float32)
    wide_lane = lax.broadcasted_iota(jnp.int32, (STEPS, LANES), 1)

    def gather(i, carry):
        number = todo[0, i]
        moved = pltpu.roll(hist[i], (number - todo[5, i] + LANES) % LANES, 1)
        trace_ref[0] = jnp.where(wide_lane == number, moved, trace_ref[0])
        return carry

    lax.fori_loop(0, count, gather, 0)
    for i in range(1, trace_ref.shape[0]):
        trace_ref[i] = trace_ref[0]

    lane = lane_ids()
    plain = temp.at[0]

    def hand_on(h, carry):
        for j in range(COLS):
            even, odd = a_ref[0, HALO + h, j], a_ref[1, HALO + h, j]
            joined = jnp.where(lane < 64, even, pltpu.roll(odd, 64, 1))
            plain[pl.ds(j, 8, stride=COLS), :] = joined
        out_ref[h] = plain[pl.ds(HALO, WIDE), :]
        return carry

    lax.fori_loop(0, HIGH, hand_on, 0)


def order_kernel(split_ref, out_ref):
    order = in_order()

    def layer(h, carry):
        for j in range(WIDE // 8):
            rows = pl.ds(8 * j, 8)
            out_ref[h, rows, :] = regroup(split_ref[h, rows, :], order)
        return carry

    lax.fori_loop(0, split_ref.shape[0], layer, 0)


def relay_kernel(got_ref, out_ref):
    total = got_ref[0]
    for i in range(1, got_ref.shape[0]):
        total = total + got_ref[i]
    for i in range(out_ref.shape[0]):
        out_ref[i] = total


def field(*shape):
    return jax.ShapeDtypeStruct(shape, jnp.float32)


def call(kernel, name, outs, ins, scratch=(), scalars=0, limit=8):
    return pl.pallas_call(
        kernel,
        out_shape=tuple(field(*shape) for shape in outs),
        in_specs=[SMEM] * scalars + [VMEM] * (len(ins) - scalars),
        out_specs=tuple(VMEM for _ in outs),
        scratch_shapes=list(scratch),
        name=name,
        compiler_params=pltpu.CompilerParams(vmem_limit_bytes=limit << 20),
    )(*ins)


def shift(x, axis, move):
    size = lax.axis_size(axis)
    pairs = [(i, i + move) for i in range(size) if 0 <= i + move < size]
    return lax.ppermute(x, axis, pairs)


def per_device(
    pressure_now, pressure_old, classes, admittance, source_cells, source_signal, receiver_cells
):
    parts = 4
    layers = HIGH // parts

    def block(*shape):
        return pl.BlockSpec((layers,) + shape, lambda i: (i,) + (0,) * len(shape))

    s, to_left, to_right = pl.pallas_call(
        pack_kernel,
        grid=(parts,),
        out_shape=(
            field(HIGH, 3, WIDE, LANES),
            field(HIGH, WIDE // 2, LANES),
            field(HIGH, WIDE // 2, LANES),
        ),
        in_specs=[SMEM] + [block(WIDE, LANES)] * 3,
        out_specs=(block(3, WIDE, LANES), block(WIDE // 2, LANES), block(WIDE // 2, LANES)),
        name="pack",
        compiler_params=pltpu.CompilerParams(vmem_limit_bytes=8 << 20),
    )(admittance, pressure_now, pressure_old, classes)
    from_right = shift(to_left, "len", -1)
    from_left = shift(to_right, "len", 1)
    over, under = shift(s, "hgt", -1), shift(s, "hgt", 1)
    face = (HIGH, 4, HALO, LANES)
    edge, head, tail = call(
        edge_kernel, "edge", [(HIGH, WIDE, LANES), face, face], [from_right, from_left, s]
    )
    before = shift(tail, "wid", 1)
    after = shift(head, "wid", -1)
    rim = (HALF, RIM, LANES)
    low, top = call(rim_kernel, "rim", [rim, rim], [edge, before, after])
    over_rim, under_rim = shift(low, "hgt", -1), shift(top, "hgt", 1)
    state = pltpu.VMEM((2, TALL, COLS, 8, LANES), jnp.float32)
    depth = lax.axis_size("len")
    sides = lax.axis_size("wid") * lax.axis_size("hgt")
    split, traces = call(
        march_kernel,
        "march",
        [(HIGH, WIDE, LANES), (depth, STEPS, LANES)],
        [source_cells, source_signal, receiver_cells.T, s, edge, before, after]
        + [under, under_rim, over, over_rim],
        scratch=[
            state,
            state,
            state,
            pltpu.VMEM((4, BROAD, LANES), jnp.float32),
            pltpu.VMEM((LANES, STEPS, LANES), jnp.float32),
            pltpu.SMEM((8, LANES), jnp.int32),
        ],
        scalars=3,
        limit=LIMIT,
    )
    traces = lax.all_to_all(traces, "len", 0, 0, tiled=True)
    (traces,) = call(relay_kernel, "relay", [(sides, STEPS, LANES)], [traces])
    traces = lax.all_to_all(traces, ("wid", "hgt"), 0, 0, tiled=True)
    (now,) = call(order_kernel, "order", [(HIGH, WIDE, DEEP)], [split])
    return now, jnp.sum(traces, axis=0)


LIMIT = 32


def solution(mesh):
    block = P("hgt", "wid", "len")
    return jax.shard_map(
        per_device,
        mesh=mesh,
        in_specs=(block, block, block, P(), P(), P(), P()),
        out_specs=(block, P()),
        check_vma=False,
    )
```

time: 2160 us -> 161 us (0.07)
  blocking collectives: 1570 us -> 16.8 us
  starting transfers between devices: 308 us -> 35 us
  local copies, waits for them, and re-layouts: 109 us -> 5.7 us
  other arithmetic: 70.1 us -> 0.63 us
  Pallas kernels: 0 us -> 52.8 us
  waiting for transfers between devices: 84.5 us -> 48.3 us
    psum x16 -> x0, blocking collectives: 1570 us -> none  [report(): return lax.psum(values, ('len', 'wid', 'hgt'))]
    ppermute x96 -> x8, starting transfers between devices: 308 us -> 23.4 us  [shift(): return lax.ppermute(x, axis, pairs)]
    pallas_call x0 -> x6, Pallas kernels: none -> 52.8 us  [the longest x5 47.6 us: call(): pl.pallas_call(kernel, out_shape=tuple((field(*shape) for shape in outs))...]
    ppermute x96 -> x8, waiting for transfers between devices: 84.5 us -> 39.1 us  [shift(): return lax.ppermute(x, axis, pairs)]
    while x416 -> x0, local copies, waits for them, and re-layouts: 35.1 us -> none
    div x16 -> x0, other arithmetic: 28.7 us -> none  [update(): (2.0 * now - (1.0 - loss) * old + courant_sq * (beside - 6.0 * now)) / (1...]
    gather x16 -> x0, local copies, waits for them, and re-layouts: 23.7 us -> none  [sample(): field[local[:, 0], local[:, 1], local[:, 2]]]
  transfers between devices with their start and end apart: 96 -> 9, of which waited for: 48 -> 4; matrix products, arithmetic and copies ran while one was open for 2% -> 0% of each run, Pallas kernels for 0% -> 3%
where the time goes in v2:
time: 161 us; the launch traced here: 160 us
  Pallas kernels  52.8 us (33%)
  waiting for transfers between devices  48.3 us (30%)
  starting transfers between devices  35 us (22%)
  blocking collectives  16.8 us (10%)
  local copies, waits for them, and re-layouts  5.7 us (4%)
    pallas_call x5, Pallas kernels, call(): pl.pallas_call(kernel, out_shape=tuple((field(*shape) for shape in outs))...  47.6 us
    ppermute x8, waiting for transfers between devices, shift(): return lax.ppermute(x, axis, pairs)  39.1 us
    ppermute x8, starting transfers between devices, shift(): return lax.ppermute(x, axis, pairs)  23.4 us
    all_to_all x1, blocking collectives, per_device(): traces = lax.all_to_all(traces, 'len', 0, 0, tiled=True)  16.8 us
    all_to_all x1, starting transfers between devices, per_device(): traces = lax.all_to_all(traces, ('wid', 'hgt'), 0, 0, tiled=True)  11.6 us
    all_to_all x1, waiting for transfers between devices, per_device(): traces = lax.all_to_all(traces, ('wid', 'hgt'), 0, 0, tiled=True)  9.2 us
    unnamed x19, local copies, waits for them, and re-layouts  5.7 us
    pallas_call x1, Pallas kernels, per_device(): pl.pallas_call(pack_kernel, grid=(parts,), out_shape=(field(HIGH, 3, WIDE...  5.27 us
  transfers between devices with their start and end apart: 9, of which 4 were waited for; matrix products, arithmetic and copies ran while one was open for 0% of the time, Pallas kernels for 3%

profile of v2, /device:TPU:1, one launch (start us, length us, event | category | flops | bytes accessed | tf_op | source)
XLA Modules:
  0.0 160.1 jit_solution(18037250888320668082)
XLA Ops:
  0.6 0.0 copy-start
  0.6 1.0 copy-done
  1.7 0.0 copy-start.1
  1.7 1.0 copy-done.1
  2.7 0.0 copy-start.2
  2.7 1.0 copy-done.2
  3.8 0.0 copy-start.7
  3.8 0.7 copy-done.7
  4.4 5.3 %pack.1 = (f32[16,3,64,128]{3,2,1,0:T(8,128)S(1)}, f32[16,32,128]{2,1,0:T(8,128)S(1)}, f32[16,32,128]{2,1,0:T(8,128)S(1)}) custom-call(f32[8]{0:T(128)S(1)} %copy-done.7, f32[16,64,128]{2,1,0:T(8,128)S(1)} %copy-done, f32[16,64,128]{2,1,0:T(8,128)S(1)} %copy-done.1, s32[16,64,128]{2,1,0:T(8,128)S(1)} %copy-done.2), custom_call_target="tpu_custom_call" | custom-call | tf_op jit(solution)/shard_map/pack/pallas_call | solution.py:394
  9.7 8.8 %collective-permute-start = (f32[16,32,128]{2,1,0:T(8,128)S(1)}, f32[16,32,128]{2,1,0:T(8,128)S(1)}, u32[]{:S(2)}, u32[]{:S(2)}) collective-permute-start(f32[16,32,128]{2,1,0:T(8,128)S(1)} %get-tuple-element.13), channel_id=1, source_target_pairs={{32,0},{64,32},{96,64},{128,96},{160,128},{192,160},{224,192},{256... | collective-permute-start | bytes 786440 | tf_op jit(solution)/shard_map/ppermute | solution.py:382
  18.5 1.9 %collective-permute-start.1 = (f32[16,32,128]{2,1,0:T(8,128)S(1)}, f32[16,32,128]{2,1,0:T(8,128)S(1)}, u32[]{:S(2)}, u32[]{:S(2)}) collective-permute-start(f32[16,32,128]{2,1,0:T(8,128)S(1)} %get-tuple-element.14), channel_id=1, source_target_pairs={{0,32},{32,64},{64,96},{96,128},{128,160},{160,192},{192,224},{224... | collective-permute-start | bytes 786440 | tf_op jit(solution)/shard_map/ppermute | solution.py:382
  20.4 0.0 copy-start.8
  20.4 0.0 copy-start.5
  20.4 0.0 copy-start.6
  20.4 1.4 collective-permute-start.6
  21.9 5.2 %collective-permute-start.4 = (f32[16,3,64,128]{3,2,1,0:T(8,128)S(1)}, f32[16,3,64,128]{3,2,1,0:T(8,128)}, u32[]{:S(2)}, u32[]{:S(2)}) collective-permute-start(f32[16,3,64,128]{3,2,1,0:T(8,128)S(1)} %get-tuple-element.12.s_ref.refs_0_), channel_id=1, source_target_pairs={{0,1},{1,2},{2,3},{4,5},{5,6},{6,7},{8,9},{9,10},{10,11},{12,13},{... | collective-permute-start | bytes 4718600 | tf_op jit(solution)/shard_map/ppermute | solution.py:382
  27.0 0.0 collective-permute-done.from_right_ref
  27.0 0.0 collective-permute-done.1.from_left_ref
  27.0 1.2 edge.1
  28.2 1.3 collective-permute-start.2
  29.6 1.3 collective-permute-start.3
  30.9 9.1 %collective-permute-done.2.before_ref.refs_2_ = f32[16,4,16,128]{3,2,1,0:T(8,128)S(1)} collective-permute-done((f32[16,4,16,128]{3,2,1,0:T(8,128)S(1)}, f32[16,4,16,128]{3,2,1,0:T(8,128)S(1)}, u32[]{:S(2)}, u32[]{:S(2)}) %collective-permute-start.2) | collective-permute-done | bytes 524320 | tf_op jit(solution)/shard_map/ppermute | solution.py:382
  40.0 3.9 %collective-permute-done.3.after_ref.refs_3_ = f32[16,4,16,128]{3,2,1,0:T(8,128)S(1)} collective-permute-done((f32[16,4,16,128]{3,2,1,0:T(8,128)S(1)}, f32[16,4,16,128]{3,2,1,0:T(8,128)S(1)}, u32[]{:S(2)}, u32[]{:S(2)}) %collective-permute-start.3) | collective-permute-done | bytes 524320 | tf_op jit(solution)/shard_map/ppermute | solution.py:382
  43.9 2.2 %rim.1 = (f32[8,192,128]{2,1,0:T(8,128)}, f32[8,192,128]{2,1,0:T(8,128)}) custom-call(f32[16,64,128]{2,1,0:T(8,128)S(1)} %get-tuple-element.15.e_ref.refs_1_, f32[16,4,16,128]{3,2,1,0:T(8,128)S(1)} %collective-permute-done.2.before_ref.refs_2_, f32[16,4,16,128]{3,2,1,0:T(8,128)S(1)} %collective-permute-done.3.after_ref.refs_3_), custom_call_target="tpu_custom_call" | custom-call | tf_op jit(solution)/shard_map/rim/pallas_call | solution.py:368
  46.1 2.2 %collective-permute-start.5 = (f32[8,192,128]{2,1,0:T(8,128)}, f32[8,192,128]{2,1,0:T(8,128)}, u32[]{:S(2)}, u32[]{:S(2)}) collective-permute-start(f32[8,192,128]{2,1,0:T(8,128)} %get-tuple-element.18), channel_id=1, source_target_pairs={{0,1},{1,2},{2,3},{4,5},{5,6},{6,7},{8,9},{9,10},{10,11},{12,13},{... | collective-permute-start | bytes 2359304 | tf_op jit(solution)/shard_map/ppermute | solution.py:382
  48.3 1.3 collective-permute-start.7
  49.6 0.0 copy-done.8
  49.6 0.1 copy.9.sig_ref
  49.7 26.1 %collective-permute-done.5.refs_5_ = f32[8,192,128]{2,1,0:T(8,128)} collective-permute-done((f32[8,192,128]{2,1,0:T(8,128)}, f32[8,192,128]{2,1,0:T(8,128)}, u32[]{:S(2)}, u32[]{:S(2)}) %collective-permute-start.5) | collective-permute-done | bytes 786464 | tf_op jit(solution)/shard_map/ppermute | solution.py:382
  75.7 0.0 collective-permute-done.7.refs_7_
  75.7 0.0 collective-permute-done.6.refs_6_
  75.7 0.0 collective-permute-done.4.refs_4_
  75.8 0.0 copy-done.5
  75.8 0.0 copy-done.6
  75.8 41.4 %march.1 = (f32[16,64,128]{2,1,0:T(8,128)S(1)}, f32[16,16,128]{2,1,0:T(8,128)S(1)}) custom-call(s32[4,3]{1,0:T(4,128)S(1)} %copy-done.5, f32[16,4]{1,0:T(8,128)S(1)} %copy.9.sig_ref, s32[3,128]{1,0:T(4,128)S(1)} %bitcast.1, f32[16,3,64,128]{3,2,1,0:T(8,128)S(1)} %get-tuple-element.12.s_ref.refs_0_, f32[16,64,128]{2,1,0:T(8,128)S(1)} %get-tuple-element.15.e_ref.refs_1_, ...), custom_call_target="tpu_custom_call" | custom-call | tf_op jit(solution)/shard_map/march/pallas_call | solution.py:368
  117.2 0.0 copy-start.3
  117.2 0.8 copy-done.3
  118.0 16.8 %all_to_all.10.got_ref = f32[16,16,128]{2,1,0:T(8,128)S(1)} all-to-all(f32[16,16,128]{2,1,0:T(8,128)S(1)} %get-tuple-element.21), channel_id=1, replica_groups=mesh['len'=16,'wid'=8,'hgt'=4] {'len'}, dimensions={0} | all-to-all | bytes 262144 | tf_op jit(solution)/shard_map/all_to_all | solution.py:439
  134.8 0.7 relay.1
  135.5 11.6 %all-to-all-start.1 = ((f32[32,16,128]{2,1,0:T(8,128)}), f32[32,16,128]{2,1,0:T(8,128)S(1)}, u32[]{:S(2)}, u32[]{:S(2)}) async-start(f32[32,16,128]{2,1,0:T(8,128)} %relay.1), calls=%async_computation.1 | async-start | bytes 524288 | tf_op jit(solution)/shard_map/all_to_all | solution.py:441
  147.2 0.0 copy-start.4
  147.2 1.0 copy-done.4
  148.2 2.0 %order.1 = f32[16,64,128]{2,1,0:T(8,128)} custom-call(f32[16,64,128]{2,1,0:T(8,128)S(1)} %copy-done.4), custom_call_target="tpu_custom_call" | custom-call | tf_op jit(solution)/shard_map/order/pallas_call | solution.py:368
  150.3 9.2 %all-to-all-done.1 = f32[32,16,128]{2,1,0:T(8,128)S(1)} async-done(((f32[32,16,128]{2,1,0:T(8,128)}), f32[32,16,128]{2,1,0:T(8,128)S(1)}, u32[]{:S(2)}, u32[]{:S(2)}) %all-to-all-start.1) | async-done | bytes 262176 | tf_op jit(solution)/shard_map/all_to_all | solution.py:441
  159.5 0.6 reduce_sum.9
Async XLA Ops:
  0.6 1.0 copy-start
  1.7 1.0 copy-start.1
  2.7 1.0 copy-start.2
  3.8 0.7 copy-start.7
  9.7 17.4 %collective-permute-start = (f32[16,32,128]{2,1,0:T(8,128)S(1)}, f32[16,32,128]{2,1,0:T(8,128)S(1)}, u32[]{:S(2)}, u32[]{:S(2)}) collective-permute-start(f32[16,32,128]{2,1,0:T(8,128)S(1)} %get-tuple-element.13), channel_id=1, source_target_pairs={{32,0},{64,32},{96,64},{128,96},{160,128},{192,160},{224,192},{256... | collective-permute-start | bytes 786440 | tf_op jit(solution)/shard_map/ppermute | solution.py:382
  18.5 8.6 %collective-permute-start.1 = (f32[16,32,128]{2,1,0:T(8,128)S(1)}, f32[16,32,128]{2,1,0:T(8,128)S(1)}, u32[]{:S(2)}, u32[]{:S(2)}) collective-permute-start(f32[16,32,128]{2,1,0:T(8,128)S(1)} %get-tuple-element.14), channel_id=1, source_target_pairs={{0,32},{32,64},{64,96},{96,128},{128,160},{160,192},{192,224},{224... | collective-permute-start | bytes 786440 | tf_op jit(solution)/shard_map/ppermute | solution.py:382
  20.4 29.2 %copy-start.8 = (f32[16,4]{0,1:T(4,128)S(1)}, f32[16,4]{0,1:T(4,128)}, u32[]{:S(2)}) copy-start(f32[16,4]{0,1:T(4,128)} %param.12) | copy-start | bytes 772
  20.4 55.3 %copy-start.5 = (s32[4,3]{1,0:T(4,128)S(1)}, s32[4,3]{1,0:T(4,128)}, u32[]{:S(2)}) copy-start(s32[4,3]{1,0:T(4,128)} %src_ref.1) | copy-start | bytes 148
  20.4 55.3 %copy-start.6 = (s32[128,3]{0,1:T(4,128)S(1)}, s32[128,3]{0,1:T(4,128)}, u32[]{:S(2)}) copy-start(s32[128,3]{0,1:T(4,128)} %param.13) | copy-start | bytes 4612
  20.4 55.3 %collective-permute-start.6 = (f32[16,3,64,128]{3,2,1,0:T(8,128)S(1)}, f32[16,3,64,128]{3,2,1,0:T(8,128)}, u32[]{:S(2)}, u32[]{:S(2)}) collective-permute-start(f32[16,3,64,128]{3,2,1,0:T(8,128)S(1)} %get-tuple-element.12.s_ref.refs_0_), channel_id=1, source_target_pairs={{1,0},{2,1},{3,2},{5,4},{6,5},{7,6},{9,8},{10,9},{11,10},{13,12},{... | collective-permute-start | bytes 4718600 | tf_op jit(solution)/shard_map/ppermute | solution.py:382
  21.9 53.9 %collective-permute-start.4 = (f32[16,3,64,128]{3,2,1,0:T(8,128)S(1)}, f32[16,3,64,128]{3,2,1,0:T(8,128)}, u32[]{:S(2)}, u32[]{:S(2)}) collective-permute-start(f32[16,3,64,128]{3,2,1,0:T(8,128)S(1)} %get-tuple-element.12.s_ref.refs_0_), channel_id=1, source_target_pairs={{0,1},{1,2},{2,3},{4,5},{5,6},{6,7},{8,9},{9,10},{10,11},{12,13},{... | collective-permute-start | bytes 4718600 | tf_op jit(solution)/shard_map/ppermute | solution.py:382
  28.2 11.7 %collective-permute-start.2 = (f32[16,4,16,128]{3,2,1,0:T(8,128)S(1)}, f32[16,4,16,128]{3,2,1,0:T(8,128)S(1)}, u32[]{:S(2)}, u32[]{:S(2)}) collective-permute-start(f32[16,4,16,128]{3,2,1,0:T(8,128)S(1)} %get-tuple-element.16), channel_id=1, source_target_pairs={{0,4},{4,8},{8,12},{12,16},{16,20},{20,24},{24,28},{1,5},{5,9},{9,... | collective-permute-start | bytes 1572872 | tf_op jit(solution)/shard_map/ppermute | solution.py:382
  29.6 14.3 %collective-permute-start.3 = (f32[16,4,16,128]{3,2,1,0:T(8,128)S(1)}, f32[16,4,16,128]{3,2,1,0:T(8,128)S(1)}, u32[]{:S(2)}, u32[]{:S(2)}) collective-permute-start(f32[16,4,16,128]{3,2,1,0:T(8,128)S(1)} %get-tuple-element.17), channel_id=1, source_target_pairs={{4,0},{8,4},{12,8},{16,12},{20,16},{24,20},{28,24},{5,1},{9,5},{13... | collective-permute-start | bytes 1572872 | tf_op jit(solution)/shard_map/ppermute | solution.py:382
  46.1 29.6 %collective-permute-start.5 = (f32[8,192,128]{2,1,0:T(8,128)}, f32[8,192,128]{2,1,0:T(8,128)}, u32[]{:S(2)}, u32[]{:S(2)}) collective-permute-start(f32[8,192,128]{2,1,0:T(8,128)} %get-tuple-element.18), channel_id=1, source_target_pairs={{0,1},{1,2},{2,3},{4,5},{5,6},{6,7},{8,9},{9,10},{10,11},{12,13},{... | collective-permute-start | bytes 2359304 | tf_op jit(solution)/shard_map/ppermute | solution.py:382
  48.3 27.4 %collective-permute-start.7 = (f32[8,192,128]{2,1,0:T(8,128)}, f32[8,192,128]{2,1,0:T(8,128)}, u32[]{:S(2)}, u32[]{:S(2)}) collective-permute-start(f32[8,192,128]{2,1,0:T(8,128)} %get-tuple-element.19), channel_id=1, source_target_pairs={{1,0},{2,1},{3,2},{5,4},{6,5},{7,6},{9,8},{10,9},{11,10},{13,12},{... | collective-permute-start | bytes 2359304 | tf_op jit(solution)/shard_map/ppermute | solution.py:382
  117.2 0.8 copy-start.3
  135.5 23.9 %all-to-all-start.1 = ((f32[32,16,128]{2,1,0:T(8,128)}), f32[32,16,128]{2,1,0:T(8,128)S(1)}, u32[]{:S(2)}, u32[]{:S(2)}) async-start(f32[32,16,128]{2,1,0:T(8,128)} %relay.1), calls=%async_computation.1 | async-start | bytes 524288 | tf_op jit(solution)/shard_map/all_to_all | solution.py:441
  147.2 1.0 copy-start.4

commit v3 on v2

--- a/solution.py
+++ b/solution.py
@@ -38,7 +38,9 @@
     return (lane // 2) + 64 * (lane % 2)
 
 
-def pack_kernel(adm_ref, now_ref, old_ref, cls_ref, s_ref, left_ref, right_ref):
+def pack_kernel(
+    adm_ref, now_ref, old_ref, cls_ref, s_ref, left_ref, right_ref, head_ref, tail_ref
+):
     lane = lane_ids()
     order = even_odd()
 
@@ -55,6 +57,10 @@
             for a, field in enumerate((now_ref[h, rows, :], old_ref[h, rows, :], gain)):
                 split = regroup(field, order)
                 s_ref[h, a, rows, :] = split
+                if j < HALO // 8:
+                    head_ref[h, a, rows, :] = split
+                if j >= (WIDE - HALO) // 8:
+                    tail_ref[h, a, pl.ds(8 * j - WIDE + HALO, 8), :] = split
                 moved = pltpu.roll(split, 72, 1)
                 both = jnp.where((lane < 8) | ((lane >= 56) & (lane < 64)), split, moved)
                 if a == 0:
@@ -73,10 +79,10 @@
             right_ref[h, rows, :] = jnp.where((lane >= 56) & (lane < 104), rims[j], other)
         return carry
 
-    lax.fori_loop(0, now_ref.shape[0], layer, 0)
-
-
-def edge_kernel(from_right_ref, from_left_ref, s_ref, e_ref, head_ref, tail_ref):
+    lax.fori_loop(0, HIGH, layer, 0)
+
+
+def edge_kernel(from_right_ref, from_left_ref, e_ref, head_ref, tail_ref):
     lane = lane_ids()
     zero = jnp.float32(0.0)
     used = (lane < 48) | ((lane >= 56) & (lane < 104))
@@ -88,13 +94,14 @@
             a, b = from_right_ref[h, rows, :], from_left_ref[h, rows, :]
             first = jnp.where(lane < 48, a, b)
             second = pltpu.roll(jnp.where((lane >= 64) & (lane < 112), a, b), 64, 1)
-            e_ref[h, rows, :] = jnp.where(used, first, zero)
-            e_ref[h, pl.ds(8 * (j + half), 8), :] = jnp.where(used, second, zero)
-        for a in range(3):
-            head_ref[h, a] = s_ref[h, a, pl.ds(0, HALO), :]
-            tail_ref[h, a] = s_ref[h, a, pl.ds(WIDE - HALO, HALO), :]
-        head_ref[h, 3] = e_ref[h, pl.ds(0, HALO), :]
-        tail_ref[h, 3] = e_ref[h, pl.ds(WIDE - HALO, HALO), :]
+            first = jnp.where(used, first, zero)
+            second = jnp.where(used, second, zero)
+            e_ref[h, rows, :] = first
+            e_ref[h, pl.ds(8 * (j + half), 8), :] = second
+            if j < HALO // 8:
+                head_ref[h, rows, :] = first
+            if j >= half - HALO // 8:
+                tail_ref[h, pl.ds(8 * (j - half) + HALO, 8), :] = second
         return carry
 
     lax.fori_loop(0, HIGH, layer, 0)
@@ -108,7 +115,7 @@
     return right, n, (right & (k < n)) | (~right & (k >= 8 - n))
 
 
-def rim_kernel(e_ref, before_ref, after_ref, low_ref, top_ref):
+def rim_kernel(e_ref, before_ref, after_ref, before_e, after_e, low_ref, top_ref):
     row = lax.broadcasted_iota(jnp.int32, (HALO, LANES), 0)
 
     def pair(out_ref, i, near, far):
@@ -121,13 +128,13 @@
         right, n, mask = beside_lanes(i)
         for j in range(COLS):
             if j < HALO // 8:
-                a, b = before_ref[near, 3, pl.ds(8 * j, 8), :], before_ref[far, 3, pl.ds(8 * j, 8), :]
+                a, b = before_e[near, pl.ds(8 * j, 8), :], before_e[far, pl.ds(8 * j, 8), :]
             elif j < COLS - HALO // 8:
                 at = 8 * j - HALO
                 a, b = e_ref[near, pl.ds(at, 8), :], e_ref[far, pl.ds(at, 8), :]
             else:
                 at = 8 * j - HALO - WIDE
-                a, b = after_ref[near, 3, pl.ds(at, 8), :], after_ref[far, 3, pl.ds(at, 8), :]
+                a, b = after_e[near, pl.ds(at, 8), :], after_e[far, pl.ds(at, 8), :]
             moved = jnp.where(right, pltpu.roll(b, n, 1), pltpu.roll(b, LANES - n, 1))
             out_ref[i, pl.ds(6 * HALO + 8 * j, 8), :] = jnp.where(mask, a, moved)
 
@@ -154,15 +161,16 @@
                 ref[parity, at, j] = jnp.where(lane < 64, mid, near)
 
 
-def fill_own(refs, temp, s_ref, e_ref, before_ref, after_ref):
+def fill_own(refs, temp, s_ref, e_ref, before_ref, after_ref, before_e, after_e):
     def layer(h, carry):
         for a in range(3):
             temp[a, pl.ds(HALO, WIDE), :] = s_ref[h, a]
-        temp[3, pl.ds(HALO, WIDE), :] = e_ref[h]
-        for a in range(4):
             temp[a, pl.ds(0, HALO), :] = before_ref[h, a]
             temp[a, pl.ds(HALO + WIDE, HALO), :] = after_ref[h, a]
-        fill(refs, temp, HALO + h)
+        temp[3, pl.ds(0, HALO), :] = before_e[h]
+        temp[3, pl.ds(HALO, WIDE), :] = e_ref[h]
+        temp[3, pl.ds(HALO + WIDE, HALO), :] = after_e[h]
+        fill(refs, temp, h)
         return carry
 
     lax.fori_loop(0, HIGH, layer, 0)
@@ -225,7 +233,7 @@
 
         return count + mine.astype(jnp.int32)
 
-    return lax.fori_loop(0, rec_ref.shape[1], note, jnp.int32(0))
+    todo[6, 0] = lax.fori_loop(0, rec_ref.shape[1], note, jnp.int32(0))
 
 
 def list_sources(src_ref):
@@ -246,10 +254,10 @@
     return points
 
 
-def sweep(now, old, p_ref, low, high):
-    def chunk(first, layers):
+def sweep(now, old, p_ref, first, trips, layers):
+    def chunk(i, carry):
         for u in range(layers):
-            h = first + u
+            h = first(i) + u
             for parity in range(2):
                 other = [now[1 - parity, h, j] for j in range(COLS)]
                 mine = [now[parity, h, j] for j in range(COLS)]
@@ -261,68 +269,109 @@
                     total = total + beside
                     past = old[parity, h, j]
                     old[parity, h, j] = past + p_ref[parity, h, j] * (total - 6.0 * past)
-
-    fours = (high - low) // 4
-
-    def four(i, carry):
-        chunk(low + 4 * i, 4)
-        return carry
-
-    def two(i, carry):
-        chunk(low + 4 * fours + 2 * i, 2)
-        return carry
-
-    lax.fori_loop(0, fours, four, 0)
-    lax.fori_loop(0, (high - low - 4 * fours) // 2, two, 0)
-
-
-def march_kernel(src_ref, sig_ref, rec_ref, *refs):
-    s_ref, e_ref, before_ref, after_ref = refs[:4]
-    under, under_rim, over, over_rim = refs[4:8]
-    out_ref, trace_ref = refs[8:10]
-    a_ref, b_ref, p_ref, temp, hist, todo = refs[10:]
-    zero = jnp.float32(0.0)
-    fields = (a_ref, b_ref, p_ref)
-
-    fill_own(fields, temp, s_ref, e_ref, before_ref, after_ref)
-    fill_beside(fields, temp, under, under_rim, lambda i: (HALO - 1 - i, i))
-    fill_beside(fields, temp, over, over_rim, lambda i: (HALO + HIGH + i, TALL - 1 - i))
-
-    count = list_receivers(rec_ref, todo)
+        return carry
+
+    lax.fori_loop(0, trips, chunk, 0)
+
+
+def inject(field, points, sig_ref, t, base, inside):
+    for s, (near, parity, h, j, spot) in enumerate(points):
+
+        @pl.when(near & inside(h))
+        def _():
+            add = jnp.where(spot, sig_ref[s, t], jnp.float32(0.0))
+            field[parity, h - base, j] = field[parity, h - base, j] + add
+
+
+def keep(field, todo, hist, t, base):
+    def one(i, carry):
+        row = field[todo[4, i], todo[1, i] - base, todo[2, i], pl.ds(todo[3, i], 1), :]
+        hist[i, pl.ds(t, 1), :] = row
+        return carry
+
+    lax.fori_loop(0, todo[6, 0], one, 0)
+
+
+def gather(trace, todo, hist, early):
+    lane = lax.broadcasted_iota(jnp.int32, (STEPS, LANES), 1)
+    step = lax.broadcasted_iota(jnp.int32, (STEPS, LANES), 0)
+
+    def one(i, carry):
+        number, h = todo[0, i], todo[1, i]
+        moved = pltpu.roll(hist[i], (number - todo[5, i] + LANES) % LANES, 1)
+        done_early = (h > HALO + step) & (h < TALL - HALO - 1 - step)
+        now = done_early if early else ~done_early
+        trace[...] = jnp.where((lane == number) & now, moved, trace[...])
+        return carry
+
+    lax.fori_loop(0, todo[6, 0], one, 0)
+
+
+def inner_kernel(src_ref, sig_ref, rec_ref, *refs):
+    a_ref, b_ref, p_ref, trace_ref, todo, temp, hist = refs[6:]
+    list_receivers(rec_ref, todo)
+    fill_own((a_ref, b_ref, p_ref), temp, *refs[:6])
     points = list_sources(src_ref)
 
     def step(now, old, t):
-        sweep(now, old, p_ref, t + 1, TALL - t - 1)
-        for s, (near, parity, h, j, spot) in enumerate(points):
-
-            @pl.when(near)
-            def _():
-                old[parity, h, j] = old[parity, h, j] + jnp.where(spot, sig_ref[t, s], zero)
-
-        def keep(i, carry):
-            value = old[todo[4, i], todo[1, i], todo[2, i], pl.ds(todo[3, i], 1), :]
-            hist[i, pl.ds(t, 1), :] = value
-            return carry
-
-        lax.fori_loop(0, count, keep, 0)
+        sweep(now, old, p_ref, lambda i: t + 1 + 2 * i, HALF - 1 - t, 2)
+        inject(old, points, sig_ref, t, HALO, lambda h: (h > HALO + t) & (h < HALO + HIGH - 1 - t))
+        keep(old, todo, hist, t, HALO)
 
     def pair(i, carry):
         step(a_ref, b_ref, 2 * i)
         step(b_ref, a_ref, 2 * i + 1)
         return carry
 
+    lax.fori_loop(0, HALF // 2, pair, 0)
+    trace_ref[...] = jnp.zeros((STEPS, LANES), jnp.float32)
+    gather(trace_ref, todo, hist, True)
+
+
+def march_kernel(src_ref, sig_ref, todo, *refs):
+    own = refs[:3]
+    early_ref, under, under_rim, over, over_rim = refs[3:8]
+    out_ref, trace_ref = refs[8:10]
+    a_ref, b_ref, p_ref, temp, hist = refs[10:]
+    fields = (a_ref, b_ref, p_ref)
+
+    def take(h, carry):
+        for ref, got in zip(fields, own):
+            for parity in range(2):
+                ref[parity, HALO + h] = got[parity, h]
+        return carry
+
+    lax.fori_loop(0, HIGH, take, 0)
+    fill_beside(fields, temp, under, under_rim, lambda i: (HALO - 1 - i, i))
+    fill_beside(fields, temp, over, over_rim, lambda i: (HALO + HIGH + i, TALL - 1 - i))
+    points = list_sources(src_ref)
+
+    def step(now, old, t):
+        early = t < HALF - 1
+        full = TALL - 2 * (t + 1)
+        fours = jnp.where(early, HIGH // 2, full // 4)
+        gap = jnp.where(early, HIGH - 2 * (t + 1), 0)
+        sweep(
+            now,
+            old,
+            p_ref,
+            lambda i: t + 1 + 4 * i + jnp.where(i >= HIGH // 4, gap, 0),
+            fours,
+            4,
+        )
+        sweep(now, old, p_ref, lambda i: t + 1 + 4 * fours, jnp.where(early, 0, (full % 4) // 2), 2)
+        inject(old, points, sig_ref, t, 0, lambda h: (h <= HALO + t) | (h >= HALO + HIGH - 1 - t))
+        keep(old, todo, hist, t, 0)
+
+    def pair(i, carry):
+        step(a_ref, b_ref, 2 * i)
+        step(b_ref, a_ref, 2 * i + 1)
+        return carry
+
     lax.fori_loop(0, STEPS // 2, pair, 0)
 
-    trace_ref[0] = jnp.zeros((STEPS, LANES), jnp.float32)
-    wide_lane = lax.broadcasted_iota(jnp.int32, (STEPS, LANES), 1)
-
-    def gather(i, carry):
-        number = todo[0, i]
-        moved = pltpu.roll(hist[i], (number - todo[5, i] + LANES) % LANES, 1)
-        trace_ref[0] = jnp.where(wide_lane == number, moved, trace_ref[0])
-        return carry
-
-    lax.fori_loop(0, count, gather, 0)
+    trace_ref[0] = early_ref[...]
+    gather(trace_ref.at[0], todo, hist, False)
     for i in range(1, trace_ref.shape[0]):
         trace_ref[i] = trace_ref[0]
 
@@ -364,12 +413,17 @@
     return jax.ShapeDtypeStruct(shape, jnp.float32)
 
 
-def call(kernel, name, outs, ins, scratch=(), scalars=0, limit=8):
+def call(kernel, name, outs, ins, scratch=(), scalars=0, limit=8, listed=False):
+    out_shape = [field(*shape) for shape in outs]
+    out_specs = [VMEM for _ in outs]
+    if listed:
+        out_shape.append(jax.ShapeDtypeStruct((8, LANES), jnp.int32))
+        out_specs.append(SMEM)
     return pl.pallas_call(
         kernel,
-        out_shape=tuple(field(*shape) for shape in outs),
+        out_shape=tuple(out_shape),
         in_specs=[SMEM] * scalars + [VMEM] * (len(ins) - scalars),
-        out_specs=tuple(VMEM for _ in outs),
+        out_specs=tuple(out_specs),
         scratch_shapes=list(scratch),
         name=name,
         compiler_params=pltpu.CompilerParams(vmem_limit_bytes=limit << 20),
@@ -385,37 +439,41 @@
 def per_device(
     pressure_now, pressure_old, classes, admittance, source_cells, source_signal, receiver_cells
 ):
-    parts = 4
-    layers = HIGH // parts
-
-    def block(*shape):
-        return pl.BlockSpec((layers,) + shape, lambda i: (i,) + (0,) * len(shape))
-
-    s, to_left, to_right = pl.pallas_call(
-        pack_kernel,
-        grid=(parts,),
-        out_shape=(
-            field(HIGH, 3, WIDE, LANES),
-            field(HIGH, WIDE // 2, LANES),
-            field(HIGH, WIDE // 2, LANES),
-        ),
-        in_specs=[SMEM] + [block(WIDE, LANES)] * 3,
-        out_specs=(block(3, WIDE, LANES), block(WIDE // 2, LANES), block(WIDE // 2, LANES)),
-        name="pack",
-        compiler_params=pltpu.CompilerParams(vmem_limit_bytes=8 << 20),
-    )(admittance, pressure_now, pressure_old, classes)
+    strip = (HIGH, WIDE // 2, LANES)
+    face = (HIGH, 3, HALO, LANES)
+    outs = [(HIGH, 3, WIDE, LANES), strip, strip, face, face]
+    s, to_left, to_right, head, tail = call(
+        pack_kernel, "pack", outs, [admittance, pressure_now, pressure_old, classes], scalars=1
+    )
     from_right = shift(to_left, "len", -1)
     from_left = shift(to_right, "len", 1)
+    before, after = shift(tail, "wid", 1), shift(head, "wid", -1)
     over, under = shift(s, "hgt", -1), shift(s, "hgt", 1)
-    face = (HIGH, 4, HALO, LANES)
     edge, head, tail = call(
-        edge_kernel, "edge", [(HIGH, WIDE, LANES), face, face], [from_right, from_left, s]
+        edge_kernel,
+        "edge",
+        [(HIGH, WIDE, LANES), (HIGH, HALO, LANES), (HIGH, HALO, LANES)],
+        [from_right, from_left],
     )
-    before = shift(tail, "wid", 1)
-    after = shift(head, "wid", -1)
+    head, tail, before, after = lax.optimization_barrier((head, tail, before, after))
+    before_e, after_e = shift(tail, "wid", 1), shift(head, "wid", -1)
     rim = (HALF, RIM, LANES)
-    low, top = call(rim_kernel, "rim", [rim, rim], [edge, before, after])
+    low, top = call(rim_kernel, "rim", [rim, rim], [edge, before, after, before_e, after_e])
     over_rim, under_rim = shift(low, "hgt", -1), shift(top, "hgt", 1)
+    own = (2, HIGH, COLS, 8, LANES)
+    temp = pltpu.VMEM((4, BROAD, LANES), jnp.float32)
+    hist = pltpu.VMEM((LANES, STEPS, LANES), jnp.float32)
+    now, old, gain, early, todo = call(
+        inner_kernel,
+        "inner",
+        [own, own, own, (STEPS, LANES)],
+        [source_cells, source_signal.T, receiver_cells.T]
+        + [s, edge, before, after, before_e, after_e],
+        scratch=[temp, hist],
+        scalars=3,
+        limit=8,
+        listed=True,
+    )
     state = pltpu.VMEM((2, TALL, COLS, 8, LANES), jnp.float32)
     depth = lax.axis_size("len")
     sides = lax.axis_size("wid") * lax.axis_size("hgt")
@@ -423,27 +481,17 @@
         march_kernel,
         "march",
         [(HIGH, WIDE, LANES), (depth, STEPS, LANES)],
-        [source_cells, source_signal, receiver_cells.T, s, edge, before, after]
+        [source_cells, source_signal.T, todo, now, old, gain, early]
         + [under, under_rim, over, over_rim],
-        scratch=[
-            state,
-            state,
-            state,
-            pltpu.VMEM((4, BROAD, LANES), jnp.float32),
-            pltpu.VMEM((LANES, STEPS, LANES), jnp.float32),
-            pltpu.SMEM((8, LANES), jnp.int32),
-        ],
+        scratch=[state, state, state, temp, hist],
         scalars=3,
-        limit=LIMIT,
+        limit=20,
     )
     traces = lax.all_to_all(traces, "len", 0, 0, tiled=True)
     (traces,) = call(relay_kernel, "relay", [(sides, STEPS, LANES)], [traces])
     traces = lax.all_to_all(traces, ("wid", "hgt"), 0, 0, tiled=True)
     (now,) = call(order_kernel, "order", [(HIGH, WIDE, DEEP)], [split])
     return now, jnp.sum(traces, axis=0)
-
-
-LIMIT = 32
 
 
 def solution(mesh):

time: 161 us -> 144 us (0.89)
  waiting for transfers between devices: 48.3 us -> 30.7 us
  blocking collectives: 16.8 us -> 20.5 us
  local copies, waits for them, and re-layouts: 5.7 us -> 3.78 us
  starting transfers between devices: 35 us -> 33.2 us
    ppermute x8 -> x10, waiting for transfers between devices: 39.1 us -> 20.4 us  [shift(): return lax.ppermute(x, axis, pairs)]
    all_to_all x1, blocking collectives: 16.8 us -> 20.5 us  [per_device(): traces = lax.all_to_all(traces, 'len', 0, 0, tiled=True)]
    all_to_all x1, starting transfers between devices: 11.6 us -> 8.02 us  [per_device(): traces = lax.all_to_all(traces, ('wid', 'hgt'), 0, 0, tiled=True)]
    unnamed x19 -> x14, local copies, waits for them, and re-layouts: 5.7 us -> 3.78 us
    ppermute x8 -> x10, starting transfers between devices: 23.4 us -> 25.2 us  [shift(): return lax.ppermute(x, axis, pairs)]
    pallas_call x6 -> x7, Pallas kernels: 52.8 us -> 53.7 us  [call(): pl.pallas_call(kernel, out_shape=tuple(out_shape), in_specs=[SMEM] * scal...]
  transfers between devices with their start and end apart: 9 -> 11, of which waited for: 4 -> 8; matrix products, arithmetic and copies ran while one was open for 0% -> 0% of each run, Pallas kernels for 3% -> 11%
where the time goes in v3:
time: 144 us; the launch traced here: 143 us
  Pallas kernels  53.7 us (37%)
  starting transfers between devices  33.2 us (23%)
  waiting for transfers between devices  30.7 us (21%)
  blocking collectives  20.5 us (14%)
  local copies, waits for them, and re-layouts  3.78 us (3%)
    pallas_call x7, Pallas kernels, call(): pl.pallas_call(kernel, out_shape=tuple(out_shape), in_specs=[SMEM] * scal...  53.7 us
    ppermute x10, starting transfers between devices, shift(): return lax.ppermute(x, axis, pairs)  25.2 us
    all_to_all x1, blocking collectives, per_device(): traces = lax.all_to_all(traces, 'len', 0, 0, tiled=True)  20.5 us
    ppermute x10, waiting for transfers between devices, shift(): return lax.ppermute(x, axis, pairs)  20.4 us
    all_to_all x1, waiting for transfers between devices, per_device(): traces = lax.all_to_all(traces, ('wid', 'hgt'), 0, 0, tiled=True)  10.2 us
    all_to_all x1, starting transfers between devices, per_device(): traces = lax.all_to_all(traces, ('wid', 'hgt'), 0, 0, tiled=True)  8.02 us
    unnamed x14, local copies, waits for them, and re-layouts  3.78 us
  transfers between devices with their start and end apart: 11, of which 8 were waited for; matrix products, arithmetic and copies ran while one was open for 0% of the time, Pallas kernels for 11%

profile of v3, /device:TPU:1, one launch (start us, length us, event | category | flops | bytes accessed | tf_op | source)
XLA Modules:
  0.0 143.3 jit_solution(16946645219949118738)
XLA Ops:
  0.6 0.0 copy-start
  0.6 1.0 copy-done
  1.7 0.0 copy-start.1
  1.7 1.0 copy-done.1
  2.7 0.0 copy-start.2
  2.7 1.0 copy-done.2
  3.8 0.0 copy-start.6
  3.8 0.7 copy-done.6
  4.4 0.0 copy-start.3
  4.4 0.0 copy-start.4
  4.4 0.0 copy-start.5
  4.4 5.2 %pack.1 = (f32[16,3,64,128]{3,2,1,0:T(8,128)S(1)}, f32[16,32,128]{2,1,0:T(8,128)S(1)}, f32[16,32,128]{2,1,0:T(8,128)S(1)}, f32[16,3,16,128]{3,2,1,0:T(8,128)S(1)}, f32[16,3,16,128]{3,2,1,0:T(8,128)S(1)}) custom-call(f32[8]{0:T(128)S(1)} %copy-done.6, f32[16,64,128]{2,1,0:T(8,128)S(1)} %copy-done, f32[16,64,128]{2,1,0:T(8,128)S(1)} %copy-done.1, ...), custom_call_target="tpu_custom_call" | custom-call | tf_op jit(solution)/shard_map/pack/pallas_call | solution.py:422
  9.7 4.0 %collective-permute-start.6 = (f32[16,3,64,128]{3,2,1,0:T(8,128)S(1)}, f32[16,3,64,128]{3,2,1,0:T(8,128)S(1)}, u32[]{:S(2)}, u32[]{:S(2)}) collective-permute-start(f32[16,3,64,128]{3,2,1,0:T(8,128)S(1)} %get-tuple-element.23.refs_0_), channel_id=1, source_target_pairs={{0,1},{1,2},{2,3},{4,5},{5,6},{6,7},{8,9},{9,10},{10,11},{12,13},{... | collective-permute-start | bytes 4718600 | tf_op jit(solution)/shard_map/ppermute | solution.py:436
  13.7 1.3 collective-permute-start.8
  15.0 6.1 %collective-permute-start = (f32[16,32,128]{2,1,0:T(8,128)S(1)}, f32[16,32,128]{2,1,0:T(8,128)S(1)}, u32[]{:S(2)}, u32[]{:S(2)}) collective-permute-start(f32[16,32,128]{2,1,0:T(8,128)S(1)} %get-tuple-element.24), channel_id=1, source_target_pairs={{32,0},{64,32},{96,64},{128,96},{160,128},{192,160},{224,192},{256... | collective-permute-start | bytes 786440 | tf_op jit(solution)/shard_map/ppermute | solution.py:436
  21.1 1.3 collective-permute-start.2
  22.5 1.3 collective-permute-start.3
  23.8 0.4 collective-permute-done.from_right_ref
  24.2 2.4 %collective-permute-start.1 = (f32[16,32,128]{2,1,0:T(8,128)S(1)}, f32[16,32,128]{2,1,0:T(8,128)S(1)}, u32[]{:S(2)}, u32[]{:S(2)}) collective-permute-start(f32[16,32,128]{2,1,0:T(8,128)S(1)} %get-tuple-element.25), channel_id=1, source_target_pairs={{0,32},{32,64},{64,96},{96,128},{128,160},{160,192},{192,224},{224... | collective-permute-start | bytes 786440 | tf_op jit(solution)/shard_map/ppermute | solution.py:436
  26.6 3.3 %collective-permute-done.1.from_left_ref = f32[16,32,128]{2,1,0:T(8,128)S(1)} collective-permute-done((f32[16,32,128]{2,1,0:T(8,128)S(1)}, f32[16,32,128]{2,1,0:T(8,128)S(1)}, u32[]{:S(2)}, u32[]{:S(2)}) %collective-permute-start.1) | collective-permute-done | bytes 262176 | tf_op jit(solution)/shard_map/ppermute | solution.py:436
  29.9 1.2 edge.1
  31.1 0.0 collective-permute-done.2.refs_2_.before_ref
  31.1 4.3 %collective-permute-done.3.refs_3_.after_ref = f32[16,3,16,128]{3,2,1,0:T(8,128)S(1)} collective-permute-done((f32[16,3,16,128]{3,2,1,0:T(8,128)S(1)}, f32[16,3,16,128]{3,2,1,0:T(8,128)S(1)}, u32[]{:S(2)}, u32[]{:S(2)}) %collective-permute-start.3) | collective-permute-done | bytes 393248 | tf_op jit(solution)/shard_map/ppermute | solution.py:436
  35.3 1.8 %collective-permute-start.4 = (f32[16,16,128]{2,1,0:T(8,128)S(1)}, f32[16,16,128]{2,1,0:T(8,128)S(1)}, u32[]{:S(2)}, u32[]{:S(2)}) collective-permute-start(f32[16,16,128]{2,1,0:T(8,128)S(1)} %get-tuple-element.33), channel_id=1, source_target_pairs={{0,4},{4,8},{8,12},{12,16},{16,20},{20,24},{24,28},{1,5},{5,9},{9,... | collective-permute-start | bytes 393224 | tf_op jit(solution)/shard_map/ppermute | solution.py:436
  37.2 1.3 collective-permute-start.5
  38.5 1.0 collective-permute-done.4.refs_4_.before_e
  39.5 5.3 %collective-permute-done.5.refs_5_.after_e = f32[16,16,128]{2,1,0:T(8,128)S(1)} collective-permute-done((f32[16,16,128]{2,1,0:T(8,128)S(1)}, f32[16,16,128]{2,1,0:T(8,128)S(1)}, u32[]{:S(2)}, u32[]{:S(2)}) %collective-permute-start.5) | collective-permute-done | bytes 131104 | tf_op jit(solution)/shard_map/ppermute | solution.py:436
  44.8 1.0 rim.1
  45.9 4.3 %collective-permute-start.7 = (f32[8,192,128]{2,1,0:T(8,128)S(1)}, f32[8,192,128]{2,1,0:T(8,128)S(1)}, u32[]{:S(2)}, u32[]{:S(2)}) collective-permute-start(f32[8,192,128]{2,1,0:T(8,128)S(1)} %get-tuple-element.40), channel_id=1, source_target_pairs={{0,1},{1,2},{2,3},{4,5},{5,6},{6,7},{8,9},{9,10},{10,11},{12,13},{... | collective-permute-start | bytes 2359304 | tf_op jit(solution)/shard_map/ppermute | solution.py:436
  50.2 1.3 collective-permute-start.9
  51.5 0.0 copy-done.3
  51.5 0.0 copy-done.4
  51.5 0.0 copy-done.5
  51.5 12.1 %inner.1 = (f32[2,16,12,8,128]{4,3,2,1,0:T(8,128)S(1)}, f32[2,16,12,8,128]{4,3,2,1,0:T(8,128)S(1)}, f32[2,16,12,8,128]{4,3,2,1,0:T(8,128)S(1)}, f32[16,128]{1,0:T(8,128)S(1)}, s32[8,128]{1,0:T(8,128)S(1)}) custom-call(s32[4,3]{1,0:T(4,128)S(1)} %copy-done.3, f32[4,16]{1,0:T(4,128)S(1)} %bitcast.2, s32[3,128]{1,0:T(4,128)S(1)} %bitcast.4, ...), custom_call_target="tpu_custom_call" | custom-call | tf_op jit(solution)/shard_map/inner/pallas_call | solution.py:422
  63.7 2.2 %collective-permute-done.7.refs_5_ = f32[8,192,128]{2,1,0:T(8,128)S(1)} collective-permute-done((f32[8,192,128]{2,1,0:T(8,128)S(1)}, f32[8,192,128]{2,1,0:T(8,128)S(1)}, u32[]{:S(2)}, u32[]{:S(2)}) %collective-permute-start.7) | collective-permute-done | bytes 786464 | tf_op jit(solution)/shard_map/ppermute | solution.py:436
  65.9 3.9 %collective-permute-done.9.refs_7_ = f32[8,192,128]{2,1,0:T(8,128)S(1)} collective-permute-done((f32[8,192,128]{2,1,0:T(8,128)S(1)}, f32[8,192,128]{2,1,0:T(8,128)S(1)}, u32[]{:S(2)}, u32[]{:S(2)}) %collective-permute-start.9) | collective-permute-done | bytes 786464 | tf_op jit(solution)/shard_map/ppermute | solution.py:436
  69.8 0.0 collective-permute-done.6.refs_4_
  69.8 0.0 collective-permute-done.8.refs_6_
  69.8 31.3 %march.1 = (f32[16,64,128]{2,1,0:T(8,128)S(1)}, f32[16,16,128]{2,1,0:T(8,128)S(1)}) custom-call(s32[4,3]{1,0:T(4,128)S(1)} %copy-done.3, f32[4,16]{1,0:T(4,128)S(1)} %bitcast.3, s32[8,128]{1,0:T(8,128)S(1)} %get-tuple-element.35.todo, f32[2,16,12,8,128]{4,3,2,1,0:T(8,128)S(1)} %get-tuple-element.36.refs_0_, ...), custom_call_target="tpu_custom_call" | custom-call | tf_op jit(solution)/shard_map/march/pallas_call | solution.py:422
  101.1 20.5 %all_to_all.10.got_ref = f32[16,16,128]{2,1,0:T(8,128)S(1)} all-to-all(f32[16,16,128]{2,1,0:T(8,128)S(1)} %get-tuple-element.43), channel_id=1, replica_groups=mesh['len'=16,'wid'=8,'hgt'=4] {'len'}, dimensions={0} | all-to-all | bytes 262144 | tf_op jit(solution)/shard_map/all_to_all | solution.py:490
  121.6 0.7 relay.1
  122.3 8.0 %all-to-all-start.1 = ((f32[32,16,128]{2,1,0:T(8,128)}), f32[32,16,128]{2,1,0:T(8,128)S(1)}, u32[]{:S(2)}, u32[]{:S(2)}) async-start(f32[32,16,128]{2,1,0:T(8,128)} %relay.1), calls=%async_computation.1 | async-start | bytes 524288 | tf_op jit(solution)/shard_map/all_to_all | solution.py:492
  130.3 2.0 %order.1 = f32[16,64,128]{2,1,0:T(8,128)} custom-call(f32[16,64,128]{2,1,0:T(8,128)S(1)} %get-tuple-element.42.split_ref), custom_call_target="tpu_custom_call" | custom-call | tf_op jit(solution)/shard_map/order/pallas_call | solution.py:422
  132.4 10.2 %all-to-all-done.1 = f32[32,16,128]{2,1,0:T(8,128)S(1)} async-done(((f32[32,16,128]{2,1,0:T(8,128)}), f32[32,16,128]{2,1,0:T(8,128)S(1)}, u32[]{:S(2)}, u32[]{:S(2)}) %all-to-all-start.1) | async-done | bytes 262176 | tf_op jit(solution)/shard_map/all_to_all | solution.py:492
  142.6 0.6 reduce_sum.9
Async XLA Ops:
  0.6 1.0 copy-start
  1.7 1.0 copy-start.1
  2.7 1.0 copy-start.2
  3.8 0.7 copy-start.6
  4.4 47.1 %copy-start.3 = (s32[4,3]{1,0:T(4,128)S(1)}, s32[4,3]{1,0:T(4,128)}, u32[]{:S(2)}) copy-start(s32[4,3]{1,0:T(4,128)} %src_ref.3) | copy-start | bytes 148
  4.4 47.1 %copy-start.4 = (f32[16,4]{0,1:T(4,128)S(1)}, f32[16,4]{0,1:T(4,128)}, u32[]{:S(2)}) copy-start(f32[16,4]{0,1:T(4,128)} %param.12) | copy-start | bytes 772
  4.4 47.1 %copy-start.5 = (s32[128,3]{0,1:T(4,128)S(1)}, s32[128,3]{0,1:T(4,128)}, u32[]{:S(2)}) copy-start(s32[128,3]{0,1:T(4,128)} %param.13) | copy-start | bytes 4612
  9.7 60.1 %collective-permute-start.6 = (f32[16,3,64,128]{3,2,1,0:T(8,128)S(1)}, f32[16,3,64,128]{3,2,1,0:T(8,128)S(1)}, u32[]{:S(2)}, u32[]{:S(2)}) collective-permute-start(f32[16,3,64,128]{3,2,1,0:T(8,128)S(1)} %get-tuple-element.23.refs_0_), channel_id=1, source_target_pairs={{0,1},{1,2},{2,3},{4,5},{5,6},{6,7},{8,9},{9,10},{10,11},{12,13},{... | collective-permute-start | bytes 4718600 | tf_op jit(solution)/shard_map/ppermute | solution.py:436
  13.7 56.1 %collective-permute-start.8 = (f32[16,3,64,128]{3,2,1,0:T(8,128)S(1)}, f32[16,3,64,128]{3,2,1,0:T(8,128)S(1)}, u32[]{:S(2)}, u32[]{:S(2)}) collective-permute-start(f32[16,3,64,128]{3,2,1,0:T(8,128)S(1)} %get-tuple-element.23.refs_0_), channel_id=1, source_target_pairs={{1,0},{2,1},{3,2},{5,4},{6,5},{7,6},{9,8},{10,9},{11,10},{13,12},{... | collective-permute-start | bytes 4718600 | tf_op jit(solution)/shard_map/ppermute | solution.py:436
  15.0 9.2 %collective-permute-start = (f32[16,32,128]{2,1,0:T(8,128)S(1)}, f32[16,32,128]{2,1,0:T(8,128)S(1)}, u32[]{:S(2)}, u32[]{:S(2)}) collective-permute-start(f32[16,32,128]{2,1,0:T(8,128)S(1)} %get-tuple-element.24), channel_id=1, source_target_pairs={{32,0},{64,32},{96,64},{128,96},{160,128},{192,160},{224,192},{256... | collective-permute-start | bytes 786440 | tf_op jit(solution)/shard_map/ppermute | solution.py:436
  21.1 9.9 %collective-permute-start.2 = (f32[16,3,16,128]{3,2,1,0:T(8,128)S(1)}, f32[16,3,16,128]{3,2,1,0:T(8,128)S(1)}, u32[]{:S(2)}, u32[]{:S(2)}) collective-permute-start(f32[16,3,16,128]{3,2,1,0:T(8,128)S(1)} %get-tuple-element.29), channel_id=1, source_target_pairs={{0,4},{4,8},{8,12},{12,16},{16,20},{20,24},{24,28},{1,5},{5,9},{9,... | collective-permute-start | bytes 1179656 | tf_op jit(solution)/shard_map/ppermute | solution.py:436
  22.5 12.9 %collective-permute-start.3 = (f32[16,3,16,128]{3,2,1,0:T(8,128)S(1)}, f32[16,3,16,128]{3,2,1,0:T(8,128)S(1)}, u32[]{:S(2)}, u32[]{:S(2)}) collective-permute-start(f32[16,3,16,128]{3,2,1,0:T(8,128)S(1)} %get-tuple-element.30), channel_id=1, source_target_pairs={{4,0},{8,4},{12,8},{16,12},{20,16},{24,20},{28,24},{5,1},{9,5},{13... | collective-permute-start | bytes 1179656 | tf_op jit(solution)/shard_map/ppermute | solution.py:436
  24.2 5.7 %collective-permute-start.1 = (f32[16,32,128]{2,1,0:T(8,128)S(1)}, f32[16,32,128]{2,1,0:T(8,128)S(1)}, u32[]{:S(2)}, u32[]{:S(2)}) collective-permute-start(f32[16,32,128]{2,1,0:T(8,128)S(1)} %get-tuple-element.25), channel_id=1, source_target_pairs={{0,32},{32,64},{64,96},{96,128},{128,160},{160,192},{192,224},{224... | collective-permute-start | bytes 786440 | tf_op jit(solution)/shard_map/ppermute | solution.py:436
  35.3 4.2 %collective-permute-start.4 = (f32[16,16,128]{2,1,0:T(8,128)S(1)}, f32[16,16,128]{2,1,0:T(8,128)S(1)}, u32[]{:S(2)}, u32[]{:S(2)}) collective-permute-start(f32[16,16,128]{2,1,0:T(8,128)S(1)} %get-tuple-element.33), channel_id=1, source_target_pairs={{0,4},{4,8},{8,12},{12,16},{16,20},{20,24},{24,28},{1,5},{5,9},{9,... | collective-permute-start | bytes 393224 | tf_op jit(solution)/shard_map/ppermute | solution.py:436
  37.2 7.6 %collective-permute-start.5 = (f32[16,16,128]{2,1,0:T(8,128)S(1)}, f32[16,16,128]{2,1,0:T(8,128)S(1)}, u32[]{:S(2)}, u32[]{:S(2)}) collective-permute-start(f32[16,16,128]{2,1,0:T(8,128)S(1)} %get-tuple-element.34), channel_id=1, source_target_pairs={{4,0},{8,4},{12,8},{16,12},{20,16},{24,20},{28,24},{5,1},{9,5},{13... | collective-permute-start | bytes 393224 | tf_op jit(solution)/shard_map/ppermute | solution.py:436
  45.9 20.0 %collective-permute-start.7 = (f32[8,192,128]{2,1,0:T(8,128)S(1)}, f32[8,192,128]{2,1,0:T(8,128)S(1)}, u32[]{:S(2)}, u32[]{:S(2)}) collective-permute-start(f32[8,192,128]{2,1,0:T(8,128)S(1)} %get-tuple-element.40), channel_id=1, source_target_pairs={{0,1},{1,2},{2,3},{4,5},{5,6},{6,7},{8,9},{9,10},{10,11},{12,13},{... | collective-permute-start | bytes 2359304 | tf_op jit(solution)/shard_map/ppermute | solution.py:436
  50.2 19.6 %collective-permute-start.9 = (f32[8,192,128]{2,1,0:T(8,128)S(1)}, f32[8,192,128]{2,1,0:T(8,128)S(1)}, u32[]{:S(2)}, u32[]{:S(2)}) collective-permute-start(f32[8,192,128]{2,1,0:T(8,128)S(1)} %get-tuple-element.41), channel_id=1, source_target_pairs={{1,0},{2,1},{3,2},{5,4},{6,5},{7,6},{9,8},{10,9},{11,10},{13,12},{... | collective-permute-start | bytes 2359304 | tf_op jit(solution)/shard_map/ppermute | solution.py:436
  122.3 20.3 %all-to-all-start.1 = ((f32[32,16,128]{2,1,0:T(8,128)}), f32[32,16,128]{2,1,0:T(8,128)S(1)}, u32[]{:S(2)}, u32[]{:S(2)}) async-start(f32[32,16,128]{2,1,0:T(8,128)} %relay.1), calls=%async_computation.1 | async-start | bytes 524288 | tf_op jit(solution)/shard_map/all_to_all | solution.py:492

commit v4 on v3

--- a/solution.py
+++ b/solution.py
@@ -15,7 +15,6 @@
 TALL = HIGH + 2 * HALO
 BROAD = WIDE + 2 * HALO
 COLS = BROAD // 8
-RIM = 3 * 2 * HALO + BROAD
 VMEM = pl.BlockSpec(memory_space=pltpu.VMEM)
 SMEM = pl.BlockSpec(memory_space=pltpu.SMEM)
 
@@ -38,14 +37,10 @@
     return (lane // 2) + 64 * (lane % 2)
 
 
-def pack_kernel(
-    adm_ref, now_ref, old_ref, cls_ref, s_ref, left_ref, right_ref, head_ref, tail_ref
-):
-    lane = lane_ids()
+def pack_kernel(adm_ref, now_ref, old_ref, cls_ref, s_ref, head_ref, tail_ref):
     order = even_odd()
 
     def layer(h, carry):
-        rims = []
         for j in range(WIDE // 8):
             rows = pl.ds(8 * j, 8)
             kinds = cls_ref[h, rows, :]
@@ -53,7 +48,6 @@
             for index in range(adm_ref.shape[0]):
                 loss = jnp.where(kinds == index + 1, adm_ref[index], loss)
             gain = jnp.float32(1.0 / 3.0) / (1.0 + loss)
-            rim = None
             for a, field in enumerate((now_ref[h, rows, :], old_ref[h, rows, :], gain)):
                 split = regroup(field, order)
                 s_ref[h, a, rows, :] = split
@@ -61,61 +55,82 @@
                     head_ref[h, a, rows, :] = split
                 if j >= (WIDE - HALO) // 8:
                     tail_ref[h, a, pl.ds(8 * j - WIDE + HALO, 8), :] = split
-                moved = pltpu.roll(split, 72, 1)
-                both = jnp.where((lane < 8) | ((lane >= 56) & (lane < 64)), split, moved)
-                if a == 0:
-                    rim = both
-                else:
-                    both = pltpu.roll(both, 16 * a, 1)
-                    here = (lane >= 16 * a) & (lane < 16 * a + 16)
-                    here = here | ((lane >= 56 + 16 * a) & (lane < 72 + 16 * a))
-                    rim = jnp.where(here, both, rim)
-            rims.append(rim)
-        half = WIDE // 16
+        return carry
+
+    lax.fori_loop(0, HIGH, layer, 0)
+
+
+def face_lanes(fields):
+    lane = lane_ids()
+    out = None
+    for a, split in enumerate(fields):
+        moved = pltpu.roll(split, 72, 1)
+        both = jnp.where((lane < 8) | ((lane >= 56) & (lane < 64)), split, moved)
+        if a == 0:
+            out = both
+        else:
+            both = pltpu.roll(both, 16 * a, 1)
+            here = (lane >= 16 * a) & (lane < 16 * a + 16)
+            here = here | ((lane >= 56 + 16 * a) & (lane < 72 + 16 * a))
+            out = jnp.where(here, both, out)
+    return out
+
+
+def own_strip_kernel(rec_ref, s_ref, strip_ref, todo):
+    list_receivers(rec_ref, todo)
+
+    def layer(h, carry):
+        for j in range(WIDE // 8):
+            rows = pl.ds(8 * j, 8)
+            strip_ref[h, rows, :] = face_lanes([s_ref[h, a, rows, :] for a in range(3)])
+        return carry
+
+    lax.fori_loop(0, HIGH, layer, 0, unroll=4)
+
+
+def strip_kernel(strip_ref, before_ref, after_ref, left_ref, right_ref):
+    lane = lane_ids()
+    k = lane % 8
+    inner = HALO // 2
+    rim = face_lanes
+
+    def layer(h, carry):
+        low, high = pl.ds(0, inner), pl.ds(inner, inner)
+        rims = [rim([before_ref[h, a, high, :] for a in range(3)])]
+        for j in range(WIDE // 8):
+            rims.append(strip_ref[h, pl.ds(8 * j, 8), :])
+        rims.append(rim([after_ref[h, a, low, :] for a in range(3)]))
+        one = rim([before_ref[h, a, low, :] for a in range(3)])
+        two = rim([after_ref[h, a, high, :] for a in range(3)])
+        heads = jnp.where(k < 4, one, pltpu.roll(two, 4, 1))
+        tails = jnp.where(k >= 4, one, pltpu.roll(two, LANES - 4, 1))
+        outer = jnp.where(lane < 48, heads, tails)
+        half = len(rims) // 2
         for j in range(half):
             rows = pl.ds(8 * j, 8)
             other = pltpu.roll(rims[j + half], 64, 1)
-            left_ref[h, rows, :] = jnp.where(lane < 56, rims[j], other)
-            right_ref[h, rows, :] = jnp.where((lane >= 56) & (lane < 104), rims[j], other)
-        return carry
-
-    lax.fori_loop(0, HIGH, layer, 0)
-
-
-def edge_kernel(from_right_ref, from_left_ref, e_ref, head_ref, tail_ref):
-    lane = lane_ids()
-    zero = jnp.float32(0.0)
-    used = (lane < 48) | ((lane >= 56) & (lane < 104))
-
-    def layer(h, carry):
-        half = WIDE // 16
-        for j in range(half):
-            rows = pl.ds(8 * j, 8)
-            a, b = from_right_ref[h, rows, :], from_left_ref[h, rows, :]
-            first = jnp.where(lane < 48, a, b)
-            second = pltpu.roll(jnp.where((lane >= 64) & (lane < 112), a, b), 64, 1)
-            first = jnp.where(used, first, zero)
-            second = jnp.where(used, second, zero)
-            e_ref[h, rows, :] = first
-            e_ref[h, pl.ds(8 * (j + half), 8), :] = second
-            if j < HALO // 8:
-                head_ref[h, rows, :] = first
-            if j >= half - HALO // 8:
-                tail_ref[h, pl.ds(8 * (j - half) + HALO, 8), :] = second
-        return carry
-
-    lax.fori_loop(0, HIGH, layer, 0)
+            left = jnp.where(lane < 56, rims[j], other)
+            right = jnp.where((lane >= 56) & (lane < 104), rims[j], other)
+            if j < 3:
+                spare = pltpu.roll(outer, 48 - 16 * j, 1)
+                left = jnp.where((lane >= 48) & (lane < 64), spare, left)
+                right = jnp.where((lane >= 104) & (lane < 120), spare, right)
+            left_ref[h, rows, :] = left
+            right_ref[h, rows, :] = right
+        return carry
+
+    lax.fori_loop(0, HIGH, layer, 0, unroll=4)
 
 
 def beside_lanes(i):
     lane = lane_ids()
     k = lane % 8
     n = (HALO - i) // 2
-    right = lane < 48
+    right = (lane >= 64) & (lane < 112)
     return right, n, (right & (k < n)) | (~right & (k >= 8 - n))
 
 
-def rim_kernel(e_ref, before_ref, after_ref, before_e, after_e, low_ref, top_ref):
+def wide_rim_kernel(before_ref, after_ref, low_ref, top_ref):
     row = lax.broadcasted_iota(jnp.int32, (HALO, LANES), 0)
 
     def pair(out_ref, i, near, far):
@@ -124,19 +139,8 @@
             kept = jnp.where(row > i, before_ref[near, a], pltpu.roll(before_ref[far, a], i, 0))
             out_ref[i, pl.ds(at, HALO), :] = kept
             moved = pltpu.roll(after_ref[far, a], (HALO - i) % HALO, 0)
-            out_ref[i, pl.ds(at + HALO, HALO), :] = jnp.where(row < HALO - i - 1, after_ref[near, a], moved)
-        right, n, mask = beside_lanes(i)
-        for j in range(COLS):
-            if j < HALO // 8:
-                a, b = before_e[near, pl.ds(8 * j, 8), :], before_e[far, pl.ds(8 * j, 8), :]
-            elif j < COLS - HALO // 8:
-                at = 8 * j - HALO
-                a, b = e_ref[near, pl.ds(at, 8), :], e_ref[far, pl.ds(at, 8), :]
-            else:
-                at = 8 * j - HALO - WIDE
-                a, b = after_e[near, pl.ds(at, 8), :], after_e[far, pl.ds(at, 8), :]
-            moved = jnp.where(right, pltpu.roll(b, n, 1), pltpu.roll(b, LANES - n, 1))
-            out_ref[i, pl.ds(6 * HALO + 8 * j, 8), :] = jnp.where(mask, a, moved)
+            kept = jnp.where(row < HALO - i - 1, after_ref[near, a], moved)
+            out_ref[i, pl.ds(at + HALO, HALO), :] = kept
 
     def both(i, carry):
         pair(low_ref, i, i, HIGH - 1 - i)
@@ -144,6 +148,57 @@
         return carry
 
     lax.fori_loop(0, HALF, both, 0)
+
+
+def long_rim_kernel(from_right_ref, from_left_ref, e_ref, low_ref, top_ref):
+    lane = lane_ids()
+    zero = jnp.float32(0.0)
+    unused = ((lane >= 40) & (lane < 64)) | ((lane >= 112) & (lane < 120))
+
+    rights = (lane >= 64) & (lane < 112)
+    k = lane % 8
+    nearest = (rights & (k < 4)) | (~rights & (k >= 4))
+
+    def unfold(h, carry):
+        half = (BROAD - HALO) // 16
+        outer = zero
+        for j in range(half):
+            a, b = from_right_ref[h, pl.ds(8 * j, 8), :], from_left_ref[h, pl.ds(8 * j, 8), :]
+            first = pltpu.roll(jnp.where(lane < 48, a, b), 64, 1)
+            second = jnp.where(rights, a, b)
+            at = HALO // 2 + 8 * j
+            e_ref[h, pl.ds(at, 8), :] = jnp.where(unused, zero, first)
+            e_ref[h, pl.ds(at + 8 * half, 8), :] = jnp.where(unused, zero, second)
+            if j < 3:
+                spare = pltpu.roll(jnp.where((lane >= 48) & (lane < 64), a, b), 16 + 16 * j, 1)
+                here = (lane >= 64 + 16 * j) & (lane < 80 + 16 * j)
+                start = (120 + 16 * j) % LANES
+                if j == 0:
+                    here = here | (lane >= start) | (lane < 8)
+                else:
+                    here = here | ((lane >= start) & (lane < start + 16))
+                outer = jnp.where(here, spare, outer)
+        one = jnp.where(nearest, outer, zero)
+        two = jnp.where(rights, pltpu.roll(outer, LANES - 4, 1), pltpu.roll(outer, 4, 1))
+        e_ref[h, pl.ds(0, 8), :] = jnp.where(unused, zero, one)
+        e_ref[h, pl.ds(BROAD - 8, 8), :] = jnp.where(unused | ~nearest, zero, two)
+        return carry
+
+    lax.fori_loop(0, HIGH, unfold, 0, unroll=4)
+
+    def pair(out_ref, i, near, far):
+        right, n, mask = beside_lanes(i)
+        for j in range(COLS):
+            a, b = e_ref[near, pl.ds(8 * j, 8), :], e_ref[far, pl.ds(8 * j, 8), :]
+            moved = jnp.where(right, pltpu.roll(b, n, 1), pltpu.roll(b, LANES - n, 1))
+            out_ref[i, pl.ds(8 * j, 8), :] = jnp.where(mask, a, moved)
+
+    def both(i, carry):
+        pair(low_ref, i, i, HIGH - 1 - i)
+        pair(top_ref, i, HIGH - 1 - i, i)
+        return carry
+
+    lax.fori_loop(0, HALF, both, 0, unroll=2)
 
 
 def fill(refs, temp, at):
@@ -155,35 +210,34 @@
         for a, ref in enumerate(refs):
             main = temp[a, pl.ds(j, 8, stride=COLS), :]
             for parity in range(2):
-                near = pltpu.roll(edge, 64 - 8 * (2 * a + parity), 1)
+                turn = 8 * (2 * a + parity)
+                near = pltpu.roll(edge, LANES - turn, 1) if turn else edge
                 near = jnp.where(fringe, near, zero)
                 mid = pltpu.roll(main, 64, 1) if parity else main
                 ref[parity, at, j] = jnp.where(lane < 64, mid, near)
 
 
-def fill_own(refs, temp, s_ref, e_ref, before_ref, after_ref, before_e, after_e):
+def fill_own(refs, temp, s_ref, e_ref, before_ref, after_ref):
     def layer(h, carry):
         for a in range(3):
             temp[a, pl.ds(HALO, WIDE), :] = s_ref[h, a]
             temp[a, pl.ds(0, HALO), :] = before_ref[h, a]
             temp[a, pl.ds(HALO + WIDE, HALO), :] = after_ref[h, a]
-        temp[3, pl.ds(0, HALO), :] = before_e[h]
-        temp[3, pl.ds(HALO, WIDE), :] = e_ref[h]
-        temp[3, pl.ds(HALO + WIDE, HALO), :] = after_e[h]
+        temp[3] = e_ref[h]
         fill(refs, temp, h)
         return carry
 
     lax.fori_loop(0, HIGH, layer, 0)
 
 
-def fill_beside(refs, temp, s_ref, rim_ref, layers):
+def fill_beside(refs, temp, s_ref, rim_ref, edge_ref, layers):
     def pair(i, carry):
         near, far = layers(i)
         for a in range(3):
             temp[a, pl.ds(0, HALO), :] = rim_ref[i, pl.ds(2 * HALO * a, HALO), :]
             temp[a, pl.ds(HALO, WIDE), :] = s_ref[near % HIGH, a]
             temp[a, pl.ds(HALO + WIDE, HALO), :] = rim_ref[i, pl.ds(2 * HALO * a + HALO, HALO), :]
-        temp[3] = rim_ref[i, pl.ds(6 * HALO, BROAD), :]
+        temp[3] = edge_ref[i]
         fill(refs, temp, near)
         for a in range(3):
             before = rim_ref[i, pl.ds(2 * HALO * a, HALO), :]
@@ -195,7 +249,7 @@
         k = lane_ids() % 8
         mask = (right & (k < 8 - n)) | (~right & (k >= n))
         for j in range(COLS):
-            both = rim_ref[i, pl.ds(6 * HALO + 8 * j, 8), :]
+            both = edge_ref[i, pl.ds(8 * j, 8), :]
             moved = jnp.where(right, pltpu.roll(both, LANES - n, 1), pltpu.roll(both, n, 1))
             temp[3, pl.ds(8 * j, 8), :] = jnp.where(mask, moved, jnp.float32(0.0))
         fill(refs, temp, far)
@@ -233,7 +287,7 @@
 
         return count + mine.astype(jnp.int32)
 
-    todo[6, 0] = lax.fori_loop(0, rec_ref.shape[1], note, jnp.int32(0))
+    todo[6, 0] = lax.fori_loop(0, rec_ref.shape[1], note, jnp.int32(0), unroll=8)
 
 
 def list_sources(src_ref):
@@ -258,17 +312,26 @@
     def chunk(i, carry):
         for u in range(layers):
             h = first(i) + u
-            for parity in range(2):
-                other = [now[1 - parity, h, j] for j in range(COLS)]
-                mine = [now[parity, h, j] for j in range(COLS)]
-                for j in range(COLS):
-                    before = mine[j - 1] if j > 0 else pltpu.roll(mine[COLS - 1], 1, 0)
-                    after = mine[j + 1] if j < COLS - 1 else pltpu.roll(mine[0], 7, 0)
-                    beside = other[j] + pltpu.roll(other[j], 127 if parity else 1, 1)
-                    total = (now[parity, h - 1, j] + now[parity, h + 1, j]) + (before + after)
-                    total = total + beside
-                    past = old[parity, h, j]
-                    old[parity, h, j] = past + p_ref[parity, h, j] * (total - 6.0 * past)
+            for part in range(2):
+                js = range(part * COLS // 2, (part + 1) * COLS // 2)
+                for parity in range(2):
+                    side = {j: now[1 - parity, h, j] for j in js}
+                    rolled = {j: pltpu.roll(side[j], 127 if parity else 1, 1) for j in js}
+                    near = range(max(js[0] - 1, 0), min(js[-1] + 2, COLS))
+                    mine = {j: now[parity, h, j] for j in near}
+                    if part == 0:
+                        mine[-1] = pltpu.roll(now[parity, h, COLS - 1], 1, 0)
+                    else:
+                        mine[COLS] = pltpu.roll(now[parity, h, 0], 7, 0)
+                    known = {}
+                    for j in js:
+                        past = old[parity, h, j]
+                        total = now[parity, h - 1, j] + now[parity, h + 1, j]
+                        total = total + (mine[j - 1] + mine[j + 1]) + side[j]
+                        known[j] = (past, total - 6.0 * past)
+                    for j in js:
+                        past, total = known[j]
+                        old[parity, h, j] = past + p_ref[parity, h, j] * (total + rolled[j])
         return carry
 
     lax.fori_loop(0, trips, chunk, 0)
@@ -307,10 +370,9 @@
     lax.fori_loop(0, todo[6, 0], one, 0)
 
 
-def inner_kernel(src_ref, sig_ref, rec_ref, *refs):
-    a_ref, b_ref, p_ref, trace_ref, todo, temp, hist = refs[6:]
-    list_receivers(rec_ref, todo)
-    fill_own((a_ref, b_ref, p_ref), temp, *refs[:6])
+def inner_kernel(src_ref, sig_ref, todo, *refs):
+    a_ref, b_ref, p_ref, trace_ref, temp, hist = refs[4:]
+    fill_own((a_ref, b_ref, p_ref), temp, *refs[:4])
     points = list_sources(src_ref)
 
     def step(now, old, t):
@@ -330,9 +392,9 @@
 
 def march_kernel(src_ref, sig_ref, todo, *refs):
     own = refs[:3]
-    early_ref, under, under_rim, over, over_rim = refs[3:8]
-    out_ref, trace_ref = refs[8:10]
-    a_ref, b_ref, p_ref, temp, hist = refs[10:]
+    early_ref, under, over = refs[3], refs[4:7], refs[7:10]
+    out_ref, trace_ref = refs[10:12]
+    a_ref, b_ref, p_ref, temp, hist = refs[12:]
     fields = (a_ref, b_ref, p_ref)
 
     def take(h, carry):
@@ -342,8 +404,8 @@
         return carry
 
     lax.fori_loop(0, HIGH, take, 0)
-    fill_beside(fields, temp, under, under_rim, lambda i: (HALO - 1 - i, i))
-    fill_beside(fields, temp, over, over_rim, lambda i: (HALO + HIGH + i, TALL - 1 - i))
+    fill_beside(fields, temp, *under, lambda i: (HALO - 1 - i, i))
+    fill_beside(fields, temp, *over, lambda i: (HALO + HIGH + i, TALL - 1 - i))
     points = list_sources(src_ref)
 
     def step(now, old, t):
@@ -386,7 +448,7 @@
         out_ref[h] = plain[pl.ds(HALO, WIDE), :]
         return carry
 
-    lax.fori_loop(0, HIGH, hand_on, 0)
+    lax.fori_loop(0, HIGH, hand_on, 0, unroll=4)
 
 
 def order_kernel(split_ref, out_ref):
@@ -439,40 +501,51 @@
 def per_device(
     pressure_now, pressure_old, classes, admittance, source_cells, source_signal, receiver_cells
 ):
-    strip = (HIGH, WIDE // 2, LANES)
     face = (HIGH, 3, HALO, LANES)
-    outs = [(HIGH, 3, WIDE, LANES), strip, strip, face, face]
-    s, to_left, to_right, head, tail = call(
-        pack_kernel, "pack", outs, [admittance, pressure_now, pressure_old, classes], scalars=1
-    )
+    s, head, tail = call(
+        pack_kernel,
+        "pack",
+        [(HIGH, 3, WIDE, LANES), face, face],
+        [admittance, pressure_now, pressure_old, classes],
+        scalars=1,
+    )
+    over, under = shift(s, "hgt", -1), shift(s, "hgt", 1)
+    before, after = shift(tail, "wid", 1), shift(head, "wid", -1)
+    strip = (HIGH, (BROAD - HALO) // 2, LANES)
+    mine, todo = call(
+        own_strip_kernel,
+        "own_strip",
+        [(HIGH, WIDE, LANES)],
+        [receiver_cells.T, s],
+        scalars=1,
+        listed=True,
+    )
+    before, after, mine = lax.optimization_barrier((before, after, mine))
+    to_left, to_right = call(strip_kernel, "strip", [strip, strip], [mine, before, after])
     from_right = shift(to_left, "len", -1)
     from_left = shift(to_right, "len", 1)
-    before, after = shift(tail, "wid", 1), shift(head, "wid", -1)
-    over, under = shift(s, "hgt", -1), shift(s, "hgt", 1)
-    edge, head, tail = call(
-        edge_kernel,
-        "edge",
-        [(HIGH, WIDE, LANES), (HIGH, HALO, LANES), (HIGH, HALO, LANES)],
+    wide_rim, long_rim = (HALF, 3 * 2 * HALO, LANES), (HALF, BROAD, LANES)
+    low, top = call(wide_rim_kernel, "wide_rim", [wide_rim, wide_rim], [before, after])
+    over_rim, under_rim = shift(low, "hgt", -1), shift(top, "hgt", 1)
+    edge, low, top = call(
+        long_rim_kernel,
+        "long_rim",
+        [(HIGH, BROAD, LANES), long_rim, long_rim],
         [from_right, from_left],
     )
-    head, tail, before, after = lax.optimization_barrier((head, tail, before, after))
-    before_e, after_e = shift(tail, "wid", 1), shift(head, "wid", -1)
-    rim = (HALF, RIM, LANES)
-    low, top = call(rim_kernel, "rim", [rim, rim], [edge, before, after, before_e, after_e])
-    over_rim, under_rim = shift(low, "hgt", -1), shift(top, "hgt", 1)
+    over_edge, under_edge = shift(low, "hgt", -1), shift(top, "hgt", 1)
     own = (2, HIGH, COLS, 8, LANES)
     temp = pltpu.VMEM((4, BROAD, LANES), jnp.float32)
     hist = pltpu.VMEM((LANES, STEPS, LANES), jnp.float32)
-    now, old, gain, early, todo = call(
+    now, old, gain, early = call(
         inner_kernel,
         "inner",
         [own, own, own, (STEPS, LANES)],
-        [source_cells, source_signal.T, receiver_cells.T]
-        + [s, edge, before, after, before_e, after_e],
+        [source_cells, source_signal.T, todo]
+        + [s, edge, before, after],
         scratch=[temp, hist],
         scalars=3,
         limit=8,
-        listed=True,
     )
     state = pltpu.VMEM((2, TALL, COLS, 8, LANES), jnp.float32)
     depth = lax.axis_size("len")
@@ -482,7 +555,7 @@
         "march",
         [(HIGH, WIDE, LANES), (depth, STEPS, LANES)],
         [source_cells, source_signal.T, todo, now, old, gain, early]
-        + [under, under_rim, over, over_rim],
+        + [under, under_rim, under_edge, over, over_rim, over_edge],
         scratch=[state, state, state, temp, hist],
         scalars=3,
         limit=20,

time: 144 us -> 138 us (0.958)
  waiting for transfers between devices: 30.7 us -> 18.2 us
  starting transfers between devices: 33.2 us -> 39.8 us
  Pallas kernels: 53.7 us -> 49.6 us
  blocking collectives: 20.5 us -> 24.2 us
    ppermute x10, waiting for transfers between devices: 20.4 us -> 7.96 us  [shift(): return lax.ppermute(x, axis, pairs)]
    ppermute x10, starting transfers between devices: 25.2 us -> 29.8 us  [shift(): return lax.ppermute(x, axis, pairs)]
    pallas_call x7 -> x9, Pallas kernels: 53.7 us -> 49.6 us  [call(): pl.pallas_call(kernel, out_shape=tuple(out_shape), in_specs=[SMEM] * scal...]
    all_to_all x1, blocking collectives: 20.5 us -> 24.2 us  [per_device(): traces = lax.all_to_all(traces, 'len', 0, 0, tiled=True)]
    all_to_all x1, starting transfers between devices: 8.02 us -> 10.1 us  [per_device(): traces = lax.all_to_all(traces, ('wid', 'hgt'), 0, 0, tiled=True)]
  transfers between devices with their start and end apart: 11 -> 11, of which waited for: 8 -> 4; matrix products, arithmetic and copies ran while one was open for 0% -> 0% of each run, Pallas kernels for 11% -> 14%
where the time goes in v4:
time: 138 us; the launch traced here: 137 us
  Pallas kernels  49.6 us (36%)
  starting transfers between devices  39.8 us (29%)
  blocking collectives  24.2 us (18%)
  waiting for transfers between devices  18.2 us (13%)
  local copies, waits for them, and re-layouts  3.79 us (3%)
    pallas_call x9, Pallas kernels, call(): pl.pallas_call(kernel, out_shape=tuple(out_shape), in_specs=[SMEM] * scal...  49.6 us
    ppermute x10, starting transfers between devices, shift(): return lax.ppermute(x, axis, pairs)  29.8 us
    all_to_all x1, blocking collectives, per_device(): traces = lax.all_to_all(traces, 'len', 0, 0, tiled=True)  24.2 us
    all_to_all x1, waiting for transfers between devices, per_device(): traces = lax.all_to_all(traces, ('wid', 'hgt'), 0, 0, tiled=True)  10.2 us
    all_to_all x1, starting transfers between devices, per_device(): traces = lax.all_to_all(traces, ('wid', 'hgt'), 0, 0, tiled=True)  10.1 us
    ppermute x10, waiting for transfers between devices, shift(): return lax.ppermute(x, axis, pairs)  7.96 us
    unnamed x14, local copies, waits for them, and re-layouts  3.79 us
  transfers between devices with their start and end apart: 11, of which 4 were waited for; matrix products, arithmetic and copies ran while one was open for 0% of the time, Pallas kernels for 14%

profile of v4, /device:TPU:1, one launch (start us, length us, event | category | flops | bytes accessed | tf_op | source)
XLA Modules:
  0.0 137.1 jit_solution(10968078322936180080)
XLA Ops:
  0.6 0.0 copy-start
  0.6 1.0 copy-done
  1.7 0.0 copy-start.1
  1.7 1.0 copy-done.1
  2.7 0.0 copy-start.2
  2.7 1.0 copy-done.2
  3.8 0.0 copy-start.6
  3.8 0.7 copy-done.6
  4.4 0.0 copy-start.5
  4.4 2.2 %pack.1 = (f32[16,3,64,128]{3,2,1,0:T(8,128)S(1)}, f32[16,3,16,128]{3,2,1,0:T(8,128)S(1)}, f32[16,3,16,128]{3,2,1,0:T(8,128)S(1)}) custom-call(f32[8]{0:T(128)S(1)} %copy-done.6, f32[16,64,128]{2,1,0:T(8,128)S(1)} %copy-done, f32[16,64,128]{2,1,0:T(8,128)S(1)} %copy-done.1, s32[16,64,128]{2,1,0:T(8,128)S(1)} %copy-done.2), custom_call_target="tpu_custom_call" | custom-call | tf_op jit(solution)/shard_map/pack/pallas_call | solution.py:484
  6.6 4.0 %collective-permute-start.4 = (f32[16,3,64,128]{3,2,1,0:T(8,128)S(1)}, f32[16,3,64,128]{3,2,1,0:T(8,128)S(1)}, u32[]{:S(2)}, u32[]{:S(2)}) collective-permute-start(f32[16,3,64,128]{3,2,1,0:T(8,128)S(1)} %get-tuple-element.23.s_ref.refs_0_), channel_id=1, source_target_pairs={{0,1},{1,2},{2,3},{4,5},{5,6},{6,7},{8,9},{9,10},{10,11},{12,13},{... | collective-permute-start | bytes 4718600 | tf_op jit(solution)/shard_map/ppermute | solution.py:498
  10.6 1.3 collective-permute-start.7
  11.9 3.2 %collective-permute-start = (f32[16,3,16,128]{3,2,1,0:T(8,128)S(1)}, f32[16,3,16,128]{3,2,1,0:T(8,128)S(1)}, u32[]{:S(2)}, u32[]{:S(2)}) collective-permute-start(f32[16,3,16,128]{3,2,1,0:T(8,128)S(1)} %get-tuple-element.25), channel_id=1, source_target_pairs={{0,4},{4,8},{8,12},{12,16},{16,20},{20,24},{24,28},{1,5},{5,9},{9,... | collective-permute-start | bytes 1179656 | tf_op jit(solution)/shard_map/ppermute | solution.py:498
  15.2 1.3 collective-permute-start.1
  16.5 0.0 copy-done.5
  16.5 6.5 %own_strip.1 = (f32[16,64,128]{2,1,0:T(8,128)S(1)}, s32[8,128]{1,0:T(8,128)S(1)}) custom-call(s32[3,128]{1,0:T(4,128)S(1)} %bitcast.4, f32[16,3,64,128]{3,2,1,0:T(8,128)S(1)} %get-tuple-element.23.s_ref.refs_0_), custom_call_target="tpu_custom_call" | custom-call | tf_op jit(solution)/shard_map/own_strip/pallas_call | solution.py:484
  22.9 0.0 copy-start.3
  23.0 0.0 copy-start.4
  23.0 0.0 collective-permute-done.before_ref.refs_2_
  23.0 2.4 %collective-permute-done.1.after_ref.refs_3_ = f32[16,3,16,128]{3,2,1,0:T(8,128)S(1)} collective-permute-done((f32[16,3,16,128]{3,2,1,0:T(8,128)S(1)}, f32[16,3,16,128]{3,2,1,0:T(8,128)S(1)}, u32[]{:S(2)}, u32[]{:S(2)}) %collective-permute-start.1) | collective-permute-done | bytes 393248 | tf_op jit(solution)/shard_map/ppermute | solution.py:498
  25.3 0.2 wide_rim.1
  25.5 3.7 %collective-permute-start.5 = (f32[8,96,128]{2,1,0:T(8,128)S(1)}, f32[8,96,128]{2,1,0:T(8,128)S(1)}, u32[]{:S(2)}, u32[]{:S(2)}) collective-permute-start(f32[8,96,128]{2,1,0:T(8,128)S(1)} %get-tuple-element.38), channel_id=1, source_target_pairs={{0,1},{1,2},{2,3},{4,5},{5,6},{6,7},{8,9},{9,10},{10,11},{12,13},{... | collective-permute-start | bytes 1179656 | tf_op jit(solution)/shard_map/ppermute | solution.py:498
  29.3 1.2 strip.1
  30.5 5.7 %collective-permute-start.2 = (f32[16,40,128]{2,1,0:T(8,128)S(1)}, f32[16,40,128]{2,1,0:T(8,128)S(1)}, u32[]{:S(2)}, u32[]{:S(2)}) collective-permute-start(f32[16,40,128]{2,1,0:T(8,128)S(1)} %get-tuple-element.31), channel_id=1, source_target_pairs={{32,0},{64,32},{96,64},{128,96},{160,128},{192,160},{224,192},{256... | collective-permute-start | bytes 983048 | tf_op jit(solution)/shard_map/ppermute | solution.py:498
  36.2 3.9 %collective-permute-start.3 = (f32[16,40,128]{2,1,0:T(8,128)S(1)}, f32[16,40,128]{2,1,0:T(8,128)S(1)}, u32[]{:S(2)}, u32[]{:S(2)}) collective-permute-start(f32[16,40,128]{2,1,0:T(8,128)S(1)} %get-tuple-element.32), channel_id=1, source_target_pairs={{0,32},{32,64},{64,96},{96,128},{128,160},{160,192},{192,224},{224... | collective-permute-start | bytes 983048 | tf_op jit(solution)/shard_map/ppermute | solution.py:498
  40.1 3.1 %collective-permute-done.2.from_right_ref = f32[16,40,128]{2,1,0:T(8,128)S(1)} collective-permute-done((f32[16,40,128]{2,1,0:T(8,128)S(1)}, f32[16,40,128]{2,1,0:T(8,128)S(1)}, u32[]{:S(2)}, u32[]{:S(2)}) %collective-permute-start.2) | collective-permute-done | bytes 327712 | tf_op jit(solution)/shard_map/ppermute | solution.py:498
  43.2 1.3 collective-permute-start.8
  44.5 0.0 collective-permute-done.3.from_left_ref
  44.5 1.3 long_rim.1
  45.8 4.0 %collective-permute-start.6 = (f32[8,96,128]{2,1,0:T(8,128)S(1)}, f32[8,96,128]{2,1,0:T(8,128)S(1)}, u32[]{:S(2)}, u32[]{:S(2)}) collective-permute-start(f32[8,96,128]{2,1,0:T(8,128)S(1)} %get-tuple-element.39), channel_id=1, source_target_pairs={{0,1},{1,2},{2,3},{4,5},{5,6},{6,7},{8,9},{9,10},{10,11},{12,13},{... | collective-permute-start | bytes 1179656 | tf_op jit(solution)/shard_map/ppermute | solution.py:498
  49.9 0.0 collective-permute-done.5.refs_5_
  49.9 1.3 collective-permute-start.9
  51.2 0.0 copy-done.3
  51.2 0.0 copy-done.4
  51.2 7.6 %inner.1 = (f32[2,16,12,8,128]{4,3,2,1,0:T(8,128)S(1)}, f32[2,16,12,8,128]{4,3,2,1,0:T(8,128)S(1)}, f32[2,16,12,8,128]{4,3,2,1,0:T(8,128)S(1)}, f32[16,128]{1,0:T(8,128)S(1)}) custom-call(s32[4,3]{1,0:T(4,128)S(1)} %copy-done.3, f32[4,16]{1,0:T(4,128)S(1)} %bitcast.2, s32[8,128]{1,0:T(8,128)S(1)} %get-tuple-element.24.todo, ...), custom_call_target="tpu_custom_call" | custom-call | tf_op jit(solution)/shard_map/inner/pallas_call | solution.py:484
  58.8 0.0 collective-permute-done.8.refs_8_
  58.8 0.0 collective-permute-done.6.refs_6_
  58.8 2.5 %collective-permute-done.9.refs_9_ = f32[8,96,128]{2,1,0:T(8,128)S(1)} collective-permute-done((f32[8,96,128]{2,1,0:T(8,128)S(1)}, f32[8,96,128]{2,1,0:T(8,128)S(1)}, u32[]{:S(2)}, u32[]{:S(2)}) %collective-permute-start.9) | collective-permute-done | bytes 393248 | tf_op jit(solution)/shard_map/ppermute | solution.py:498
  61.3 0.0 collective-permute-done.4.refs_4_
  61.3 0.0 collective-permute-done.7.refs_7_
  61.3 27.9 %march.1 = (f32[16,64,128]{2,1,0:T(8,128)S(1)}, f32[16,16,128]{2,1,0:T(8,128)S(1)}) custom-call(s32[4,3]{1,0:T(4,128)S(1)} %copy-done.3, f32[4,16]{1,0:T(4,128)S(1)} %bitcast.3, s32[8,128]{1,0:T(8,128)S(1)} %get-tuple-element.24.todo, f32[2,16,12,8,128]{4,3,2,1,0:T(8,128)S(1)} %get-tuple-element.34.refs_0_, ...), custom_call_target="tpu_custom_call" | custom-call | tf_op jit(solution)/shard_map/march/pallas_call | solution.py:484
  89.2 24.2 %all_to_all.10.got_ref = f32[16,16,128]{2,1,0:T(8,128)S(1)} all-to-all(f32[16,16,128]{2,1,0:T(8,128)S(1)} %get-tuple-element.43), channel_id=1, replica_groups=mesh['len'=16,'wid'=8,'hgt'=4] {'len'}, dimensions={0} | all-to-all | bytes 262144 | tf_op jit(solution)/shard_map/all_to_all | solution.py:563
  113.4 0.7 relay.1
  114.1 10.1 %all-to-all-start.1 = ((f32[32,16,128]{2,1,0:T(8,128)}), f32[32,16,128]{2,1,0:T(8,128)S(1)}, u32[]{:S(2)}, u32[]{:S(2)}) async-start(f32[32,16,128]{2,1,0:T(8,128)} %relay.1), calls=%async_computation.1 | async-start | bytes 524288 | tf_op jit(solution)/shard_map/all_to_all | solution.py:565
  124.2 2.0 %order.1 = f32[16,64,128]{2,1,0:T(8,128)} custom-call(f32[16,64,128]{2,1,0:T(8,128)S(1)} %get-tuple-element.42.split_ref), custom_call_target="tpu_custom_call" | custom-call | tf_op jit(solution)/shard_map/order/pallas_call | solution.py:484
  126.3 10.2 %all-to-all-done.1 = f32[32,16,128]{2,1,0:T(8,128)S(1)} async-done(((f32[32,16,128]{2,1,0:T(8,128)}), f32[32,16,128]{2,1,0:T(8,128)S(1)}, u32[]{:S(2)}, u32[]{:S(2)}) %all-to-all-start.1) | async-done | bytes 262176 | tf_op jit(solution)/shard_map/all_to_all | solution.py:565
  136.5 0.6 reduce_sum.9
Async XLA Ops:
  0.6 1.0 copy-start
  1.7 1.0 copy-start.1
  2.7 1.0 copy-start.2
  3.8 0.7 copy-start.6
  4.4 12.0 %copy-start.5 = (s32[128,3]{0,1:T(4,128)S(1)}, s32[128,3]{0,1:T(4,128)}, u32[]{:S(2)}) copy-start(s32[128,3]{0,1:T(4,128)} %param.13) | copy-start | bytes 4612
  6.6 54.7 %collective-permute-start.4 = (f32[16,3,64,128]{3,2,1,0:T(8,128)S(1)}, f32[16,3,64,128]{3,2,1,0:T(8,128)S(1)}, u32[]{:S(2)}, u32[]{:S(2)}) collective-permute-start(f32[16,3,64,128]{3,2,1,0:T(8,128)S(1)} %get-tuple-element.23.s_ref.refs_0_), channel_id=1, source_target_pairs={{0,1},{1,2},{2,3},{4,5},{5,6},{6,7},{8,9},{9,10},{10,11},{12,13},{... | collective-permute-start | bytes 4718600 | tf_op jit(solution)/shard_map/ppermute | solution.py:498
  10.6 50.7 %collective-permute-start.7 = (f32[16,3,64,128]{3,2,1,0:T(8,128)S(1)}, f32[16,3,64,128]{3,2,1,0:T(8,128)S(1)}, u32[]{:S(2)}, u32[]{:S(2)}) collective-permute-start(f32[16,3,64,128]{3,2,1,0:T(8,128)S(1)} %get-tuple-element.23.s_ref.refs_0_), channel_id=1, source_target_pairs={{1,0},{2,1},{3,2},{5,4},{6,5},{7,6},{9,8},{10,9},{11,10},{13,12},{... | collective-permute-start | bytes 4718600 | tf_op jit(solution)/shard_map/ppermute | solution.py:498
  11.9 11.0 %collective-permute-start = (f32[16,3,16,128]{3,2,1,0:T(8,128)S(1)}, f32[16,3,16,128]{3,2,1,0:T(8,128)S(1)}, u32[]{:S(2)}, u32[]{:S(2)}) collective-permute-start(f32[16,3,16,128]{3,2,1,0:T(8,128)S(1)} %get-tuple-element.25), channel_id=1, source_target_pairs={{0,4},{4,8},{8,12},{12,16},{16,20},{20,24},{24,28},{1,5},{5,9},{9,... | collective-permute-start | bytes 1179656 | tf_op jit(solution)/shard_map/ppermute | solution.py:498
  15.2 10.2 %collective-permute-start.1 = (f32[16,3,16,128]{3,2,1,0:T(8,128)S(1)}, f32[16,3,16,128]{3,2,1,0:T(8,128)S(1)}, u32[]{:S(2)}, u32[]{:S(2)}) collective-permute-start(f32[16,3,16,128]{3,2,1,0:T(8,128)S(1)} %get-tuple-element.26), channel_id=1, source_target_pairs={{4,0},{8,4},{12,8},{16,12},{20,16},{24,20},{28,24},{5,1},{9,5},{13... | collective-permute-start | bytes 1179656 | tf_op jit(solution)/shard_map/ppermute | solution.py:498
  22.9 28.2 %copy-start.3 = (s32[4,3]{1,0:T(4,128)S(1)}, s32[4,3]{1,0:T(4,128)}, u32[]{:S(2)}) copy-start(s32[4,3]{1,0:T(4,128)} %src_ref.3) | copy-start | bytes 148
  23.0 28.2 %copy-start.4 = (f32[16,4]{0,1:T(4,128)S(1)}, f32[16,4]{0,1:T(4,128)}, u32[]{:S(2)}) copy-start(f32[16,4]{0,1:T(4,128)} %param.12) | copy-start | bytes 772
  25.5 24.4 %collective-permute-start.5 = (f32[8,96,128]{2,1,0:T(8,128)S(1)}, f32[8,96,128]{2,1,0:T(8,128)S(1)}, u32[]{:S(2)}, u32[]{:S(2)}) collective-permute-start(f32[8,96,128]{2,1,0:T(8,128)S(1)} %get-tuple-element.38), channel_id=1, source_target_pairs={{0,1},{1,2},{2,3},{4,5},{5,6},{6,7},{8,9},{9,10},{10,11},{12,13},{... | collective-permute-start | bytes 1179656 | tf_op jit(solution)/shard_map/ppermute | solution.py:498
  30.5 12.7 %collective-permute-start.2 = (f32[16,40,128]{2,1,0:T(8,128)S(1)}, f32[16,40,128]{2,1,0:T(8,128)S(1)}, u32[]{:S(2)}, u32[]{:S(2)}) collective-permute-start(f32[16,40,128]{2,1,0:T(8,128)S(1)} %get-tuple-element.31), channel_id=1, source_target_pairs={{32,0},{64,32},{96,64},{128,96},{160,128},{192,160},{224,192},{256... | collective-permute-start | bytes 983048 | tf_op jit(solution)/shard_map/ppermute | solution.py:498
  36.2 8.3 %collective-permute-start.3 = (f32[16,40,128]{2,1,0:T(8,128)S(1)}, f32[16,40,128]{2,1,0:T(8,128)S(1)}, u32[]{:S(2)}, u32[]{:S(2)}) collective-permute-start(f32[16,40,128]{2,1,0:T(8,128)S(1)} %get-tuple-element.32), channel_id=1, source_target_pairs={{0,32},{32,64},{64,96},{96,128},{128,160},{160,192},{192,224},{224... | collective-permute-start | bytes 983048 | tf_op jit(solution)/shard_map/ppermute | solution.py:498
  43.2 15.6 %collective-permute-start.8 = (f32[8,96,128]{2,1,0:T(8,128)S(1)}, f32[8,96,128]{2,1,0:T(8,128)S(1)}, u32[]{:S(2)}, u32[]{:S(2)}) collective-permute-start(f32[8,96,128]{2,1,0:T(8,128)S(1)} %get-tuple-element.40), channel_id=1, source_target_pairs={{1,0},{2,1},{3,2},{5,4},{6,5},{7,6},{9,8},{10,9},{11,10},{13,12},{... | collective-permute-start | bytes 1179656 | tf_op jit(solution)/shard_map/ppermute | solution.py:498
  45.8 13.0 %collective-permute-start.6 = (f32[8,96,128]{2,1,0:T(8,128)S(1)}, f32[8,96,128]{2,1,0:T(8,128)S(1)}, u32[]{:S(2)}, u32[]{:S(2)}) collective-permute-start(f32[8,96,128]{2,1,0:T(8,128)S(1)} %get-tuple-element.39), channel_id=1, source_target_pairs={{0,1},{1,2},{2,3},{4,5},{5,6},{6,7},{8,9},{9,10},{10,11},{12,13},{... | collective-permute-start | bytes 1179656 | tf_op jit(solution)/shard_map/ppermute | solution.py:498
  49.9 11.4 %collective-permute-start.9 = (f32[8,96,128]{2,1,0:T(8,128)S(1)}, f32[8,96,128]{2,1,0:T(8,128)S(1)}, u32[]{:S(2)}, u32[]{:S(2)}) collective-permute-start(f32[8,96,128]{2,1,0:T(8,128)S(1)} %get-tuple-element.41), channel_id=1, source_target_pairs={{1,0},{2,1},{3,2},{5,4},{6,5},{7,6},{9,8},{10,9},{11,10},{13,12},{... | collective-permute-start | bytes 1179656 | tf_op jit(solution)/shard_map/ppermute | solution.py:498
  114.1 22.4 %all-to-all-start.1 = ((f32[32,16,128]{2,1,0:T(8,128)}), f32[32,16,128]{2,1,0:T(8,128)S(1)}, u32[]{:S(2)}, u32[]{:S(2)}) async-start(f32[32,16,128]{2,1,0:T(8,128)} %relay.1), calls=%async_computation.1 | async-start | bytes 524288 | tf_op jit(solution)/shard_map/all_to_all | solution.py:565

commit v5 on v4

--- a/solution.py
+++ b/solution.py
@@ -17,6 +17,9 @@
 COLS = BROAD // 8
 VMEM = pl.BlockSpec(memory_space=pltpu.VMEM)
 SMEM = pl.BlockSpec(memory_space=pltpu.SMEM)
+HBM = pl.BlockSpec(memory_space=pltpu.HBM)
+PARTS = 4
+PACK_LIMIT = 60 << 20
 
 
 def lane_ids():
@@ -37,7 +40,10 @@
     return (lane // 2) + 64 * (lane % 2)
 
 
-def pack_kernel(adm_ref, now_ref, old_ref, cls_ref, s_ref, head_ref, tail_ref):
+def pack_kernel(
+    adm_hbm, now_hbm, old_hbm, cls_hbm, s_hbm, head_hbm, tail_hbm,
+    adm_ref, now_ref, old_ref, cls_ref, s_ref, head_ref, tail_ref, sems, out_sems, one_sem
+):
     order = even_odd()
 
     def layer(h, carry):
@@ -57,7 +63,31 @@
                     tail_ref[h, a, pl.ds(8 * j - WIDE + HALO, 8), :] = split
         return carry
 
-    lax.fori_loop(0, HIGH, layer, 0)
+    layers = HIGH // PARTS
+    fields = ((cls_hbm, cls_ref), (now_hbm, now_ref), (old_hbm, old_ref))
+    single = pltpu.make_async_copy(adm_hbm, adm_ref, one_sem)
+    single.start()
+    copies = []
+    for part in range(PARTS):
+        at = pl.ds(part * layers, layers)
+        for n, (src, dst) in enumerate(fields):
+            copy = pltpu.make_async_copy(src.at[at], dst.at[at], sems.at[part, n])
+            copy.start()
+            copies.append(copy)
+    results = ((s_ref, s_hbm), (head_ref, head_hbm), (tail_ref, tail_hbm))
+    last = []
+    single.wait()
+    for part in range(PARTS):
+        for copy in copies[3 * part : 3 * part + 3]:
+            copy.wait()
+        lax.fori_loop(part * layers, (part + 1) * layers, layer, 0)
+        at = pl.ds(part * layers, layers)
+        for n, (src, dst) in enumerate(results):
+            copy = pltpu.make_async_copy(src.at[at], dst.at[at], out_sems.at[part, n])
+            copy.start()
+            last.append(copy)
+    for copy in last:
+        copy.wait()
 
 
 def face_lanes(fields):
@@ -471,6 +501,13 @@
         out_ref[i] = total
 
 
+def total_kernel(got_ref, out_ref):
+    total = got_ref[0]
+    for i in range(1, got_ref.shape[0]):
+        total = total + got_ref[i]
+    out_ref[...] = total
+
+
 def field(*shape):
     return jax.ShapeDtypeStruct(shape, jnp.float32)
 
@@ -502,13 +539,27 @@
     pressure_now, pressure_old, classes, admittance, source_cells, source_signal, receiver_cells
 ):
     face = (HIGH, 3, HALO, LANES)
-    s, head, tail = call(
+    block = (HIGH, WIDE, DEEP)
+    s, head, tail = pl.pallas_call(
         pack_kernel,
-        "pack",
-        [(HIGH, 3, WIDE, LANES), face, face],
-        [admittance, pressure_now, pressure_old, classes],
-        scalars=1,
-    )
+        out_shape=(field(HIGH, 3, WIDE, LANES), field(*face), field(*face)),
+        in_specs=[HBM] * 4,
+        out_specs=(HBM,) * 3,
+        scratch_shapes=[
+            pltpu.SMEM(admittance.shape, jnp.float32),
+            pltpu.VMEM(block, jnp.float32),
+            pltpu.VMEM(block, jnp.float32),
+            pltpu.VMEM(block, jnp.int32),
+            pltpu.VMEM((HIGH, 3, WIDE, LANES), jnp.float32),
+            pltpu.VMEM(face, jnp.float32),
+            pltpu.VMEM(face, jnp.float32),
+            pltpu.SemaphoreType.DMA((PARTS, 3)),
+            pltpu.SemaphoreType.DMA((PARTS, 3)),
+            pltpu.SemaphoreType.DMA,
+        ],
+        name="pack",
+        compiler_params=pltpu.CompilerParams(vmem_limit_bytes=PACK_LIMIT),
+    )(admittance, pressure_now, pressure_old, classes)
     over, under = shift(s, "hgt", -1), shift(s, "hgt", 1)
     before, after = shift(tail, "wid", 1), shift(head, "wid", -1)
     strip = (HIGH, (BROAD - HALO) // 2, LANES)
@@ -564,7 +615,8 @@
     (traces,) = call(relay_kernel, "relay", [(sides, STEPS, LANES)], [traces])
     traces = lax.all_to_all(traces, ("wid", "hgt"), 0, 0, tiled=True)
     (now,) = call(order_kernel, "order", [(HIGH, WIDE, DEEP)], [split])
-    return now, jnp.sum(traces, axis=0)
+    (traces,) = call(total_kernel, "total", [(STEPS, LANES)], [traces])
+    return now, traces
 
 
 def solution(mesh):

time: 138 us -> 135 us (0.978)
  local copies, waits for them, and re-layouts: 3.79 us -> 1.42 us
  Pallas kernels: 49.6 us -> 51.8 us
    pallas_call x0 -> x1, Pallas kernels: none -> 3.69 us  [per_device(): pl.pallas_call(pack_kernel, out_shape=(field(HIGH, 3, WIDE, LANES), field...]
    unnamed x14 -> x10, local copies, waits for them, and re-layouts: 3.79 us -> 1.42 us
    pallas_call x9, Pallas kernels: 49.6 us -> 48.1 us  [call(): pl.pallas_call(kernel, out_shape=tuple(out_shape), in_specs=[SMEM] * scal...]
where the time goes in v5:
time: 135 us
  Pallas kernels  51.8 us (38%)
  starting transfers between devices  39.5 us (29%)
  blocking collectives  24.4 us (18%)
  waiting for transfers between devices  17 us (13%)
  local copies, waits for them, and re-layouts  1.42 us (1%)
    pallas_call x9, Pallas kernels, call(): pl.pallas_call(kernel, out_shape=tuple(out_shape), in_specs=[SMEM] * scal...  48.1 us
    ppermute x10, starting transfers between devices, shift(): return lax.ppermute(x, axis, pairs)  29.8 us
    all_to_all x1, blocking collectives, per_device(): traces = lax.all_to_all(traces, 'len', 0, 0, tiled=True)  24.4 us
    all_to_all x1, waiting for transfers between devices, per_device(): traces = lax.all_to_all(traces, ('wid', 'hgt'), 0, 0, tiled=True)  10.2 us
    all_to_all x1, starting transfers between devices, per_device(): traces = lax.all_to_all(traces, ('wid', 'hgt'), 0, 0, tiled=True)  9.71 us
    ppermute x10, waiting for transfers between devices, shift(): return lax.ppermute(x, axis, pairs)  6.74 us
    pallas_call x1, Pallas kernels, per_device(): pl.pallas_call(pack_kernel, out_shape=(field(HIGH, 3, WIDE, LANES), field...  3.69 us
  transfers between devices with their start and end apart: 11, of which 4 were waited for; matrix products, arithmetic and copies ran while one was open for 0% of the time, Pallas kernels for 14%

profile of v5, /device:TPU:1, one launch (start us, length us, event | category | flops | bytes accessed | tf_op | source)
XLA Modules:
  0.0 134.9 jit_solution(7168286886220529644)
XLA Ops:
  0.6 0.0 copy-start.4
  0.6 3.7 %pack.1 = (f32[16,3,64,128]{3,2,1,0:T(8,128)}, f32[16,3,16,128]{3,2,1,0:T(8,128)}, f32[16,3,16,128]{3,2,1,0:T(8,128)}) custom-call(f32[8]{0:T(128)} %adm_hbm.1, f32[16,64,128]{2,1,0:T(8,128)} %now_hbm.1, f32[16,64,128]{2,1,0:T(8,128)} %old_hbm.1, s32[16,64,128]{2,1,0:T(8,128)} %cls_hbm.1), custom_call_target="tpu_custom_call" | custom-call | tf_op jit(solution)/shard_map/pack/pallas_call | solution.py:543
  4.3 4.0 %collective-permute-start.4 = (f32[16,3,64,128]{3,2,1,0:T(8,128)}, f32[16,3,64,128]{3,2,1,0:T(8,128)S(1)}, u32[]{:S(2)}, u32[]{:S(2)}) collective-permute-start(f32[16,3,64,128]{3,2,1,0:T(8,128)} %get-tuple-element.23.s_ref.refs_0_), channel_id=1, source_target_pairs={{0,1},{1,2},{2,3},{4,5},{5,6},{6,7},{8,9},{9,10},{10,11},{12,13},{... | collective-permute-start | bytes 4718600 | tf_op jit(solution)/shard_map/ppermute | solution.py:535
  8.4 1.3 collective-permute-start.7
  9.7 3.2 %collective-permute-start = (f32[16,3,16,128]{3,2,1,0:T(8,128)}, f32[16,3,16,128]{3,2,1,0:T(8,128)S(1)}, u32[]{:S(2)}, u32[]{:S(2)}) collective-permute-start(f32[16,3,16,128]{3,2,1,0:T(8,128)} %get-tuple-element.25), channel_id=1, source_target_pairs={{0,4},{4,8},{8,12},{12,16},{16,20},{20,24},{24,28},{1,5},{5,9},{9,... | collective-permute-start | bytes 1179656 | tf_op jit(solution)/shard_map/ppermute | solution.py:535
  12.9 1.3 collective-permute-start.1
  14.2 0.0 copy-done.4
  14.2 0.0 copy-start
  14.2 1.4 %copy-done = f32[16,3,64,128]{3,2,1,0:T(8,128)S(1)} copy-done((f32[16,3,64,128]{3,2,1,0:T(8,128)S(1)}, f32[16,3,64,128]{3,2,1,0:T(8,128)}, u32[]{:S(2)}) %copy-start) | copy-done | bytes 1572888
  15.6 6.5 %own_strip.1 = (f32[16,64,128]{2,1,0:T(8,128)S(1)}, s32[8,128]{1,0:T(8,128)S(1)}) custom-call(s32[3,128]{1,0:T(4,128)S(1)} %bitcast.4, f32[16,3,64,128]{3,2,1,0:T(8,128)S(1)} %copy-done), custom_call_target="tpu_custom_call" | custom-call | tf_op jit(solution)/shard_map/own_strip/pallas_call | solution.py:521
  22.1 0.0 copy-start.1
  22.1 0.0 copy-start.2
  22.1 0.0 copy-start.3
  22.2 0.0 collective-permute-done.before_ref.refs_2_
  22.2 1.2 collective-permute-done.1.after_ref.refs_3_
  23.3 0.2 wide_rim.1
  23.5 3.7 %collective-permute-start.5 = (f32[8,96,128]{2,1,0:T(8,128)S(1)}, f32[8,96,128]{2,1,0:T(8,128)S(1)}, u32[]{:S(2)}, u32[]{:S(2)}) collective-permute-start(f32[8,96,128]{2,1,0:T(8,128)S(1)} %get-tuple-element.38), channel_id=1, source_target_pairs={{0,1},{1,2},{2,3},{4,5},{5,6},{6,7},{8,9},{9,10},{10,11},{12,13},{... | collective-permute-start | bytes 1179656 | tf_op jit(solution)/shard_map/ppermute | solution.py:535
  27.2 1.2 strip.1
  28.5 5.7 %collective-permute-start.2 = (f32[16,40,128]{2,1,0:T(8,128)S(1)}, f32[16,40,128]{2,1,0:T(8,128)S(1)}, u32[]{:S(2)}, u32[]{:S(2)}) collective-permute-start(f32[16,40,128]{2,1,0:T(8,128)S(1)} %get-tuple-element.31), channel_id=1, source_target_pairs={{32,0},{64,32},{96,64},{128,96},{160,128},{192,160},{224,192},{256... | collective-permute-start | bytes 983048 | tf_op jit(solution)/shard_map/ppermute | solution.py:535
  34.2 3.9 %collective-permute-start.3 = (f32[16,40,128]{2,1,0:T(8,128)S(1)}, f32[16,40,128]{2,1,0:T(8,128)S(1)}, u32[]{:S(2)}, u32[]{:S(2)}) collective-permute-start(f32[16,40,128]{2,1,0:T(8,128)S(1)} %get-tuple-element.32), channel_id=1, source_target_pairs={{0,32},{32,64},{64,96},{96,128},{128,160},{160,192},{192,224},{224... | collective-permute-start | bytes 983048 | tf_op jit(solution)/shard_map/ppermute | solution.py:535
  38.1 3.1 %collective-permute-done.2.from_right_ref = f32[16,40,128]{2,1,0:T(8,128)S(1)} collective-permute-done((f32[16,40,128]{2,1,0:T(8,128)S(1)}, f32[16,40,128]{2,1,0:T(8,128)S(1)}, u32[]{:S(2)}, u32[]{:S(2)}) %collective-permute-start.2) | collective-permute-done | bytes 327712 | tf_op jit(solution)/shard_map/ppermute | solution.py:535
  41.2 1.3 collective-permute-start.8
  42.5 0.0 collective-permute-done.3.from_left_ref
  42.5 1.3 long_rim.1
  43.8 4.0 %collective-permute-start.6 = (f32[8,96,128]{2,1,0:T(8,128)S(1)}, f32[8,96,128]{2,1,0:T(8,128)S(1)}, u32[]{:S(2)}, u32[]{:S(2)}) collective-permute-start(f32[8,96,128]{2,1,0:T(8,128)S(1)} %get-tuple-element.39), channel_id=1, source_target_pairs={{0,1},{1,2},{2,3},{4,5},{5,6},{6,7},{8,9},{9,10},{10,11},{12,13},{... | collective-permute-start | bytes 1179656 | tf_op jit(solution)/shard_map/ppermute | solution.py:535
  47.8 0.0 collective-permute-done.5.refs_5_
  47.8 1.3 collective-permute-start.9
  49.1 0.0 copy-done.1
  49.2 0.0 copy-done.2
  49.2 0.0 copy-done.3
  49.2 7.6 %inner.1 = (f32[2,16,12,8,128]{4,3,2,1,0:T(8,128)S(1)}, f32[2,16,12,8,128]{4,3,2,1,0:T(8,128)S(1)}, f32[2,16,12,8,128]{4,3,2,1,0:T(8,128)S(1)}, f32[16,128]{1,0:T(8,128)S(1)}) custom-call(s32[4,3]{1,0:T(4,128)S(1)} %copy-done.2, f32[4,16]{1,0:T(4,128)S(1)} %bitcast.2, s32[8,128]{1,0:T(8,128)S(1)} %get-tuple-element.24.todo, ...), custom_call_target="tpu_custom_call" | custom-call | tf_op jit(solution)/shard_map/inner/pallas_call | solution.py:521
  56.8 0.0 collective-permute-done.8.refs_8_
  56.8 0.0 collective-permute-done.6.refs_6_
  56.8 2.5 %collective-permute-done.9.refs_9_ = f32[8,96,128]{2,1,0:T(8,128)S(1)} collective-permute-done((f32[8,96,128]{2,1,0:T(8,128)S(1)}, f32[8,96,128]{2,1,0:T(8,128)S(1)}, u32[]{:S(2)}, u32[]{:S(2)}) %collective-permute-start.9) | collective-permute-done | bytes 393248 | tf_op jit(solution)/shard_map/ppermute | solution.py:535
  59.3 0.0 collective-permute-done.4.refs_4_
  59.3 0.0 collective-permute-done.7.refs_7_
  59.3 27.9 %march.1 = (f32[16,64,128]{2,1,0:T(8,128)S(1)}, f32[16,16,128]{2,1,0:T(8,128)S(1)}) custom-call(s32[4,3]{1,0:T(4,128)S(1)} %copy-done.2, f32[4,16]{1,0:T(4,128)S(1)} %bitcast.3, s32[8,128]{1,0:T(8,128)S(1)} %get-tuple-element.24.todo, f32[2,16,12,8,128]{4,3,2,1,0:T(8,128)S(1)} %get-tuple-element.34.refs_0_, ...), custom_call_target="tpu_custom_call" | custom-call | tf_op jit(solution)/shard_map/march/pallas_call | solution.py:521
  87.2 24.4 %all_to_all.10.got_ref = f32[16,16,128]{2,1,0:T(8,128)S(1)} all-to-all(f32[16,16,128]{2,1,0:T(8,128)S(1)} %get-tuple-element.43), channel_id=1, replica_groups=mesh['len'=16,'wid'=8,'hgt'=4] {'len'}, dimensions={0} | all-to-all | bytes 262144 | tf_op jit(solution)/shard_map/all_to_all | solution.py:614
  111.6 0.7 relay.1
  112.3 9.7 %all-to-all-start.1 = ((f32[32,16,128]{2,1,0:T(8,128)}), f32[32,16,128]{2,1,0:T(8,128)S(1)}, u32[]{:S(2)}, u32[]{:S(2)}) async-start(f32[32,16,128]{2,1,0:T(8,128)} %relay.1), calls=%async_computation.1 | async-start | bytes 524288 | tf_op jit(solution)/shard_map/all_to_all | solution.py:616
  122.0 2.0 %order.1 = f32[16,64,128]{2,1,0:T(8,128)} custom-call(f32[16,64,128]{2,1,0:T(8,128)S(1)} %get-tuple-element.42.split_ref), custom_call_target="tpu_custom_call" | custom-call | tf_op jit(solution)/shard_map/order/pallas_call | solution.py:521
  124.1 10.2 %all-to-all-done.1.got_ref = f32[32,16,128]{2,1,0:T(8,128)S(1)} async-done(((f32[32,16,128]{2,1,0:T(8,128)}), f32[32,16,128]{2,1,0:T(8,128)S(1)}, u32[]{:S(2)}, u32[]{:S(2)}) %all-to-all-start.1) | async-done | bytes 262176 | tf_op jit(solution)/shard_map/all_to_all | solution.py:616
  134.3 0.6 total.1
Async XLA Ops:
  0.6 13.6 %copy-start.4 = (s32[128,3]{0,1:T(4,128)S(1)}, s32[128,3]{0,1:T(4,128)}, u32[]{:S(2)}) copy-start(s32[128,3]{0,1:T(4,128)} %param.13) | copy-start | bytes 4612
  4.3 54.9 %collective-permute-start.4 = (f32[16,3,64,128]{3,2,1,0:T(8,128)}, f32[16,3,64,128]{3,2,1,0:T(8,128)S(1)}, u32[]{:S(2)}, u32[]{:S(2)}) collective-permute-start(f32[16,3,64,128]{3,2,1,0:T(8,128)} %get-tuple-element.23.s_ref.refs_0_), channel_id=1, source_target_pairs={{0,1},{1,2},{2,3},{4,5},{5,6},{6,7},{8,9},{9,10},{10,11},{12,13},{... | collective-permute-start | bytes 4718600 | tf_op jit(solution)/shard_map/ppermute | solution.py:535
  8.4 50.9 %collective-permute-start.7 = (f32[16,3,64,128]{3,2,1,0:T(8,128)}, f32[16,3,64,128]{3,2,1,0:T(8,128)S(1)}, u32[]{:S(2)}, u32[]{:S(2)}) collective-permute-start(f32[16,3,64,128]{3,2,1,0:T(8,128)} %get-tuple-element.23.s_ref.refs_0_), channel_id=1, source_target_pairs={{1,0},{2,1},{3,2},{5,4},{6,5},{7,6},{9,8},{10,9},{11,10},{13,12},{... | collective-permute-start | bytes 4718600 | tf_op jit(solution)/shard_map/ppermute | solution.py:535
  9.7 12.5 %collective-permute-start = (f32[16,3,16,128]{3,2,1,0:T(8,128)}, f32[16,3,16,128]{3,2,1,0:T(8,128)S(1)}, u32[]{:S(2)}, u32[]{:S(2)}) collective-permute-start(f32[16,3,16,128]{3,2,1,0:T(8,128)} %get-tuple-element.25), channel_id=1, source_target_pairs={{0,4},{4,8},{8,12},{12,16},{16,20},{20,24},{24,28},{1,5},{5,9},{9,... | collective-permute-start | bytes 1179656 | tf_op jit(solution)/shard_map/ppermute | solution.py:535
  12.9 10.4 %collective-permute-start.1 = (f32[16,3,16,128]{3,2,1,0:T(8,128)}, f32[16,3,16,128]{3,2,1,0:T(8,128)S(1)}, u32[]{:S(2)}, u32[]{:S(2)}) collective-permute-start(f32[16,3,16,128]{3,2,1,0:T(8,128)} %get-tuple-element.26), channel_id=1, source_target_pairs={{4,0},{8,4},{12,8},{16,12},{20,16},{24,20},{28,24},{5,1},{9,5},{13... | collective-permute-start | bytes 1179656 | tf_op jit(solution)/shard_map/ppermute | solution.py:535
  14.2 1.4 %copy-start = (f32[16,3,64,128]{3,2,1,0:T(8,128)S(1)}, f32[16,3,64,128]{3,2,1,0:T(8,128)}, u32[]{:S(2)}) copy-start(f32[16,3,64,128]{3,2,1,0:T(8,128)} %get-tuple-element.23.s_ref.refs_0_) | copy-start | bytes 4718596
  22.1 27.0 %copy-start.1 = (f32[16,3,64,128]{3,2,1,0:T(8,128)S(1)}, f32[16,3,64,128]{3,2,1,0:T(8,128)}, u32[]{:S(2)}) copy-start(f32[16,3,64,128]{3,2,1,0:T(8,128)} %get-tuple-element.23.s_ref.refs_0_) | copy-start | bytes 4718596
  22.1 27.0 %copy-start.2 = (s32[4,3]{1,0:T(4,128)S(1)}, s32[4,3]{1,0:T(4,128)}, u32[]{:S(2)}) copy-start(s32[4,3]{1,0:T(4,128)} %src_ref.3) | copy-start | bytes 148
  22.1 27.0 %copy-start.3 = (f32[16,4]{0,1:T(4,128)S(1)}, f32[16,4]{0,1:T(4,128)}, u32[]{:S(2)}) copy-start(f32[16,4]{0,1:T(4,128)} %param.12) | copy-start | bytes 772
  23.5 24.3 %collective-permute-start.5 = (f32[8,96,128]{2,1,0:T(8,128)S(1)}, f32[8,96,128]{2,1,0:T(8,128)S(1)}, u32[]{:S(2)}, u32[]{:S(2)}) collective-permute-start(f32[8,96,128]{2,1,0:T(8,128)S(1)} %get-tuple-element.38), channel_id=1, source_target_pairs={{0,1},{1,2},{2,3},{4,5},{5,6},{6,7},{8,9},{9,10},{10,11},{12,13},{... | collective-permute-start | bytes 1179656 | tf_op jit(solution)/shard_map/ppermute | solution.py:535
  28.5 12.7 %collective-permute-start.2 = (f32[16,40,128]{2,1,0:T(8,128)S(1)}, f32[16,40,128]{2,1,0:T(8,128)S(1)}, u32[]{:S(2)}, u32[]{:S(2)}) collective-permute-start(f32[16,40,128]{2,1,0:T(8,128)S(1)} %get-tuple-element.31), channel_id=1, source_target_pairs={{32,0},{64,32},{96,64},{128,96},{160,128},{192,160},{224,192},{256... | collective-permute-start | bytes 983048 | tf_op jit(solution)/shard_map/ppermute | solution.py:535
  34.2 8.3 %collective-permute-start.3 = (f32[16,40,128]{2,1,0:T(8,128)S(1)}, f32[16,40,128]{2,1,0:T(8,128)S(1)}, u32[]{:S(2)}, u32[]{:S(2)}) collective-permute-start(f32[16,40,128]{2,1,0:T(8,128)S(1)} %get-tuple-element.32), channel_id=1, source_target_pairs={{0,32},{32,64},{64,96},{96,128},{128,160},{160,192},{192,224},{224... | collective-permute-start | bytes 983048 | tf_op jit(solution)/shard_map/ppermute | solution.py:535
  41.2 15.6 %collective-permute-start.8 = (f32[8,96,128]{2,1,0:T(8,128)S(1)}, f32[8,96,128]{2,1,0:T(8,128)S(1)}, u32[]{:S(2)}, u32[]{:S(2)}) collective-permute-start(f32[8,96,128]{2,1,0:T(8,128)S(1)} %get-tuple-element.40), channel_id=1, source_target_pairs={{1,0},{2,1},{3,2},{5,4},{6,5},{7,6},{9,8},{10,9},{11,10},{13,12},{... | collective-permute-start | bytes 1179656 | tf_op jit(solution)/shard_map/ppermute | solution.py:535
  43.8 13.0 %collective-permute-start.6 = (f32[8,96,128]{2,1,0:T(8,128)S(1)}, f32[8,96,128]{2,1,0:T(8,128)S(1)}, u32[]{:S(2)}, u32[]{:S(2)}) collective-permute-start(f32[8,96,128]{2,1,0:T(8,128)S(1)} %get-tuple-element.39), channel_id=1, source_target_pairs={{0,1},{1,2},{2,3},{4,5},{5,6},{6,7},{8,9},{9,10},{10,11},{12,13},{... | collective-permute-start | bytes 1179656 | tf_op jit(solution)/shard_map/ppermute | solution.py:535
  47.8 11.4 %collective-permute-start.9 = (f32[8,96,128]{2,1,0:T(8,128)S(1)}, f32[8,96,128]{2,1,0:T(8,128)S(1)}, u32[]{:S(2)}, u32[]{:S(2)}) collective-permute-start(f32[8,96,128]{2,1,0:T(8,128)S(1)} %get-tuple-element.41), channel_id=1, source_target_pairs={{1,0},{2,1},{3,2},{5,4},{6,5},{7,6},{9,8},{10,9},{11,10},{13,12},{... | collective-permute-start | bytes 1179656 | tf_op jit(solution)/shard_map/ppermute | solution.py:535
  112.3 22.0 %all-to-all-start.1 = ((f32[32,16,128]{2,1,0:T(8,128)}), f32[32,16,128]{2,1,0:T(8,128)S(1)}, u32[]{:S(2)}, u32[]{:S(2)}) async-start(f32[32,16,128]{2,1,0:T(8,128)} %relay.1), calls=%async_computation.1 | async-start | bytes 524288 | tf_op jit(solution)/shard_map/all_to_all | solution.py:616

commit v6 on v5

--- a/solution.py
+++ b/solution.py
@@ -18,7 +18,7 @@
 VMEM = pl.BlockSpec(memory_space=pltpu.VMEM)
 SMEM = pl.BlockSpec(memory_space=pltpu.SMEM)
 HBM = pl.BlockSpec(memory_space=pltpu.HBM)
-PARTS = 4
+PARTS = 8
 PACK_LIMIT = 60 << 20
 
 
@@ -260,29 +260,71 @@
     lax.fori_loop(0, HIGH, layer, 0)
 
 
-def fill_beside(refs, temp, s_ref, rim_ref, edge_ref, layers):
+def fill_main(refs, temp, at):
+    lane = lane_ids()
+    for j in range(COLS):
+        for a, ref in enumerate(refs):
+            main = temp[a, pl.ds(j, 8, stride=COLS), :]
+            for parity in range(2):
+                mid = pltpu.roll(main, 64, 1) if parity else main
+                ref[parity, at, j] = jnp.where(lane < 64, mid, jnp.float32(0.0))
+
+
+def fill_edge(refs, mains, temp, at, source):
+    lane = lane_ids()
+    fringe = ((lane >= 64) & (lane < 72)) | (lane >= 120)
+    for j in range(COLS):
+        edge = temp[pl.ds(j, 8, stride=COLS), :]
+        for a, (ref, main) in enumerate(zip(refs, mains)):
+            for parity in range(2):
+                turn = 8 * (2 * a + parity)
+                near = pltpu.roll(edge, LANES - turn, 1) if turn else edge
+                ref[parity, at, j] = jnp.where(fringe, near, main[parity, source, j])
+
+
+def fill_beside(refs, temp, s_ref, rim_ref, layers):
     def pair(i, carry):
         near, far = layers(i)
         for a in range(3):
-            temp[a, pl.ds(0, HALO), :] = rim_ref[i, pl.ds(2 * HALO * a, HALO), :]
+            before = rim_ref[i, pl.ds(2 * HALO * a, HALO), :]
+            after = rim_ref[i, pl.ds(2 * HALO * a + HALO, HALO), :]
+            temp[a, pl.ds(0, HALO), :] = before
             temp[a, pl.ds(HALO, WIDE), :] = s_ref[near % HIGH, a]
-            temp[a, pl.ds(HALO + WIDE, HALO), :] = rim_ref[i, pl.ds(2 * HALO * a + HALO, HALO), :]
-        temp[3] = edge_ref[i]
-        fill(refs, temp, near)
+            temp[a, pl.ds(HALO + WIDE, HALO), :] = after
+        fill_main(refs, temp, near)
         for a in range(3):
             before = rim_ref[i, pl.ds(2 * HALO * a, HALO), :]
+            after = rim_ref[i, pl.ds(2 * HALO * a + HALO, HALO), :]
             temp[a, pl.ds(0, HALO), :] = pltpu.roll(before, (HALO - i) % HALO, 0)
             temp[a, pl.ds(HALO, WIDE), :] = s_ref[far % HIGH, a]
-            after = rim_ref[i, pl.ds(2 * HALO * a + HALO, HALO), :]
             temp[a, pl.ds(HALO + WIDE, HALO), :] = pltpu.roll(after, i, 0)
+        fill_main(refs, temp, far)
+        return carry
+
+    lax.fori_loop(0, HALF, pair, 0)
+
+
+def beside_kernel(under, under_rim, over, over_rim, *refs):
+    fields, temp = refs[:3], refs[3]
+    fill_beside(fields, temp, under, under_rim, lambda i: (HALO - 1 - i, i))
+    fill_beside(fields, temp, over, over_rim, lambda i: (HALO + i, 2 * HALO - 1 - i))
+
+
+def fill_edges(refs, mains, temp, edge_ref, layers, skip):
+    first, second = temp.at[0], temp.at[1]
+
+    def pair(i, carry):
+        near, far = layers(i)
+        first[...] = edge_ref[i]
+        fill_edge(refs, mains, first, near + skip, near)
         right, n, _ = beside_lanes(i)
         k = lane_ids() % 8
         mask = (right & (k < 8 - n)) | (~right & (k >= n))
         for j in range(COLS):
             both = edge_ref[i, pl.ds(8 * j, 8), :]
             moved = jnp.where(right, pltpu.roll(both, LANES - n, 1), pltpu.roll(both, n, 1))
-            temp[3, pl.ds(8 * j, 8), :] = jnp.where(mask, moved, jnp.float32(0.0))
-        fill(refs, temp, far)
+            second[pl.ds(8 * j, 8), :] = jnp.where(mask, moved, jnp.float32(0.0))
+        fill_edge(refs, mains, second, far + skip, far)
         return carry
 
     lax.fori_loop(0, HALF, pair, 0)
@@ -368,12 +410,18 @@
 
 
 def inject(field, points, sig_ref, t, base, inside):
-    for s, (near, parity, h, j, spot) in enumerate(points):
-
-        @pl.when(near & inside(h))
-        def _():
-            add = jnp.where(spot, sig_ref[s, t], jnp.float32(0.0))
-            field[parity, h - base, j] = field[parity, h - base, j] + add
+    some = points[0][0]
+    for point in points[1:]:
+        some = some | point[0]
+
+    @pl.when(some)
+    def _():
+        for s, (near, parity, h, j, spot) in enumerate(points):
+
+            @pl.when(near & inside(h))
+            def _():
+                add = jnp.where(spot, sig_ref[s, t], jnp.float32(0.0))
+                field[parity, h - base, j] = field[parity, h - base, j] + add
 
 
 def keep(field, todo, hist, t, base):
@@ -422,9 +470,9 @@
 
 def march_kernel(src_ref, sig_ref, todo, *refs):
     own = refs[:3]
-    early_ref, under, over = refs[3], refs[4:7], refs[7:10]
-    out_ref, trace_ref = refs[10:12]
-    a_ref, b_ref, p_ref, temp, hist = refs[12:]
+    early_ref, mains, under_edge, over_edge = refs[3], refs[4:7], refs[7], refs[8]
+    out_ref, trace_ref = refs[9:11]
+    a_ref, b_ref, p_ref, temp, hist = refs[11:]
     fields = (a_ref, b_ref, p_ref)
 
     def take(h, carry):
@@ -434,8 +482,8 @@
         return carry
 
     lax.fori_loop(0, HIGH, take, 0)
-    fill_beside(fields, temp, *under, lambda i: (HALO - 1 - i, i))
-    fill_beside(fields, temp, *over, lambda i: (HALO + HIGH + i, TALL - 1 - i))
+    fill_edges(fields, mains, temp, under_edge, lambda i: (HALO - 1 - i, i), 0)
+    fill_edges(fields, mains, temp, over_edge, lambda i: (HALO + i, 2 * HALO - 1 - i), HIGH)
     points = list_sources(src_ref)
 
     def step(now, old, t):
@@ -584,7 +632,9 @@
         [(HIGH, BROAD, LANES), long_rim, long_rim],
         [from_right, from_left],
     )
-    over_edge, under_edge = shift(low, "hgt", -1), shift(top, "hgt", 1)
+    under_edge = shift(top, "hgt", 1)
+    low, under = lax.optimization_barrier((low, under))
+    over_edge = shift(low, "hgt", -1)
     own = (2, HIGH, COLS, 8, LANES)
     temp = pltpu.VMEM((4, BROAD, LANES), jnp.float32)
     hist = pltpu.VMEM((LANES, STEPS, LANES), jnp.float32)
@@ -598,6 +648,15 @@
         scalars=3,
         limit=8,
     )
+    halos = (2, 2 * HALO, COLS, 8, LANES)
+    mains = call(
+        beside_kernel,
+        "beside",
+        [halos] * 3,
+        [under, under_rim, over, over_rim],
+        scratch=[temp],
+        limit=16,
+    )
     state = pltpu.VMEM((2, TALL, COLS, 8, LANES), jnp.float32)
     depth = lax.axis_size("len")
     sides = lax.axis_size("wid") * lax.axis_size("hgt")
@@ -606,7 +665,7 @@
         "march",
         [(HIGH, WIDE, LANES), (depth, STEPS, LANES)],
         [source_cells, source_signal.T, todo, now, old, gain, early]
-        + [under, under_rim, under_edge, over, over_rim, over_edge],
+        + [*mains, under_edge, over_edge],
         scratch=[state, state, state, temp, hist],
         scalars=3,
         limit=20,

time: 135 us -> 133 us (0.985)
  waiting for transfers between devices: 17 us -> 14.9 us
    ppermute x10, waiting for transfers between devices: 6.74 us -> 4.67 us  [shift(): return lax.ppermute(x, axis, pairs)]
    pallas_call x9 -> x10, Pallas kernels: 48.1 us -> 48.8 us  [call(): pl.pallas_call(kernel, out_shape=tuple(out_shape), in_specs=[SMEM] * scal...]
  transfers between devices with their start and end apart: 11 -> 11, of which waited for: 4 -> 3; matrix products, arithmetic and copies ran while one was open for 0% -> 0% of each run, Pallas kernels for 14% -> 16%
where the time goes in v6:
time: 133 us
  Pallas kernels  52.5 us (39%)
  starting transfers between devices  39 us (29%)
  blocking collectives  24.1 us (18%)
  waiting for transfers between devices  14.9 us (11%)
  local copies, waits for them, and re-layouts  1.42 us (1%)
    pallas_call x10, Pallas kernels, call(): pl.pallas_call(kernel, out_shape=tuple(out_shape), in_specs=[SMEM] * scal...  48.8 us
    ppermute x10, starting transfers between devices, shift(): return lax.ppermute(x, axis, pairs)  29.5 us
    all_to_all x1, blocking collectives, per_device(): traces = lax.all_to_all(traces, 'len', 0, 0, tiled=True)  24.1 us
    all_to_all x1, waiting for transfers between devices, per_device(): traces = lax.all_to_all(traces, ('wid', 'hgt'), 0, 0, tiled=True)  10.2 us
    all_to_all x1, starting transfers between devices, per_device(): traces = lax.all_to_all(traces, ('wid', 'hgt'), 0, 0, tiled=True)  9.49 us
    ppermute x10, waiting for transfers between devices, shift(): return lax.ppermute(x, axis, pairs)  4.67 us
    pallas_call x1, Pallas kernels, per_device(): pl.pallas_call(pack_kernel, out_shape=(field(HIGH, 3, WIDE, LANES), field...  3.7 us
  transfers between devices with their start and end apart: 11, of which 3 were waited for; matrix products, arithmetic and copies ran while one was open for 0% of the time, Pallas kernels for 16%

profile of v6, /device:TPU:1, one launch (start us, length us, event | category | flops | bytes accessed | tf_op | source)
XLA Modules:
  0.0 132.8 jit_solution(4501074735718816040)
XLA Ops:
  0.6 0.0 copy-start.4
  0.6 3.7 %pack.1 = (f32[16,3,64,128]{3,2,1,0:T(8,128)}, f32[16,3,16,128]{3,2,1,0:T(8,128)}, f32[16,3,16,128]{3,2,1,0:T(8,128)}) custom-call(f32[8]{0:T(128)} %adm_hbm.1, f32[16,64,128]{2,1,0:T(8,128)} %now_hbm.1, f32[16,64,128]{2,1,0:T(8,128)} %old_hbm.1, s32[16,64,128]{2,1,0:T(8,128)} %cls_hbm.1), custom_call_target="tpu_custom_call" | custom-call | tf_op jit(solution)/shard_map/pack/pallas_call | solution.py:591
  4.4 4.0 %collective-permute-start.4 = (f32[16,3,64,128]{3,2,1,0:T(8,128)}, f32[16,3,64,128]{3,2,1,0:T(8,128)S(1)}, u32[]{:S(2)}, u32[]{:S(2)}) collective-permute-start(f32[16,3,64,128]{3,2,1,0:T(8,128)} %get-tuple-element.28.s_ref.refs_0_), channel_id=1, source_target_pairs={{0,1},{1,2},{2,3},{4,5},{5,6},{6,7},{8,9},{9,10},{10,11},{12,13},{... | collective-permute-start | bytes 4718600 | tf_op jit(solution)/shard_map/ppermute | solution.py:583
  8.4 1.3 collective-permute-start.6
  9.7 3.2 %collective-permute-start = (f32[16,3,16,128]{3,2,1,0:T(8,128)}, f32[16,3,16,128]{3,2,1,0:T(8,128)S(1)}, u32[]{:S(2)}, u32[]{:S(2)}) collective-permute-start(f32[16,3,16,128]{3,2,1,0:T(8,128)} %get-tuple-element.30), channel_id=1, source_target_pairs={{0,4},{4,8},{8,12},{12,16},{16,20},{20,24},{24,28},{1,5},{5,9},{9,... | collective-permute-start | bytes 1179656 | tf_op jit(solution)/shard_map/ppermute | solution.py:583
  12.9 1.3 collective-permute-start.1
  14.2 0.0 copy-done.4
  14.2 0.0 copy-start
  14.3 1.4 %copy-done = f32[16,3,64,128]{3,2,1,0:T(8,128)S(1)} copy-done((f32[16,3,64,128]{3,2,1,0:T(8,128)S(1)}, f32[16,3,64,128]{3,2,1,0:T(8,128)}, u32[]{:S(2)}) %copy-start) | copy-done | bytes 1572888
  15.7 6.5 %own_strip.1 = (f32[16,64,128]{2,1,0:T(8,128)S(1)}, s32[8,128]{1,0:T(8,128)S(1)}) custom-call(s32[3,128]{1,0:T(4,128)S(1)} %bitcast.4, f32[16,3,64,128]{3,2,1,0:T(8,128)S(1)} %copy-done), custom_call_target="tpu_custom_call" | custom-call | tf_op jit(solution)/shard_map/own_strip/pallas_call | solution.py:569
  22.1 0.0 copy-start.1
  22.1 0.0 copy-start.2
  22.2 0.0 copy-start.3
  22.2 0.0 collective-permute-done.before_ref.refs_2_
  22.2 1.2 collective-permute-done.1.after_ref.refs_3_
  23.3 1.2 strip.1
  24.6 5.1 %collective-permute-start.2 = (f32[16,40,128]{2,1,0:T(8,128)S(1)}, f32[16,40,128]{2,1,0:T(8,128)S(1)}, u32[]{:S(2)}, u32[]{:S(2)}) collective-permute-start(f32[16,40,128]{2,1,0:T(8,128)S(1)} %get-tuple-element.36), channel_id=1, source_target_pairs={{32,0},{64,32},{96,64},{128,96},{160,128},{192,160},{224,192},{256... | collective-permute-start | bytes 983048 | tf_op jit(solution)/shard_map/ppermute | solution.py:583
  29.7 3.9 %collective-permute-start.3 = (f32[16,40,128]{2,1,0:T(8,128)S(1)}, f32[16,40,128]{2,1,0:T(8,128)S(1)}, u32[]{:S(2)}, u32[]{:S(2)}) collective-permute-start(f32[16,40,128]{2,1,0:T(8,128)S(1)} %get-tuple-element.37), channel_id=1, source_target_pairs={{0,32},{32,64},{64,96},{96,128},{128,160},{160,192},{192,224},{224... | collective-permute-start | bytes 983048 | tf_op jit(solution)/shard_map/ppermute | solution.py:583
  33.6 0.2 wide_rim.1
  33.8 4.0 %collective-permute-start.5 = (f32[8,96,128]{2,1,0:T(8,128)S(1)}, f32[8,96,128]{2,1,0:T(8,128)S(1)}, u32[]{:S(2)}, u32[]{:S(2)}) collective-permute-start(f32[8,96,128]{2,1,0:T(8,128)S(1)} %get-tuple-element.45), channel_id=1, source_target_pairs={{0,1},{1,2},{2,3},{4,5},{5,6},{6,7},{8,9},{9,10},{10,11},{12,13},{... | collective-permute-start | bytes 1179656 | tf_op jit(solution)/shard_map/ppermute | solution.py:583
  37.8 0.0 collective-permute-done.2.from_right_ref
  37.8 1.3 collective-permute-start.7
  39.1 0.0 collective-permute-done.3.from_left_ref
  39.1 1.3 long_rim.1
  40.5 4.0 %collective-permute-start.8 = (f32[8,96,128]{2,1,0:T(8,128)S(1)}, f32[8,96,128]{2,1,0:T(8,128)S(1)}, u32[]{:S(2)}, u32[]{:S(2)}) collective-permute-start(f32[8,96,128]{2,1,0:T(8,128)S(1)} %get-tuple-element.50), channel_id=1, source_target_pairs={{0,1},{1,2},{2,3},{4,5},{5,6},{6,7},{8,9},{9,10},{10,11},{12,13},{... | collective-permute-start | bytes 1179656 | tf_op jit(solution)/shard_map/ppermute | solution.py:583
  44.5 0.0 collective-permute-done.4.under
  44.5 1.3 collective-permute-start.9
  45.8 0.0 copy-done.1
  45.8 0.0 copy-done.2
  45.8 0.0 copy-done.3
  45.8 7.4 %inner.1 = (f32[2,16,12,8,128]{4,3,2,1,0:T(8,128)S(1)}, f32[2,16,12,8,128]{4,3,2,1,0:T(8,128)S(1)}, f32[2,16,12,8,128]{4,3,2,1,0:T(8,128)S(1)}, f32[16,128]{1,0:T(8,128)S(1)}) custom-call(s32[4,3]{1,0:T(4,128)S(1)} %copy-done.2, f32[4,16]{1,0:T(4,128)S(1)} %bitcast.2, s32[8,128]{1,0:T(8,128)S(1)} %get-tuple-element.29.todo, ...), custom_call_target="tpu_custom_call" | custom-call | tf_op jit(solution)/shard_map/inner/pallas_call | solution.py:569
  53.2 0.0 collective-permute-done.5.under_rim
  53.2 0.0 collective-permute-done.7.over_rim
  53.2 0.0 collective-permute-done.6.over
  53.3 2.6 %beside.1 = (f32[2,32,12,8,128]{4,3,2,1,0:T(8,128)S(1)}, f32[2,32,12,8,128]{4,3,2,1,0:T(8,128)S(1)}, f32[2,32,12,8,128]{4,3,2,1,0:T(8,128)S(1)}) custom-call(f32[16,3,64,128]{3,2,1,0:T(8,128)S(1)} %collective-permute-done.4.under, f32[8,96,128]{2,1,0:T(8,128)S(1)} %collective-permute-done.5.under_rim, f32[16,3,64,128]{3,2,1,0:T(8,128)S(1)} %collective-permute-done.6.over, ...), custom_call_target="tpu_custom_call" | custom-call | tf_op jit(solution)/shard_map/beside/pallas_call | solution.py:569
  55.8 0.0 collective-permute-done.8.refs_7_
  55.8 3.5 %collective-permute-done.9.refs_8_ = f32[8,96,128]{2,1,0:T(8,128)S(1)} collective-permute-done((f32[8,96,128]{2,1,0:T(8,128)S(1)}, f32[8,96,128]{2,1,0:T(8,128)S(1)}, u32[]{:S(2)}, u32[]{:S(2)}) %collective-permute-start.9) | collective-permute-done | bytes 393248 | tf_op jit(solution)/shard_map/ppermute | solution.py:583
  59.3 26.2 %march.1 = (f32[16,64,128]{2,1,0:T(8,128)S(1)}, f32[16,16,128]{2,1,0:T(8,128)S(1)}) custom-call(s32[4,3]{1,0:T(4,128)S(1)} %copy-done.2, f32[4,16]{1,0:T(4,128)S(1)} %bitcast.3, s32[8,128]{1,0:T(8,128)S(1)} %get-tuple-element.29.todo, f32[2,16,12,8,128]{4,3,2,1,0:T(8,128)S(1)} %get-tuple-element.39.refs_0_, ...), custom_call_target="tpu_custom_call" | custom-call | tf_op jit(solution)/shard_map/march/pallas_call | solution.py:569
  85.6 24.1 %all_to_all.10.got_ref = f32[16,16,128]{2,1,0:T(8,128)S(1)} all-to-all(f32[16,16,128]{2,1,0:T(8,128)S(1)} %get-tuple-element.53), channel_id=1, replica_groups=mesh['len'=16,'wid'=8,'hgt'=4] {'len'}, dimensions={0} | all-to-all | bytes 262144 | tf_op jit(solution)/shard_map/all_to_all | solution.py:673
  109.7 0.7 relay.1
  110.4 9.5 %all-to-all-start.1 = ((f32[32,16,128]{2,1,0:T(8,128)}), f32[32,16,128]{2,1,0:T(8,128)S(1)}, u32[]{:S(2)}, u32[]{:S(2)}) async-start(f32[32,16,128]{2,1,0:T(8,128)} %relay.1), calls=%async_computation.1 | async-start | bytes 524288 | tf_op jit(solution)/shard_map/all_to_all | solution.py:675
  119.9 2.0 %order.1 = f32[16,64,128]{2,1,0:T(8,128)} custom-call(f32[16,64,128]{2,1,0:T(8,128)S(1)} %get-tuple-element.52.split_ref), custom_call_target="tpu_custom_call" | custom-call | tf_op jit(solution)/shard_map/order/pallas_call | solution.py:569
  122.0 10.2 %all-to-all-done.1.got_ref = f32[32,16,128]{2,1,0:T(8,128)S(1)} async-done(((f32[32,16,128]{2,1,0:T(8,128)}), f32[32,16,128]{2,1,0:T(8,128)S(1)}, u32[]{:S(2)}, u32[]{:S(2)}) %all-to-all-start.1) | async-done | bytes 262176 | tf_op jit(solution)/shard_map/all_to_all | solution.py:675
  132.2 0.6 total.1
Async XLA Ops:
  0.6 13.6 %copy-start.4 = (s32[128,3]{0,1:T(4,128)S(1)}, s32[128,3]{0,1:T(4,128)}, u32[]{:S(2)}) copy-start(s32[128,3]{0,1:T(4,128)} %param.13) | copy-start | bytes 4612
  4.4 40.1 %collective-permute-start.4 = (f32[16,3,64,128]{3,2,1,0:T(8,128)}, f32[16,3,64,128]{3,2,1,0:T(8,128)S(1)}, u32[]{:S(2)}, u32[]{:S(2)}) collective-permute-start(f32[16,3,64,128]{3,2,1,0:T(8,128)} %get-tuple-element.28.s_ref.refs_0_), channel_id=1, source_target_pairs={{0,1},{1,2},{2,3},{4,5},{5,6},{6,7},{8,9},{9,10},{10,11},{12,13},{... | collective-permute-start | bytes 4718600 | tf_op jit(solution)/shard_map/ppermute | solution.py:583
  8.4 44.8 %collective-permute-start.6 = (f32[16,3,64,128]{3,2,1,0:T(8,128)}, f32[16,3,64,128]{3,2,1,0:T(8,128)S(1)}, u32[]{:S(2)}, u32[]{:S(2)}) collective-permute-start(f32[16,3,64,128]{3,2,1,0:T(8,128)} %get-tuple-element.28.s_ref.refs_0_), channel_id=1, source_target_pairs={{1,0},{2,1},{3,2},{5,4},{6,5},{7,6},{9,8},{10,9},{11,10},{13,12},{... | collective-permute-start | bytes 4718600 | tf_op jit(solution)/shard_map/ppermute | solution.py:583
  9.7 12.5 %collective-permute-start = (f32[16,3,16,128]{3,2,1,0:T(8,128)}, f32[16,3,16,128]{3,2,1,0:T(8,128)S(1)}, u32[]{:S(2)}, u32[]{:S(2)}) collective-permute-start(f32[16,3,16,128]{3,2,1,0:T(8,128)} %get-tuple-element.30), channel_id=1, source_target_pairs={{0,4},{4,8},{8,12},{12,16},{16,20},{20,24},{24,28},{1,5},{5,9},{9,... | collective-permute-start | bytes 1179656 | tf_op jit(solution)/shard_map/ppermute | solution.py:583
  12.9 10.4 %collective-permute-start.1 = (f32[16,3,16,128]{3,2,1,0:T(8,128)}, f32[16,3,16,128]{3,2,1,0:T(8,128)S(1)}, u32[]{:S(2)}, u32[]{:S(2)}) collective-permute-start(f32[16,3,16,128]{3,2,1,0:T(8,128)} %get-tuple-element.31), channel_id=1, source_target_pairs={{4,0},{8,4},{12,8},{16,12},{20,16},{24,20},{28,24},{5,1},{9,5},{13... | collective-permute-start | bytes 1179656 | tf_op jit(solution)/shard_map/ppermute | solution.py:583
  14.2 1.4 %copy-start = (f32[16,3,64,128]{3,2,1,0:T(8,128)S(1)}, f32[16,3,64,128]{3,2,1,0:T(8,128)}, u32[]{:S(2)}) copy-start(f32[16,3,64,128]{3,2,1,0:T(8,128)} %get-tuple-element.28.s_ref.refs_0_) | copy-start | bytes 4718596
  22.1 23.7 %copy-start.1 = (f32[16,3,64,128]{3,2,1,0:T(8,128)S(1)}, f32[16,3,64,128]{3,2,1,0:T(8,128)}, u32[]{:S(2)}) copy-start(f32[16,3,64,128]{3,2,1,0:T(8,128)} %get-tuple-element.28.s_ref.refs_0_) | copy-start | bytes 4718596
  22.1 23.7 %copy-start.2 = (s32[4,3]{1,0:T(4,128)S(1)}, s32[4,3]{1,0:T(4,128)}, u32[]{:S(2)}) copy-start(s32[4,3]{1,0:T(4,128)} %src_ref.3) | copy-start | bytes 148
  22.2 23.7 %copy-start.3 = (f32[16,4]{0,1:T(4,128)S(1)}, f32[16,4]{0,1:T(4,128)}, u32[]{:S(2)}) copy-start(f32[16,4]{0,1:T(4,128)} %param.12) | copy-start | bytes 772
  24.6 13.2 %collective-permute-start.2 = (f32[16,40,128]{2,1,0:T(8,128)S(1)}, f32[16,40,128]{2,1,0:T(8,128)S(1)}, u32[]{:S(2)}, u32[]{:S(2)}) collective-permute-start(f32[16,40,128]{2,1,0:T(8,128)S(1)} %get-tuple-element.36), channel_id=1, source_target_pairs={{32,0},{64,32},{96,64},{128,96},{160,128},{192,160},{224,192},{256... | collective-permute-start | bytes 983048 | tf_op jit(solution)/shard_map/ppermute | solution.py:583
  29.7 9.4 %collective-permute-start.3 = (f32[16,40,128]{2,1,0:T(8,128)S(1)}, f32[16,40,128]{2,1,0:T(8,128)S(1)}, u32[]{:S(2)}, u32[]{:S(2)}) collective-permute-start(f32[16,40,128]{2,1,0:T(8,128)S(1)} %get-tuple-element.37), channel_id=1, source_target_pairs={{0,32},{32,64},{64,96},{96,128},{128,160},{160,192},{192,224},{224... | collective-permute-start | bytes 983048 | tf_op jit(solution)/shard_map/ppermute | solution.py:583
  33.8 19.4 %collective-permute-start.5 = (f32[8,96,128]{2,1,0:T(8,128)S(1)}, f32[8,96,128]{2,1,0:T(8,128)S(1)}, u32[]{:S(2)}, u32[]{:S(2)}) collective-permute-start(f32[8,96,128]{2,1,0:T(8,128)S(1)} %get-tuple-element.45), channel_id=1, source_target_pairs={{0,1},{1,2},{2,3},{4,5},{5,6},{6,7},{8,9},{9,10},{10,11},{12,13},{... | collective-permute-start | bytes 1179656 | tf_op jit(solution)/shard_map/ppermute | solution.py:583
  37.8 15.4 %collective-permute-start.7 = (f32[8,96,128]{2,1,0:T(8,128)S(1)}, f32[8,96,128]{2,1,0:T(8,128)S(1)}, u32[]{:S(2)}, u32[]{:S(2)}) collective-permute-start(f32[8,96,128]{2,1,0:T(8,128)S(1)} %get-tuple-element.46), channel_id=1, source_target_pairs={{1,0},{2,1},{3,2},{5,4},{6,5},{7,6},{9,8},{10,9},{11,10},{13,12},{... | collective-permute-start | bytes 1179656 | tf_op jit(solution)/shard_map/ppermute | solution.py:583
  40.5 15.4 %collective-permute-start.8 = (f32[8,96,128]{2,1,0:T(8,128)S(1)}, f32[8,96,128]{2,1,0:T(8,128)S(1)}, u32[]{:S(2)}, u32[]{:S(2)}) collective-permute-start(f32[8,96,128]{2,1,0:T(8,128)S(1)} %get-tuple-element.50), channel_id=1, source_target_pairs={{0,1},{1,2},{2,3},{4,5},{5,6},{6,7},{8,9},{9,10},{10,11},{12,13},{... | collective-permute-start | bytes 1179656 | tf_op jit(solution)/shard_map/ppermute | solution.py:583
  44.5 14.9 %collective-permute-start.9 = (f32[8,96,128]{2,1,0:T(8,128)S(1)}, f32[8,96,128]{2,1,0:T(8,128)S(1)}, u32[]{:S(2)}, u32[]{:S(2)}) collective-permute-start(f32[8,96,128]{2,1,0:T(8,128)S(1)} %get-tuple-element.51), channel_id=1, source_target_pairs={{1,0},{2,1},{3,2},{5,4},{6,5},{7,6},{9,8},{10,9},{11,10},{13,12},{... | collective-permute-start | bytes 1179656 | tf_op jit(solution)/shard_map/ppermute | solution.py:583
  110.4 21.8 %all-to-all-start.1 = ((f32[32,16,128]{2,1,0:T(8,128)}), f32[32,16,128]{2,1,0:T(8,128)S(1)}, u32[]{:S(2)}, u32[]{:S(2)}) async-start(f32[32,16,128]{2,1,0:T(8,128)} %relay.1), calls=%async_computation.1 | async-start | bytes 524288 | tf_op jit(solution)/shard_map/all_to_all | solution.py:675

commit v7 on v6

--- a/solution.py
+++ b/solution.py
@@ -327,7 +327,7 @@
         fill_edge(refs, mains, second, far + skip, far)
         return carry
 
-    lax.fori_loop(0, HALF, pair, 0)
+    lax.fori_loop(0, HALF, pair, 0, unroll=2)
 
 
 def corner():
@@ -481,7 +481,7 @@
                 ref[parity, HALO + h] = got[parity, h]
         return carry
 
-    lax.fori_loop(0, HIGH, take, 0)
+    lax.fori_loop(0, HIGH, take, 0, unroll=2)
     fill_edges(fields, mains, temp, under_edge, lambda i: (HALO - 1 - i, i), 0)
     fill_edges(fields, mains, temp, over_edge, lambda i: (HALO + i, 2 * HALO - 1 - i), HIGH)
     points = list_sources(src_ref)
@@ -489,17 +489,19 @@
     def step(now, old, t):
         early = t < HALF - 1
         full = TALL - 2 * (t + 1)
-        fours = jnp.where(early, HIGH // 2, full // 4)
         gap = jnp.where(early, HIGH - 2 * (t + 1), 0)
+        eights = jnp.where(early, HIGH // 4, full // 8)
+        rest = jnp.where(early, 0, full % 8)
         sweep(
             now,
             old,
             p_ref,
-            lambda i: t + 1 + 4 * i + jnp.where(i >= HIGH // 4, gap, 0),
-            fours,
-            4,
+            lambda i: t + 1 + 8 * i + jnp.where(i >= HIGH // 8, gap, 0),
+            eights,
+            8,
         )
-        sweep(now, old, p_ref, lambda i: t + 1 + 4 * fours, jnp.where(early, 0, (full % 4) // 2), 2)
+        sweep(now, old, p_ref, lambda i: t + 1 + 8 * eights, rest // 4, 4)
+        sweep(now, old, p_ref, lambda i: t + 1 + full - 2, (rest % 4) // 2, 2)
         inject(old, points, sig_ref, t, 0, lambda h: (h <= HALO + t) | (h >= HALO + HIGH - 1 - t))
         keep(old, todo, hist, t, 0)
 

time: 133 us -> 130 us (0.977)
  Pallas kernels: 52.5 us -> 49.7 us
    pallas_call x10, Pallas kernels: 48.8 us -> 46 us  [call(): pl.pallas_call(kernel, out_shape=tuple(out_shape), in_specs=[SMEM] * scal...]
where the time goes in v7:
time: 130 us
  Pallas kernels  49.7 us (38%)
  starting transfers between devices  38.8 us (30%)
  blocking collectives  24.1 us (19%)
  waiting for transfers between devices  14.8 us (11%)
  local copies, waits for them, and re-layouts  1.42 us (1%)
    pallas_call x10, Pallas kernels, call(): pl.pallas_call(kernel, out_shape=tuple(out_shape), in_specs=[SMEM] * scal...  46 us
    ppermute x10, starting transfers between devices, shift(): return lax.ppermute(x, axis, pairs)  29.5 us
    all_to_all x1, blocking collectives, per_device(): traces = lax.all_to_all(traces, 'len', 0, 0, tiled=True)  24.1 us
    all_to_all x1, waiting for transfers between devices, per_device(): traces = lax.all_to_all(traces, ('wid', 'hgt'), 0, 0, tiled=True)  10.2 us
    all_to_all x1, starting transfers between devices, per_device(): traces = lax.all_to_all(traces, ('wid', 'hgt'), 0, 0, tiled=True)  9.28 us
    ppermute x10, waiting for transfers between devices, shift(): return lax.ppermute(x, axis, pairs)  4.55 us
    pallas_call x1, Pallas kernels, per_device(): pl.pallas_call(pack_kernel, out_shape=(field(HIGH, 3, WIDE, LANES), field...  3.7 us
  transfers between devices with their start and end apart: 11, of which 3 were waited for; matrix products, arithmetic and copies ran while one was open for 0% of the time, Pallas kernels for 16%

profile of v7, /device:TPU:1, one launch (start us, length us, event | category | flops | bytes accessed | tf_op | source)
XLA Modules:
  0.0 129.7 jit_solution(14880957069099975060)
XLA Ops:
  0.6 0.0 copy-start.4
  0.6 3.7 %pack.1 = (f32[16,3,64,128]{3,2,1,0:T(8,128)}, f32[16,3,16,128]{3,2,1,0:T(8,128)}, f32[16,3,16,128]{3,2,1,0:T(8,128)}) custom-call(f32[8]{0:T(128)} %adm_hbm.1, f32[16,64,128]{2,1,0:T(8,128)} %now_hbm.1, f32[16,64,128]{2,1,0:T(8,128)} %old_hbm.1, s32[16,64,128]{2,1,0:T(8,128)} %cls_hbm.1), custom_call_target="tpu_custom_call" | custom-call | tf_op jit(solution)/shard_map/pack/pallas_call | solution.py:593
  4.4 4.0 %collective-permute-start.4 = (f32[16,3,64,128]{3,2,1,0:T(8,128)}, f32[16,3,64,128]{3,2,1,0:T(8,128)S(1)}, u32[]{:S(2)}, u32[]{:S(2)}) collective-permute-start(f32[16,3,64,128]{3,2,1,0:T(8,128)} %get-tuple-element.28.s_ref.refs_0_), channel_id=1, source_target_pairs={{0,1},{1,2},{2,3},{4,5},{5,6},{6,7},{8,9},{9,10},{10,11},{12,13},{... | collective-permute-start | bytes 4718600 | tf_op jit(solution)/shard_map/ppermute | solution.py:585
  8.4 1.3 collective-permute-start.6
  9.7 3.2 %collective-permute-start = (f32[16,3,16,128]{3,2,1,0:T(8,128)}, f32[16,3,16,128]{3,2,1,0:T(8,128)S(1)}, u32[]{:S(2)}, u32[]{:S(2)}) collective-permute-start(f32[16,3,16,128]{3,2,1,0:T(8,128)} %get-tuple-element.30), channel_id=1, source_target_pairs={{0,4},{4,8},{8,12},{12,16},{16,20},{20,24},{24,28},{1,5},{5,9},{9,... | collective-permute-start | bytes 1179656 | tf_op jit(solution)/shard_map/ppermute | solution.py:585
  12.9 1.3 collective-permute-start.1
  14.2 0.0 copy-done.4
  14.2 0.0 copy-start
  14.3 1.4 %copy-done = f32[16,3,64,128]{3,2,1,0:T(8,128)S(1)} copy-done((f32[16,3,64,128]{3,2,1,0:T(8,128)S(1)}, f32[16,3,64,128]{3,2,1,0:T(8,128)}, u32[]{:S(2)}) %copy-start) | copy-done | bytes 1572888
  15.7 6.5 %own_strip.1 = (f32[16,64,128]{2,1,0:T(8,128)S(1)}, s32[8,128]{1,0:T(8,128)S(1)}) custom-call(s32[3,128]{1,0:T(4,128)S(1)} %bitcast.4, f32[16,3,64,128]{3,2,1,0:T(8,128)S(1)} %copy-done), custom_call_target="tpu_custom_call" | custom-call | tf_op jit(solution)/shard_map/own_strip/pallas_call | solution.py:571
  22.1 0.0 copy-start.1
  22.1 0.0 copy-start.2
  22.2 0.0 copy-start.3
  22.2 0.0 collective-permute-done.before_ref.refs_2_
  22.2 1.2 collective-permute-done.1.after_ref.refs_3_
  23.3 1.2 strip.1
  24.6 5.1 %collective-permute-start.2 = (f32[16,40,128]{2,1,0:T(8,128)S(1)}, f32[16,40,128]{2,1,0:T(8,128)S(1)}, u32[]{:S(2)}, u32[]{:S(2)}) collective-permute-start(f32[16,40,128]{2,1,0:T(8,128)S(1)} %get-tuple-element.36), channel_id=1, source_target_pairs={{32,0},{64,32},{96,64},{128,96},{160,128},{192,160},{224,192},{256... | collective-permute-start | bytes 983048 | tf_op jit(solution)/shard_map/ppermute | solution.py:585
  29.7 3.9 %collective-permute-start.3 = (f32[16,40,128]{2,1,0:T(8,128)S(1)}, f32[16,40,128]{2,1,0:T(8,128)S(1)}, u32[]{:S(2)}, u32[]{:S(2)}) collective-permute-start(f32[16,40,128]{2,1,0:T(8,128)S(1)} %get-tuple-element.37), channel_id=1, source_target_pairs={{0,32},{32,64},{64,96},{96,128},{128,160},{160,192},{192,224},{224... | collective-permute-start | bytes 983048 | tf_op jit(solution)/shard_map/ppermute | solution.py:585
  33.6 0.2 wide_rim.1
  33.8 4.0 %collective-permute-start.5 = (f32[8,96,128]{2,1,0:T(8,128)S(1)}, f32[8,96,128]{2,1,0:T(8,128)S(1)}, u32[]{:S(2)}, u32[]{:S(2)}) collective-permute-start(f32[8,96,128]{2,1,0:T(8,128)S(1)} %get-tuple-element.45), channel_id=1, source_target_pairs={{0,1},{1,2},{2,3},{4,5},{5,6},{6,7},{8,9},{9,10},{10,11},{12,13},{... | collective-permute-start | bytes 1179656 | tf_op jit(solution)/shard_map/ppermute | solution.py:585
  37.8 0.0 collective-permute-done.2.from_right_ref
  37.8 1.3 collective-permute-start.7
  39.1 0.0 collective-permute-done.3.from_left_ref
  39.1 1.3 %long_rim.1 = (f32[16,96,128]{2,1,0:T(8,128)S(1)}, f32[8,96,128]{2,1,0:T(8,128)S(1)}, f32[8,96,128]{2,1,0:T(8,128)S(1)}) custom-call(f32[16,40,128]{2,1,0:T(8,128)S(1)} %collective-permute-done.2.from_right_ref, f32[16,40,128]{2,1,0:T(8,128)S(1)} %collective-permute-done.3.from_left_ref), custom_call_target="tpu_custom_call" | custom-call | tf_op jit(solution)/shard_map/long_rim/pallas_call | solution.py:571
  40.5 4.0 %collective-permute-start.8 = (f32[8,96,128]{2,1,0:T(8,128)S(1)}, f32[8,96,128]{2,1,0:T(8,128)S(1)}, u32[]{:S(2)}, u32[]{:S(2)}) collective-permute-start(f32[8,96,128]{2,1,0:T(8,128)S(1)} %get-tuple-element.50), channel_id=1, source_target_pairs={{0,1},{1,2},{2,3},{4,5},{5,6},{6,7},{8,9},{9,10},{10,11},{12,13},{... | collective-permute-start | bytes 1179656 | tf_op jit(solution)/shard_map/ppermute | solution.py:585
  44.5 0.0 collective-permute-done.4.under
  44.5 1.3 collective-permute-start.9
  45.8 0.0 copy-done.1
  45.8 0.0 copy-done.2
  45.8 0.0 copy-done.3
  45.8 7.5 %inner.1 = (f32[2,16,12,8,128]{4,3,2,1,0:T(8,128)S(1)}, f32[2,16,12,8,128]{4,3,2,1,0:T(8,128)S(1)}, f32[2,16,12,8,128]{4,3,2,1,0:T(8,128)S(1)}, f32[16,128]{1,0:T(8,128)S(1)}) custom-call(s32[4,3]{1,0:T(4,128)S(1)} %copy-done.2, f32[4,16]{1,0:T(4,128)S(1)} %bitcast.2, s32[8,128]{1,0:T(8,128)S(1)} %get-tuple-element.29.todo, ...), custom_call_target="tpu_custom_call" | custom-call | tf_op jit(solution)/shard_map/inner/pallas_call | solution.py:571
  53.4 0.0 collective-permute-done.5.under_rim
  53.4 0.0 collective-permute-done.7.over_rim
  53.4 0.0 collective-permute-done.6.over
  53.4 2.6 %beside.1 = (f32[2,32,12,8,128]{4,3,2,1,0:T(8,128)S(1)}, f32[2,32,12,8,128]{4,3,2,1,0:T(8,128)S(1)}, f32[2,32,12,8,128]{4,3,2,1,0:T(8,128)S(1)}) custom-call(f32[16,3,64,128]{3,2,1,0:T(8,128)S(1)} %collective-permute-done.4.under, f32[8,96,128]{2,1,0:T(8,128)S(1)} %collective-permute-done.5.under_rim, f32[16,3,64,128]{3,2,1,0:T(8,128)S(1)} %collective-permute-done.6.over, ...), custom_call_target="tpu_custom_call" | custom-call | tf_op jit(solution)/shard_map/beside/pallas_call | solution.py:571
  56.0 0.0 collective-permute-done.8.refs_7_
  56.0 3.4 %collective-permute-done.9.refs_8_ = f32[8,96,128]{2,1,0:T(8,128)S(1)} collective-permute-done((f32[8,96,128]{2,1,0:T(8,128)S(1)}, f32[8,96,128]{2,1,0:T(8,128)S(1)}, u32[]{:S(2)}, u32[]{:S(2)}) %collective-permute-start.9) | collective-permute-done | bytes 393248 | tf_op jit(solution)/shard_map/ppermute | solution.py:585
  59.3 23.3 %march.1 = (f32[16,64,128]{2,1,0:T(8,128)S(1)}, f32[16,16,128]{2,1,0:T(8,128)S(1)}) custom-call(s32[4,3]{1,0:T(4,128)S(1)} %copy-done.2, f32[4,16]{1,0:T(4,128)S(1)} %bitcast.3, s32[8,128]{1,0:T(8,128)S(1)} %get-tuple-element.29.todo, f32[2,16,12,8,128]{4,3,2,1,0:T(8,128)S(1)} %get-tuple-element.39.refs_0_, ...), custom_call_target="tpu_custom_call" | custom-call | tf_op jit(solution)/shard_map/march/pallas_call | solution.py:571
  82.6 24.1 %all_to_all.10.got_ref = f32[16,16,128]{2,1,0:T(8,128)S(1)} all-to-all(f32[16,16,128]{2,1,0:T(8,128)S(1)} %get-tuple-element.53), channel_id=1, replica_groups=mesh['len'=16,'wid'=8,'hgt'=4] {'len'}, dimensions={0} | all-to-all | bytes 262144 | tf_op jit(solution)/shard_map/all_to_all | solution.py:675
  106.7 0.7 relay.1
  107.5 9.3 %all-to-all-start.1 = ((f32[32,16,128]{2,1,0:T(8,128)}), f32[32,16,128]{2,1,0:T(8,128)S(1)}, u32[]{:S(2)}, u32[]{:S(2)}) async-start(f32[32,16,128]{2,1,0:T(8,128)} %relay.1), calls=%async_computation.1 | async-start | bytes 524288 | tf_op jit(solution)/shard_map/all_to_all | solution.py:677
  116.8 2.0 %order.1 = f32[16,64,128]{2,1,0:T(8,128)} custom-call(f32[16,64,128]{2,1,0:T(8,128)S(1)} %get-tuple-element.52.split_ref), custom_call_target="tpu_custom_call" | custom-call | tf_op jit(solution)/shard_map/order/pallas_call | solution.py:571
  118.8 10.2 %all-to-all-done.1.got_ref = f32[32,16,128]{2,1,0:T(8,128)S(1)} async-done(((f32[32,16,128]{2,1,0:T(8,128)}), f32[32,16,128]{2,1,0:T(8,128)S(1)}, u32[]{:S(2)}, u32[]{:S(2)}) %all-to-all-start.1) | async-done | bytes 262176 | tf_op jit(solution)/shard_map/all_to_all | solution.py:677
  129.1 0.6 total.1
Async XLA Ops:
  0.6 13.6 %copy-start.4 = (s32[128,3]{0,1:T(4,128)S(1)}, s32[128,3]{0,1:T(4,128)}, u32[]{:S(2)}) copy-start(s32[128,3]{0,1:T(4,128)} %param.13) | copy-start | bytes 4612
  4.4 40.1 %collective-permute-start.4 = (f32[16,3,64,128]{3,2,1,0:T(8,128)}, f32[16,3,64,128]{3,2,1,0:T(8,128)S(1)}, u32[]{:S(2)}, u32[]{:S(2)}) collective-permute-start(f32[16,3,64,128]{3,2,1,0:T(8,128)} %get-tuple-element.28.s_ref.refs_0_), channel_id=1, source_target_pairs={{0,1},{1,2},{2,3},{4,5},{5,6},{6,7},{8,9},{9,10},{10,11},{12,13},{... | collective-permute-start | bytes 4718600 | tf_op jit(solution)/shard_map/ppermute | solution.py:585
  8.4 45.0 %collective-permute-start.6 = (f32[16,3,64,128]{3,2,1,0:T(8,128)}, f32[16,3,64,128]{3,2,1,0:T(8,128)S(1)}, u32[]{:S(2)}, u32[]{:S(2)}) collective-permute-start(f32[16,3,64,128]{3,2,1,0:T(8,128)} %get-tuple-element.28.s_ref.refs_0_), channel_id=1, source_target_pairs={{1,0},{2,1},{3,2},{5,4},{6,5},{7,6},{9,8},{10,9},{11,10},{13,12},{... | collective-permute-start | bytes 4718600 | tf_op jit(solution)/shard_map/ppermute | solution.py:585
  9.7 12.5 %collective-permute-start = (f32[16,3,16,128]{3,2,1,0:T(8,128)}, f32[16,3,16,128]{3,2,1,0:T(8,128)S(1)}, u32[]{:S(2)}, u32[]{:S(2)}) collective-permute-start(f32[16,3,16,128]{3,2,1,0:T(8,128)} %get-tuple-element.30), channel_id=1, source_target_pairs={{0,4},{4,8},{8,12},{12,16},{16,20},{20,24},{24,28},{1,5},{5,9},{9,... | collective-permute-start | bytes 1179656 | tf_op jit(solution)/shard_map/ppermute | solution.py:585
  12.9 10.4 %collective-permute-start.1 = (f32[16,3,16,128]{3,2,1,0:T(8,128)}, f32[16,3,16,128]{3,2,1,0:T(8,128)S(1)}, u32[]{:S(2)}, u32[]{:S(2)}) collective-permute-start(f32[16,3,16,128]{3,2,1,0:T(8,128)} %get-tuple-element.31), channel_id=1, source_target_pairs={{4,0},{8,4},{12,8},{16,12},{20,16},{24,20},{28,24},{5,1},{9,5},{13... | collective-permute-start | bytes 1179656 | tf_op jit(solution)/shard_map/ppermute | solution.py:585
  14.2 1.4 %copy-start = (f32[16,3,64,128]{3,2,1,0:T(8,128)S(1)}, f32[16,3,64,128]{3,2,1,0:T(8,128)}, u32[]{:S(2)}) copy-start(f32[16,3,64,128]{3,2,1,0:T(8,128)} %get-tuple-element.28.s_ref.refs_0_) | copy-start | bytes 4718596
  22.1 23.7 %copy-start.1 = (f32[16,3,64,128]{3,2,1,0:T(8,128)S(1)}, f32[16,3,64,128]{3,2,1,0:T(8,128)}, u32[]{:S(2)}) copy-start(f32[16,3,64,128]{3,2,1,0:T(8,128)} %get-tuple-element.28.s_ref.refs_0_) | copy-start | bytes 4718596
  22.1 23.7 %copy-start.2 = (s32[4,3]{1,0:T(4,128)S(1)}, s32[4,3]{1,0:T(4,128)}, u32[]{:S(2)}) copy-start(s32[4,3]{1,0:T(4,128)} %src_ref.3) | copy-start | bytes 148
  22.2 23.7 %copy-start.3 = (f32[16,4]{0,1:T(4,128)S(1)}, f32[16,4]{0,1:T(4,128)}, u32[]{:S(2)}) copy-start(f32[16,4]{0,1:T(4,128)} %param.12) | copy-start | bytes 772
  24.6 13.2 %collective-permute-start.2 = (f32[16,40,128]{2,1,0:T(8,128)S(1)}, f32[16,40,128]{2,1,0:T(8,128)S(1)}, u32[]{:S(2)}, u32[]{:S(2)}) collective-permute-start(f32[16,40,128]{2,1,0:T(8,128)S(1)} %get-tuple-element.36), channel_id=1, source_target_pairs={{32,0},{64,32},{96,64},{128,96},{160,128},{192,160},{224,192},{256... | collective-permute-start | bytes 983048 | tf_op jit(solution)/shard_map/ppermute | solution.py:585
  29.7 9.4 %collective-permute-start.3 = (f32[16,40,128]{2,1,0:T(8,128)S(1)}, f32[16,40,128]{2,1,0:T(8,128)S(1)}, u32[]{:S(2)}, u32[]{:S(2)}) collective-permute-start(f32[16,40,128]{2,1,0:T(8,128)S(1)} %get-tuple-element.37), channel_id=1, source_target_pairs={{0,32},{32,64},{64,96},{96,128},{128,160},{160,192},{192,224},{224... | collective-permute-start | bytes 983048 | tf_op jit(solution)/shard_map/ppermute | solution.py:585
  33.8 19.6 %collective-permute-start.5 = (f32[8,96,128]{2,1,0:T(8,128)S(1)}, f32[8,96,128]{2,1,0:T(8,128)S(1)}, u32[]{:S(2)}, u32[]{:S(2)}) collective-permute-start(f32[8,96,128]{2,1,0:T(8,128)S(1)} %get-tuple-element.45), channel_id=1, source_target_pairs={{0,1},{1,2},{2,3},{4,5},{5,6},{6,7},{8,9},{9,10},{10,11},{12,13},{... | collective-permute-start | bytes 1179656 | tf_op jit(solution)/shard_map/ppermute | solution.py:585
  37.8 15.5 %collective-permute-start.7 = (f32[8,96,128]{2,1,0:T(8,128)S(1)}, f32[8,96,128]{2,1,0:T(8,128)S(1)}, u32[]{:S(2)}, u32[]{:S(2)}) collective-permute-start(f32[8,96,128]{2,1,0:T(8,128)S(1)} %get-tuple-element.46), channel_id=1, source_target_pairs={{1,0},{2,1},{3,2},{5,4},{6,5},{7,6},{9,8},{10,9},{11,10},{13,12},{... | collective-permute-start | bytes 1179656 | tf_op jit(solution)/shard_map/ppermute | solution.py:585
  40.5 15.5 %collective-permute-start.8 = (f32[8,96,128]{2,1,0:T(8,128)S(1)}, f32[8,96,128]{2,1,0:T(8,128)S(1)}, u32[]{:S(2)}, u32[]{:S(2)}) collective-permute-start(f32[8,96,128]{2,1,0:T(8,128)S(1)} %get-tuple-element.50), channel_id=1, source_target_pairs={{0,1},{1,2},{2,3},{4,5},{5,6},{6,7},{8,9},{9,10},{10,11},{12,13},{... | collective-permute-start | bytes 1179656 | tf_op jit(solution)/shard_map/ppermute | solution.py:585
  44.5 14.9 %collective-permute-start.9 = (f32[8,96,128]{2,1,0:T(8,128)S(1)}, f32[8,96,128]{2,1,0:T(8,128)S(1)}, u32[]{:S(2)}, u32[]{:S(2)}) collective-permute-start(f32[8,96,128]{2,1,0:T(8,128)S(1)} %get-tuple-element.51), channel_id=1, source_target_pairs={{1,0},{2,1},{3,2},{5,4},{6,5},{7,6},{9,8},{10,9},{11,10},{13,12},{... | collective-permute-start | bytes 1179656 | tf_op jit(solution)/shard_map/ppermute | solution.py:585
  107.5 21.6 %all-to-all-start.1 = ((f32[32,16,128]{2,1,0:T(8,128)}), f32[32,16,128]{2,1,0:T(8,128)S(1)}, u32[]{:S(2)}, u32[]{:S(2)}) async-start(f32[32,16,128]{2,1,0:T(8,128)} %relay.1), calls=%async_computation.1 | async-start | bytes 524288 | tf_op jit(solution)/shard_map/all_to_all | solution.py:677
